TPU v7x, 32 devices: a whole 2x2x4 slice. The times are simulated.
32 devices in a mesh: sector: 16 (over z, y, x), term: 2 (over core).
Axes of the slice: x: 2, y: 2, z: 4, core: 2. Of those that a mesh axis runs over, the one named last changes fastest.
Arguments:
- psi: bfloat16 [4, 16, 4, 256, 256], P(None, 'sector'), may hold values from -6 to 6
- left_env: bfloat16 [4, 16, 256, 256], P('term', 'sector'), may hold values from -0.375 to 0.375
- right_env: bfloat16 [4, 16, 256, 256], P('term', 'sector'), may hold values from -0.375 to 0.375
- op_index: int32 [4], P('term'), may hold values from 0 to 4
- kept_rows: int32 [16], P('sector'), may hold values from 64 to 256, as said below
Outputs:
- sigma: float32 [4, 16, 4, 256, 256], P(None, 'sector', None, 'term')
Inputs may be any that keep to these rules, and one draw needn't show every extreme that they name: `kept_rows`: some sector keeps all 256 rows and some other keeps 256 // 4.
All inputs are finite; a program needn't handle non-finite values.
Results may differ from a plain program's by a relative error of at most 0.0029.
Values may be sent and summed in bfloat16 or wider, within the bound.
No kernel may reach another device: no remote copies, remote signals or barrier semaphores. Data moves between devices by JAX's collectives and lax.ppermute only.
A program may use at most 64 MiB of HBM per device.

v0:
```python
import jax
import jax.numpy as jnp
from jax import lax
from jax.sharding import PartitionSpec as P

OP_KINDS = 5


def padded_2(block, sides, width):
    for axis, dim in sides:
        count = lax.axis_size(axis)
        forward = [(i, i + 1) for i in range(count - 1)]
        backward = [(target, source) for source, target in forward]
        low = lax.ppermute(
            lax.slice_in_dim(block, block.shape[dim] - width, None, axis=dim), axis, forward
        )
        high = lax.ppermute(lax.slice_in_dim(block, 0, width, axis=dim), axis, backward)
        block = jnp.concatenate([low, block, high], axis=dim)
    return block


def diagonal_matrix(values):
    return [[values[r] if r == c else 0.0 for c in range(4)] for r in range(4)]


def operator_table():
    flip = [[0.0, 0.0, 0.0, 0.0], [0.0, 0.0, 0.5, 0.0], [0.0, 0.5, 0.0, 0.0], [0.0, 0.0, 0.0, 0.0]]
    stacked = [
        diagonal_matrix([1.0, 1.0, 1.0, 1.0]),
        diagonal_matrix([0.25, -0.25, -0.25, 0.25]),
        flip,
        diagonal_matrix([0.5, 0.5, -0.5, -0.5]),
        diagonal_matrix([0.5, -0.5, 0.5, -0.5]),
    ]
    return jnp.asarray(stacked, jnp.float32)


def combine_terms(term_factor, mapped_vectors):
    return jnp.einsum(
        "uci,ufimy->fcmy", term_factor, mapped_vectors, precision=lax.Precision.HIGHEST
    )


def finish_sum(blocks_full, own_rows):
    row_ids = jnp.arange(blocks_full.shape[2], dtype=jnp.int32)
    blocks_full = jnp.where(row_ids[None, None, :, None] < own_rows, blocks_full, 0.0)
    return lax.psum_scatter(blocks_full, "term", scatter_dimension=2, tiled=True)


def shards(psi, left_env, right_env, op_index, kept_rows):
    trial_vectors = psi[:, 0]
    left_mat = left_env[:, 0]
    right_mat = right_env[:, 0]
    size_b = trial_vectors.shape[-1]
    onehot = (op_index[:, None] == jnp.arange(OP_KINDS, dtype=jnp.int32)[None, :]).astype(
        jnp.float32
    )
    term_factor = jnp.einsum(
        "tk,kpq->tpq", onehot, operator_table(), precision=lax.Precision.HIGHEST
    )
    lifted = jnp.einsum(
        "tab,vpbc->tvpac", left_mat, trial_vectors, preferred_element_type=jnp.float32
    ).astype(jnp.bfloat16)
    own_rows = kept_rows[0]
    indices = jnp.arange(size_b, dtype=jnp.int32)
    rim_blocks = jnp.stack([lifted[:, :, 3], lifted[:, :, 0]], 0)
    padded = padded_2(rim_blocks, (("sector", 0),), 1)
    arrived = jnp.stack([padded[0], lifted[:, :, 1], lifted[:, :, 2], padded[3]], 2)
    mapped_vectors = jnp.einsum(
        "tvpac,tdc->tvpad", arrived, right_mat, preferred_element_type=jnp.float32
    )
    right_side = combine_terms(term_factor, mapped_vectors)
    right_side = jnp.where(indices[None, None, None, :] < own_rows, right_side, 0.0)
    returned = padded_2(jnp.stack([right_side[:, 0], right_side[:, 3]], 0), (("sector", 0),), 1)
    blocks_full = jnp.stack([returned[3], right_side[:, 1], right_side[:, 2], returned[0]], 1)
    result = finish_sum(blocks_full, own_rows)
    return result[:, None]


def solution(mesh):
    in_specs = (
        P(None, "sector", None, None, None),
        P("term", "sector", None, None),
        P("term", "sector", None, None),
        P("term"),
        P("sector"),
    )
    out_specs = P(None, "sector", None, "term", None)
    return jax.shard_map(shards, mesh=mesh, in_specs=in_specs, out_specs=out_specs, check_vma=False)
```

profile of v0, /device:TPU:0, one launch (start us, length us, event | category | flops | bytes accessed | tf_op | source)
XLA Modules:
  0.0 167.7 jit_solution(11256219477450217974)
XLA Ops:
  6.5 0.0 copy-start
  6.5 0.0 reduce-scatter.5.cloned.1.call-start
  6.5 1.6 copy-done
  8.1 2.3 %convert_bitcast_fusion = bf16[2,4,4,256,256]{3,4,0,2,1:T(8,128)(2,1)S(1)} fusion(bf16[4,1,4,256,256]{4,3,2,1,0:T(8,128)(2,1)S(1)} %copy-done, bf16[2,1,256,256]{3,2,1,0:T(8,128)(2,1)} %param.7), kind=kOutput, calls=%fused_computation.9 | convolution fusion | flops 1075838976 | bytes 6553600 | tf_op jit(solution)/shard_map/tab,vpbc->tvpac/dot_general | solution.py:61
  10.4 0.0 copy-start.2
  10.4 0.0 copy-start.3
  10.4 0.0 copy-start.1
  10.4 0.1 slice_bitcast_fusion.3
  10.6 4.9 %collective-permute-start = (bf16[1,2,4,256,256]{3,4,1,2,0:T(8,128)(2,1)S(1)}, bf16[1,2,4,256,256]{3,4,1,2,0:T(8,128)(2,1)S(1)}, u32[]{:S(2)}, u32[]{:S(2)}) collective-permute-start(bf16[1,2,4,256,256]{3,4,1,2,0:T(8,128)(2,1)S(1)} %get-tuple-element.7), channel_id=1, source_target_pairs={{0,2},{2,4},{4,6},{6,8},{8,10},{10,12},{12,14},{14,16},{16,18},{18... | collective-permute-start | bytes 3145736 | tf_op jit(solution)/shard_map/ppermute | solution.py:14
  15.5 1.3 collective-permute-start.1
  16.8 0.2 slice.29
  17.6 0.0 copy-done.2
  17.7 0.0 copy-done.3
  17.7 0.2 convolution_bitcast_fusion
  17.9 42.4 %collective-permute-done = bf16[1,2,4,256,256]{3,4,1,2,0:T(8,128)(2,1)S(1)} collective-permute-done((bf16[1,2,4,256,256]{3,4,1,2,0:T(8,128)(2,1)S(1)}, bf16[1,2,4,256,256]{3,4,1,2,0:T(8,128)(2,1)S(1)}, u32[]{:S(2)}, u32[]{:S(2)}) %collective-permute-start) | collective-permute-done | bytes 1048608 | tf_op jit(solution)/shard_map/ppermute | solution.py:14
  60.3 1.9 %collective-permute-done.1 = bf16[1,2,4,256,256]{3,4,1,2,0:T(8,128)(2,1)S(1)} collective-permute-done((bf16[1,2,4,256,256]{3,4,1,2,0:T(8,128)(2,1)S(1)}, bf16[1,2,4,256,256]{3,4,1,2,0:T(8,128)(2,1)S(1)}, u32[]{:S(2)}, u32[]{:S(2)}) %collective-permute-start.1) | collective-permute-done | bytes 1048608 | tf_op jit(solution)/shard_map/ppermute | solution.py:17
  62.2 0.0 copy-done.1
  62.2 2.2 %fusion.3 = f32[2,4,4,256,256]{4,3,2,1,0:T(8,128)S(1)} fusion(bf16[2,1,256,256]{3,2,1,0:T(8,128)(2,1)S(1)} %copy-done.1, bf16[2,4,1,256,256]{3,4,0,2,1:T(8,128)(2,1)S(1)} %bitcast.67, bf16[2,4,2,256,256]{3,4,0,2,1:T(8,128)(2,1)S(1)} %slice.29, bf16[2,4,1,256,256]{3,4,0,2,1:T(8,128)(2,1)S(1)} %bitcast.66), kind=kOutput, calls=%fused_computation.7 | convolution fusion | flops 1077936128 | bytes 12845056 | tf_op jit(solution)/shard_map/tvpac,tdc->tvpad/dot_general | solution.py:69
  64.5 14.2 %fusion.2 = f32[4,4,256,256]{3,1,2,0:T(4,128)S(1)} fusion(f32[2,4,4,256,256]{4,3,2,1,0:T(8,128)S(1)} %fusion.3, pred[256]{0:T(512)(128)(4,1)S(1)} %iota_compare_fusion, f32[2,4,4,1,1]{2,0,1,4,3:T(2,128)S(1)} %convolution_bitcast_fusion), kind=kOutput, calls=%fused_computation.6 | convolution fusion | flops 101711872 | bytes 12583296 | tf_op jit(solution)/shard_map/uci,ufimy->fcmy/dot_general | solution.py:39
  78.7 1.6 slice_bitcast_fusion.1
  80.3 1.3 collective-permute-start.2
  81.6 4.8 %collective-permute-start.3 = (f32[1,4,256,256]{3,0,2,1:T(1,128)S(1)}, f32[1,4,256,256]{3,0,2,1:T(1,128)S(1)}, u32[]{:S(2)}, u32[]{:S(2)}) collective-permute-start(f32[1,4,256,256]{3,0,2,1:T(1,128)S(1)} %get-tuple-element.6), channel_id=1, source_target_pairs={{0,2},{2,4},{4,6},{6,8},{8,10},{10,12},{12,14},{14,16},{16,18},{18... | collective-permute-start | bytes 3145736 | tf_op jit(solution)/shard_map/ppermute | solution.py:14
  86.4 1.1 slice.32
  87.5 20.8 %collective-permute-done.2 = f32[1,4,256,256]{3,0,2,1:T(1,128)S(1)} collective-permute-done((f32[1,4,256,256]{3,0,2,1:T(1,128)S(1)}, f32[1,4,256,256]{3,0,2,1:T(1,128)S(1)}, u32[]{:S(2)}, u32[]{:S(2)}) %collective-permute-start.2) | collective-permute-done | bytes 1048608 | tf_op jit(solution)/shard_map/ppermute | solution.py:17
  108.3 19.2 %collective-permute-done.3 = f32[1,4,256,256]{3,0,2,1:T(1,128)S(1)} collective-permute-done((f32[1,4,256,256]{3,0,2,1:T(1,128)S(1)}, f32[1,4,256,256]{3,0,2,1:T(1,128)S(1)}, u32[]{:S(2)}, u32[]{:S(2)}) %collective-permute-start.3) | collective-permute-done | bytes 1048608 | tf_op jit(solution)/shard_map/ppermute | solution.py:14
  127.5 5.7 %copy_bitcast_fusion = f32[256,4,4,256]{3,2,1,0:T(4,128)} fusion(f32[4,1,256,256]{3,1,2,0:T(1,128)S(1)} %bitcast.65, f32[4,2,256,256]{3,1,2,0:T(2,128)S(1)} %slice.32, f32[4,1,256,256]{3,1,2,0:T(1,128)S(1)} %bitcast.64, pred[256]{0:T(512)(128)(4,1)S(1)} %iota_compare_fusion), kind=kLoop, calls=%fused_computation.4 | loop fusion | flops 3145728 | bytes 8388864
  133.2 5.8 %reshape.17 = f32[256,4096]{1,0:T(8,128)} reshape(f32[256,4,4,256]{3,2,1,0:T(4,128)} %copy_bitcast_fusion) | data formatting | bytes 8388608
  139.0 0.0 reduce-scatter.5.cloned.1.call-update
  139.0 14.6 %reduce-scatter.5.cloned.1.call-done = f32[128,4096]{1,0:T(8,128)} async-done(((f32[256,4096]{1,0:T(8,128)}), f32[128,4096]{1,0:T(8,128)}) %reduce-scatter.5.cloned.1.call-update) | async-done | bytes 2097168
  153.6 3.6 %reshape.18 = f32[128,4,4,256]{3,2,1,0:T(4,128)} reshape(f32[128,4096]{1,0:T(8,128)} %reduce-scatter.5.cloned.1.call-done) | data formatting | bytes 4194304
  157.2 2.0 %copy_bitcast_fusion.1 = f32[4,1,4,128,256]{4,2,3,0,1:T(4,128)S(1)} fusion(f32[128,4,4,256]{3,2,1,0:T(4,128)} %reshape.18), kind=kLoop, calls=%fused_computation.11 | loop fusion | bytes 4194304 | tf_op jit(solution)/shard_map/broadcast_in_dim | solution.py:77
  159.2 1.7 %copy.14 = f32[4,1,4,128,256]{4,3,2,1,0:T(8,128)} copy(f32[4,1,4,128,256]{4,2,3,0,1:T(4,128)S(1)} %copy_bitcast_fusion.1) | data formatting | bytes 4194304 | tf_op jit(solution)/shard_map/broadcast_in_dim | solution.py:77
  (1 shorter events, 0.0 us)
Async XLA Ops:
  6.5 1.6 copy-start
  6.5 147.1 %reduce-scatter.5.cloned.1.call-start = ((), (), s32[]{:S(2)}) async-start(), calls=%async_computation.1 | async-start | bytes 6291456
  10.4 7.3 %copy-start.2 = (s32[2]{0:T(128)S(1)}, s32[2]{0:T(128)}, u32[]{:S(2)}) copy-start(s32[2]{0:T(128)} %param.9) | copy-start | bytes 28
  10.4 7.3 %copy-start.3 = (f32[5,4,4]{0,2,1:T(4,128)S(1)}, f32[5,4,4]{0,2,1:T(4,128)}, u32[]{:S(2)}) copy-start(f32[5,4,4]{0,2,1:T(4,128)} %constant.9) | copy-start | bytes 964
  10.4 51.8 %copy-start.1 = (bf16[2,1,256,256]{3,2,1,0:T(8,128)(2,1)S(1)}, bf16[2,1,256,256]{3,2,1,0:T(8,128)(2,1)}, u32[]{:S(2)}) copy-start(bf16[2,1,256,256]{3,2,1,0:T(8,128)(2,1)} %param.8) | copy-start | bytes 786436
  10.6 49.7 %collective-permute-start = (bf16[1,2,4,256,256]{3,4,1,2,0:T(8,128)(2,1)S(1)}, bf16[1,2,4,256,256]{3,4,1,2,0:T(8,128)(2,1)S(1)}, u32[]{:S(2)}, u32[]{:S(2)}) collective-permute-start(bf16[1,2,4,256,256]{3,4,1,2,0:T(8,128)(2,1)S(1)} %get-tuple-element.7), channel_id=1, source_target_pairs={{0,2},{2,4},{4,6},{6,8},{8,10},{10,12},{12,14},{14,16},{16,18},{18... | collective-permute-start | bytes 3145736 | tf_op jit(solution)/shard_map/ppermute | solution.py:14
  15.5 46.7 %collective-permute-start.1 = (bf16[1,2,4,256,256]{3,4,1,2,0:T(8,128)(2,1)S(1)}, bf16[1,2,4,256,256]{3,4,1,2,0:T(8,128)(2,1)S(1)}, u32[]{:S(2)}, u32[]{:S(2)}) collective-permute-start(bf16[1,2,4,256,256]{3,4,1,2,0:T(8,128)(2,1)S(1)} %get-tuple-element.8), channel_id=1, source_target_pairs={{2,0},{4,2},{6,4},{8,6},{10,8},{12,10},{14,12},{16,14},{18,16},{20... | collective-permute-start | bytes 3145736 | tf_op jit(solution)/shard_map/ppermute | solution.py:17
  80.3 28.0 %collective-permute-start.2 = (f32[1,4,256,256]{3,0,2,1:T(1,128)S(1)}, f32[1,4,256,256]{3,0,2,1:T(1,128)S(1)}, u32[]{:S(2)}, u32[]{:S(2)}) collective-permute-start(f32[1,4,256,256]{3,0,2,1:T(1,128)S(1)} %get-tuple-element.5), channel_id=1, source_target_pairs={{2,0},{4,2},{6,4},{8,6},{10,8},{12,10},{14,12},{16,14},{18,16},{20... | collective-permute-start | bytes 3145736 | tf_op jit(solution)/shard_map/ppermute | solution.py:17
  81.6 45.9 %collective-permute-start.3 = (f32[1,4,256,256]{3,0,2,1:T(1,128)S(1)}, f32[1,4,256,256]{3,0,2,1:T(1,128)S(1)}, u32[]{:S(2)}, u32[]{:S(2)}) collective-permute-start(f32[1,4,256,256]{3,0,2,1:T(1,128)S(1)} %get-tuple-element.6), channel_id=1, source_target_pairs={{0,2},{2,4},{4,6},{6,8},{8,10},{10,12},{12,14},{14,16},{16,18},{18... | collective-permute-start | bytes 3145736 | tf_op jit(solution)/shard_map/ppermute | solution.py:14
Sparse Core Ops, SparseCore 0:
  139.1 14.4 reduce-scatter.4
where the time goes:
time: 168 us
  waiting for transfers between devices  99 us (59%)
  matrix products  18.9 us (11%)
  local copies, waits for them, and re-layouts  17.7 us (11%)
  between operations  14.2 us (8%)
  starting transfers between devices  12.3 us (7%)
  other arithmetic  5.66 us (3%)
    ppermute x2, waiting for transfers between devices, padded_2(): lax.ppermute(lax.slice_in_dim(block, block.shape[dim] - width, None, axis...  61.6 us
    ppermute x2, waiting for transfers between devices, padded_2(): lax.ppermute(lax.slice_in_dim(block, 0, width, axis=dim), axis, backward)  22.7 us
    unnamed x2, waiting for transfers between devices  14.6 us
    dot_general x1, matrix products, combine_terms(): jnp.einsum('uci,ufimy->fcmy', term_factor, mapped_vectors, precision=lax....  14.2 us
    unnamed x10, local copies, waits for them, and re-layouts  11 us
    ppermute x2, starting transfers between devices, padded_2(): lax.ppermute(lax.slice_in_dim(block, block.shape[dim] - width, None, axis...  9.7 us
    unnamed x1, other arithmetic  5.65 us
    broadcast_in_dim x2, local copies, waits for them, and re-layouts, shards(): return result[:, None]  3.64 us
  transfers between devices with their start and end apart: 5, of which 5 were waited for; matrix products, arithmetic and copies ran while one was open for 1% of the time, Pallas kernels for 0%

commit v1 on v0

v1 whole, which is shorter than its diff:
```python
import jax
import jax.numpy as jnp
from jax import lax
from jax.experimental import pallas as pl
from jax.experimental.pallas import tpu as pltpu
from jax.sharding import PartitionSpec as P

FLIP = 2
COEFFICIENTS = (
    (1.0, 1.0, 1.0, 1.0),
    (0.25, -0.25, -0.25, 0.25),
    (0.0, 0.5, 0.5, 0.0),
    (0.5, 0.5, -0.5, -0.5),
    (0.5, -0.5, 0.5, -0.5),
)
EXTRA = 16
VMEM_LIMIT = 40 * 1024 * 1024
VMEM = pl.BlockSpec(memory_space=pltpu.VMEM)
SMEM = pl.BlockSpec(memory_space=pltpu.SMEM)
ANY = pl.BlockSpec(memory_space=pl.ANY)


def coefficient(op, p):
    value = jnp.float32(COEFFICIENTS[-1][p])
    for kind in range(len(COEFFICIENTS) - 1):
        value = jnp.where(op == kind, jnp.float32(COEFFICIENTS[kind][p]), value)
    return value


def times_transpose(a, b):
    return lax.dot_general(a, b, (((1,), (1,)), ((), ())), preferred_element_type=jnp.float32)


def centre_kernel(pos, kept, op_own, op_other, psi, left_own, left_other, right_own, right_other,
                  sigma, rim, psi_buf, lefts, centre, out_buf, psi_sem, out_sem):
    nvec = psi.shape[0]
    own, half, size = left_own.shape[0], sigma.shape[3], psi.shape[4]
    terms = own + left_other.shape[0]
    loads = [pltpu.make_async_copy(psi.at[v, 0], psi_buf.at[v], psi_sem.at[v]) for v in range(nvec)]
    for load in loads:
        load.start()
    first_row, state_a = pl.multiple_of(pos[0], half), pos[1]
    for t in range(terms):
        source, k = (left_own, t) if t < own else (left_other, t - own)
        lefts[pl.ds(t * half, half), :] = source[k, 0, pl.ds(first_row, half), :]
    ops = [op_own[t] if t < own else op_other[t - own] for t in range(terms)]
    for v in range(nvec):
        loads[v].wait()
        for q in range(4):
            lifted = jnp.dot(lefts[...], psi_buf[v, q], preferred_element_type=jnp.float32)
            for t in range(terms):
                part = lifted[t * half:(t + 1) * half]
                if q in (0, 3):
                    block = (part * coefficient(ops[t], q)).astype(jnp.bfloat16)
                    slot = jnp.where(state_a == q, 0, 1)
                    rim[slot, t, pl.ds(v * half, half), :] = block
                else:
                    flipped = ops[t] == FLIP
                    factor = jnp.where(flipped, coefficient(ops[t], 3 - q), coefficient(ops[t], q))
                    slot = jnp.where(flipped, 2 - q, q - 1)
                    centre[t, pl.ds((slot * nvec + v) * half, half), :] = (part * factor).astype(
                        jnp.bfloat16
                    )
    rows = lax.broadcasted_iota(jnp.int32, (half, size), 0) + first_row
    cols = lax.broadcasted_iota(jnp.int32, (half, size), 1)
    keep = (rows < kept[0]) & (cols < kept[0])
    for slot in range(2):
        total = None
        for t in range(terms):
            r = right_own[t, 0] if t < own else right_other[t - own, 0]
            part = times_transpose(centre[t, pl.ds(slot * nvec * half, nvec * half), :], r)
            total = part if total is None else total + part
        for v in range(nvec):
            out_buf[slot, v] = jnp.where(keep, total[v * half:(v + 1) * half], 0.0)
        pltpu.make_async_copy(out_buf.at[slot], sigma.at[:, 0, slot + 1], out_sem.at[slot]).start()
    for slot in range(2):
        pltpu.make_async_copy(out_buf.at[slot], sigma.at[:, 0, slot + 1], out_sem.at[slot]).wait()


def make_rim_kernel(which):
    def kernel(pos, kept, rim, right_own, right_other, sigma_in, sigma, out_buf, out_sem):
        nvec, half, size = out_buf.shape
        terms = rim.shape[1]
        own = terms // 2 if right_own.shape[0] != right_other.shape[0] else 0
        total = None
        for t in range(terms):
            source, k = (right_own, t) if t < own else (right_other, t - own)
            part = times_transpose(rim[which, t], source[k * size:(k + 1) * size])
            total = part if total is None else total + part
        note = right_own if right_own.shape[0] > right_other.shape[0] else right_other
        edge = note[own * size:own * size + 1].astype(jnp.float32)
        rows = lax.broadcasted_iota(jnp.int32, (half, size), 0) + pos[0]
        cols = lax.broadcasted_iota(jnp.int32, (half, size), 1).astype(jnp.float32)
        keep = (rows < kept[0]) & (cols < edge) & (pos[3 + which] > 0)
        for v in range(nvec):
            out_buf[v] = jnp.where(keep, total[v * half:(v + 1) * half], 0.0)
        copy = pltpu.make_async_copy(out_buf, sigma.at[:, 0, pos[1 + which]], out_sem)
        copy.start()
        copy.wait()

    return kernel


def with_note(blocks, kept_rows):
    size = blocks.shape[-1]
    note = jnp.broadcast_to(kept_rows.astype(blocks.dtype)[:, None], (EXTRA, size))
    return jnp.concatenate([blocks.reshape(-1, size), note], 0)


def two_core_cycle(sectors):
    up = [(2 * i, 2 * i + 2) for i in range(sectors - 1)]
    down = [(2 * i + 3, 2 * i + 1) for i in range(sectors - 1)]
    return up + [(2 * sectors - 2, 2 * sectors - 1)] + down + [(1, 0)]


def shards(psi, left_env, right_env, op_index, kept_rows):
    sectors, cores = lax.axis_size("sector"), lax.axis_size("term")
    me, core = lax.axis_index("sector"), lax.axis_index("term")
    nvec, size = psi.shape[0], psi.shape[-1]
    half = size // cores
    terms = left_env.shape[0] * cores
    has_below, has_above = me > 0, me < sectors - 1
    swap = [(0, 1), (1, 0)]

    if cores == 2:
        below_is_a = core == 0
        cycle = two_core_cycle(sectors)
        reverse = [(b, a) for a, b in cycle]
        own_a = lax.ppermute(right_env, ("sector", "term"), cycle)
        own_b = lax.ppermute(with_note(right_env, kept_rows), ("sector", "term"), reverse)
        left_own, right_own, op_own = left_env, right_env, op_index
        left_other = lax.ppermute(left_env, "term", swap)
        right_other = lax.ppermute(right_env, "term", swap)
        op_other = lax.ppermute(op_index, "term", swap)
    else:
        below_is_a = core >= 0
        forward = [(i, i + 1) for i in range(sectors - 1)]
        backward = [(b, a) for a, b in forward]
        gathered = [lax.all_gather(x, "term", tiled=True) for x in (left_env, right_env, op_index)]
        (left_own, left_other), (right_own, right_other), (op_own, op_other) = [
            jnp.split(x, 2) for x in gathered
        ]

        def neighbour(pairs):
            blocks = lax.all_gather(lax.ppermute(right_env, "sector", pairs), "term", tiled=True)
            first, second = jnp.split(blocks, 2)
            return first, second, lax.ppermute(kept_rows, "sector", pairs)

        own_a, other_a, kept_a = neighbour(forward)
        own_b, other_b, kept_b = neighbour(backward)
        other_a, own_b = with_note(other_a, kept_a), with_note(own_b, kept_b)

    state_a = jnp.where(below_is_a, 3, 0)
    has_a = jnp.where(below_is_a, has_below, has_above)
    has_b = jnp.where(below_is_a, has_above, has_below)
    pos = jnp.stack([core * half, state_a, 3 - state_a, has_a, has_b]).astype(jnp.int32)

    sigma_shape = jax.ShapeDtypeStruct((nvec, 1, 4, half, size), jnp.float32)
    rim_shape = jax.ShapeDtypeStruct((2, terms, nvec * half, size), jnp.bfloat16)
    block = size * size
    sigma, rim = pl.pallas_call(
        centre_kernel,
        out_shape=(sigma_shape, rim_shape),
        in_specs=[SMEM, SMEM, SMEM, SMEM, ANY, VMEM, VMEM, VMEM, VMEM],
        out_specs=(ANY, VMEM),
        scratch_shapes=[
            pltpu.VMEM((nvec, 4, size, size), jnp.bfloat16),
            pltpu.VMEM((terms * half, size), jnp.bfloat16),
            pltpu.VMEM((terms, 2 * nvec * half, size), jnp.bfloat16),
            pltpu.VMEM((2, nvec, half, size), jnp.float32),
            pltpu.SemaphoreType.DMA((nvec,)),
            pltpu.SemaphoreType.DMA((2,)),
        ],
        compiler_params=pltpu.CompilerParams(vmem_limit_bytes=VMEM_LIMIT),
        cost_estimate=pl.CostEstimate(
            flops=12 * nvec * terms * half * block, bytes_accessed=14 * nvec * block, transcendentals=0
        ),
        name="centre",
    )(pos, kept_rows, op_own, op_other, psi, left_own, left_other, right_own, right_other)

    def finish(which, sigma, rim, right_own, right_other):
        return pl.pallas_call(
            make_rim_kernel(which),
            out_shape=sigma_shape,
            in_specs=[SMEM, SMEM, VMEM, VMEM, VMEM, ANY],
            out_specs=ANY,
            scratch_shapes=[pltpu.VMEM((nvec, half, size), jnp.float32), pltpu.SemaphoreType.DMA],
            input_output_aliases={5: 0},
            compiler_params=pltpu.CompilerParams(vmem_limit_bytes=VMEM_LIMIT),
            cost_estimate=pl.CostEstimate(
                flops=2 * nvec * terms * half * block, bytes_accessed=4 * nvec * block, transcendentals=0
            ),
            name="rim",
        )(pos, kept_rows, rim, right_own, right_other, sigma)

    own_a, sigma, rim = lax.optimization_barrier((own_a.reshape(-1, size), sigma, rim))
    if cores == 2:
        other_b = lax.ppermute(own_a, "term", swap)
        own_b, other_b = lax.optimization_barrier((own_b, other_b))
        other_a = lax.ppermute(own_b, "term", swap)
    sigma = finish(1, sigma, rim, own_b, other_b.reshape(-1, size))
    return finish(0, sigma, rim, own_a, other_a)


def solution(mesh):
    in_specs = (
        P(None, "sector", None, None, None),
        P("term", "sector", None, None),
        P("term", "sector", None, None),
        P("term"),
        P("sector"),
    )
    out_specs = P(None, "sector", None, "term", None)
    return jax.shard_map(shards, mesh=mesh, in_specs=in_specs, out_specs=out_specs, check_vma=False)
```

time: 168 us -> 20.7 us (0.12)
  waiting for transfers between devices: 99 us -> 2.57 us
  matrix products: 18.9 us -> 0 us
  between operations: 14.2 us -> 0.71 us
  local copies, waits for them, and re-layouts: 17.7 us -> 5.19 us
  starting transfers between devices: 12.3 us -> 4.28 us
  Pallas kernels: 0 us -> 7.68 us
  other arithmetic: 5.66 us -> 0 us
    ppermute x4 -> x7, waiting for transfers between devices: 84.4 us -> 2.57 us  [the longest x1 1.16 us: shards(): own_a = lax.ppermute(right_env, ('sector', 'term'), cycle)]
    dot_general x4 -> x0, matrix products: 18.9 us -> none  [the longest x1 14.2 us: combine_terms(): jnp.einsum('uci,ufimy->fcmy', term_factor, mapped_vectors, precision=lax....]
    unnamed x2 -> x0, waiting for transfers between devices: 14.6 us -> none
    ppermute x4 -> x7, starting transfers between devices: 12.3 us -> 4.28 us  [the longest x1 2.94 us: shards(): own_a = lax.ppermute(right_env, ('sector', 'term'), cycle)]
    pallas_call x0 -> x3, Pallas kernels: none -> 7.68 us  [the longest x1 4.06 us: shards(): pl.pallas_call(centre_kernel, out_shape=(sigma_shape, rim_shape), in_spec...]
    unnamed x10 -> x8, local copies, waits for them, and re-layouts: 11 us -> 4.14 us
    unnamed x1 -> x0, other arithmetic: 5.65 us -> none
    broadcast_in_dim x2 -> x0, local copies, waits for them, and re-layouts: 3.64 us -> none  [shards(): return result[:, None]]
  transfers between devices with their start and end apart: 5 -> 7, of which waited for: 5 -> 3; matrix products, arithmetic and copies ran while one was open for 1% -> 5% of each run, Pallas kernels for 0% -> 29%
where the time goes in v1:
time: 20.7 us; the launch traced here: 20.4 us
  Pallas kernels  7.68 us (37%)
  local copies, waits for them, and re-layouts  5.19 us (25%)
  starting transfers between devices  4.28 us (21%)
  waiting for transfers between devices  2.57 us (12%)
  between operations  0.71 us (3%)
    unnamed x8, local copies, waits for them, and re-layouts  4.14 us
    pallas_call x1, Pallas kernels, shards(): pl.pallas_call(centre_kernel, out_shape=(sigma_shape, rim_shape), in_spec...  4.06 us
    pallas_call x2, Pallas kernels, finish(): pl.pallas_call(make_rim_kernel(which), out_shape=sigma_shape, in_specs=[S...  3.63 us
    ppermute x1, starting transfers between devices, shards(): own_a = lax.ppermute(right_env, ('sector', 'term'), cycle)  2.94 us
    ppermute x1, waiting for transfers between devices, shards(): own_a = lax.ppermute(right_env, ('sector', 'term'), cycle)  1.16 us
    concatenate x1, local copies, waits for them, and re-layouts, with_note(): return jnp.concatenate([blocks.reshape(-1, size), note], 0)  0.97 us
    ppermute x1, waiting for transfers between devices, shards(): other_b = lax.ppermute(own_a, 'term', swap)  0.73 us
    ppermute x1, waiting for transfers between devices, shards(): lax.ppermute(with_note(right_env, kept_rows), ('sector', 'term'), reverse)  0.68 us
  transfers between devices with their start and end apart: 7, of which 3 were waited for; matrix products, arithmetic and copies ran while one was open for 5% of the time, Pallas kernels for 29%

profile of v1, /device:TPU:0, one launch (start us, length us, event | category | flops | bytes accessed | tf_op | source)
XLA Modules:
  0.0 20.4 jit_solution(18369617506795417021)
XLA Ops:
  0.0 0.5 %collective-permute-start.2 = (bf16[2,1,256,256]{3,2,1,0:T(8,128)(2,1)}, bf16[2,1,256,256]{3,2,1,0:T(8,128)(2,1)S(1)}, u32[]{:S(2)}, u32[]{:S(2)}) collective-permute-start(bf16[2,1,256,256]{3,2,1,0:T(8,128)(2,1)} %left_own.1), channel_id=1, source_target_pairs={{0,1},{1,0},{2,3},{3,2},{4,5},{5,4},{6,7},{7,6},{8,9},{9,8},{10,11... | collective-permute-start | bytes 786440 | tf_op jit(solution)/shard_map/ppermute | solution.py:132
  0.5 0.1 collective-permute-start.3
  0.5 2.9 %collective-permute-start = (bf16[2,1,256,256]{3,2,1,0:T(8,128)(2,1)}, bf16[2,1,256,256]{3,2,1,0:T(8,128)(2,1)S(1)}, u32[]{:S(2)}, u32[]{:S(2)}) collective-permute-start(bf16[2,1,256,256]{3,2,1,0:T(8,128)(2,1)} %right_own.1), channel_id=1, source_target_pairs={{0,2},{2,4},{4,6},{6,8},{8,10},{10,12},{12,14},{14,16},{16,18},{18... | collective-permute-start | bytes 786440 | tf_op jit(solution)/shard_map/ppermute | solution.py:129
  3.5 0.0 collective-permute-start.1
  4.1 1.0 %concatenate.3 = bf16[528,256]{1,0:T(8,128)(2,1)S(1)} pad(bf16[512,256]{1,0:T(8,128)(2,1)} %bitcast.10, bf16[]{:T(256)} %bitcast.7), padding=0_16x0_0 | pad | bytes 532482 | tf_op jit(solution)/shard_map/concatenate | solution.py:107
  5.1 0.6 %collective-permute-start.4 = (bf16[528,256]{1,0:T(8,128)(2,1)S(1)}, bf16[528,256]{1,0:T(8,128)(2,1)S(1)}, u32[]{:S(2)}, u32[]{:S(2)}) collective-permute-start(bf16[528,256]{1,0:T(8,128)(2,1)S(1)} %concatenate.3), channel_id=1, source_target_pairs={{2,0},{4,2},{6,4},{8,6},{10,8},{12,10},{14,12},{16,14},{18,16},{20... | collective-permute-start | bytes 811016 | tf_op jit(solution)/shard_map/ppermute | solution.py:130
  5.6 0.1 stack.31.pos
  5.7 0.0 collective-permute-done.1.op_other
  5.7 0.0 collective-permute-done.2.left_other
  5.7 0.0 collective-permute-done.3.right_other
  5.7 0.0 copy-start
  5.8 0.9 %copy-done = bf16[2,1,256,256]{3,2,1,0:T(8,128)(2,1)S(1)} copy-done((bf16[2,1,256,256]{3,2,1,0:T(8,128)(2,1)S(1)}, bf16[2,1,256,256]{3,2,1,0:T(8,128)(2,1)}, u32[]{:S(2)}) %copy-start) | copy-done | bytes 262168
  6.7 0.0 copy-start.1
  6.7 1.6 %copy-done.1 = bf16[4,1,4,256,256]{4,3,2,1,0:T(8,128)(2,1)S(1)} copy-done((bf16[4,1,4,256,256]{4,3,2,1,0:T(8,128)(2,1)S(1)}, bf16[4,1,4,256,256]{4,3,2,1,0:T(8,128)(2,1)}, u32[]{:S(2)}) %copy-start.1) | copy-done | bytes 2097176
  8.3 0.0 copy-start.2
  8.3 0.9 %copy-done.2 = bf16[2,1,256,256]{3,2,1,0:T(8,128)(2,1)S(1)} copy-done((bf16[2,1,256,256]{3,2,1,0:T(8,128)(2,1)S(1)}, bf16[2,1,256,256]{3,2,1,0:T(8,128)(2,1)}, u32[]{:S(2)}) %copy-start.2) | copy-done | bytes 262168
  9.2 0.0 copy-start.3
  9.2 0.7 %copy-done.3 = s32[2]{0:T(128)S(1)} copy-done((s32[2]{0:T(128)S(1)}, s32[2]{0:T(128)}, u32[]{:S(2)}) %copy-start.3) | copy-done | bytes 32
  9.9 4.1 %centre.1 = (f32[4,1,4,128,256]{4,3,2,1,0:T(8,128)}, bf16[2,4,512,256]{3,2,1,0:T(8,128)(2,1)S(1)}) custom-call(s32[5]{0:T(128)S(1)} %stack.31.pos, s32[1]{0:T(128)S(6)} %copy.10.kept, s32[2]{0:T(128)S(1)} %copy-done.3, s32[2]{0:T(128)S(1)} %collective-permute-done.1.op_other, bf16[4,1,4,256,256]{4,3,2,1,0:T(8,128)(2,1)S(1)} %copy-done.1, ...), custom_call_target="tpu_custom_call" | custom-call | flops 1610612736 | bytes 3670016 | tf_op jit(solution)/shard_map/centre/pallas_call | solution.py:161
  14.0 1.2 %collective-permute-done = bf16[2,1,256,256]{3,2,1,0:T(8,128)(2,1)S(1)} collective-permute-done((bf16[2,1,256,256]{3,2,1,0:T(8,128)(2,1)}, bf16[2,1,256,256]{3,2,1,0:T(8,128)(2,1)S(1)}, u32[]{:S(2)}, u32[]{:S(2)}) %collective-permute-start) | collective-permute-done | bytes 262176 | tf_op jit(solution)/shard_map/ppermute | solution.py:129
  15.1 0.1 collective-permute-start.5
  15.2 0.7 %collective-permute-done.4.right_own = bf16[528,256]{1,0:T(8,128)(2,1)S(1)} collective-permute-done((bf16[528,256]{1,0:T(8,128)(2,1)S(1)}, bf16[528,256]{1,0:T(8,128)(2,1)S(1)}, u32[]{:S(2)}, u32[]{:S(2)}) %collective-permute-start.4) | collective-permute-done | bytes 270368 | tf_op jit(solution)/shard_map/ppermute | solution.py:130
  15.9 0.7 %collective-permute-done.5.right_other = bf16[512,256]{1,0:T(8,128)(2,1)S(1)} collective-permute-done((bf16[512,256]{1,0:T(8,128)(2,1)S(1)}, bf16[512,256]{1,0:T(8,128)(2,1)S(1)}, u32[]{:S(2)}, u32[]{:S(2)}) %collective-permute-start.5) | collective-permute-done | bytes 262176 | tf_op jit(solution)/shard_map/ppermute | solution.py:198
  16.7 0.1 collective-permute-start.6
  16.8 1.8 %rim.2.sigma_in = f32[4,1,4,128,256]{4,3,2,1,0:T(8,128)} custom-call(s32[5]{0:T(128)S(1)} %stack.31.pos, s32[1]{0:T(128)S(6)} %copy.10.kept, bf16[2,4,512,256]{3,2,1,0:T(8,128)(2,1)S(1)} %get-tuple-element.14.rim, bf16[528,256]{1,0:T(8,128)(2,1)S(1)} %collective-permute-done.4.right_own, ...), custom_call_target="tpu_custom_call", output_to_operand_aliasing={{}: (5, {})} | custom-call | flops 268435456 | bytes 1048576 | tf_op jit(solution)/shard_map/rim/pallas_call | solution.py:182
  18.6 0.0 collective-permute-done.6.right_other
  18.6 1.8 %rim.3 = f32[4,1,4,128,256]{4,3,2,1,0:T(8,128)} custom-call(s32[5]{0:T(128)S(1)} %stack.31.pos, s32[1]{0:T(128)S(6)} %copy.10.kept, bf16[2,4,512,256]{3,2,1,0:T(8,128)(2,1)S(1)} %get-tuple-element.14.rim, bf16[512,256]{1,0:T(8,128)(2,1)S(1)} %bitcast.9, bf16[528,256]{1,0:T(8,128)(2,1)S(1)} %collective-permute-done.6.right_other, ...), custom_call_target="tpu_custom_call", output_to_operand_aliasing={{}: (5, {})} | custom-call | flops 268435456 | bytes 1048576 | tf_op jit(solution)/shard_map/rim/pallas_call | solution.py:182
Async XLA Ops:
  0.0 5.7 %collective-permute-start.2 = (bf16[2,1,256,256]{3,2,1,0:T(8,128)(2,1)}, bf16[2,1,256,256]{3,2,1,0:T(8,128)(2,1)S(1)}, u32[]{:S(2)}, u32[]{:S(2)}) collective-permute-start(bf16[2,1,256,256]{3,2,1,0:T(8,128)(2,1)} %left_own.1), channel_id=1, source_target_pairs={{0,1},{1,0},{2,3},{3,2},{4,5},{5,4},{6,7},{7,6},{8,9},{9,8},{10,11... | collective-permute-start | bytes 786440 | tf_op jit(solution)/shard_map/ppermute | solution.py:132
  0.5 5.3 %collective-permute-start.3 = (bf16[2,1,256,256]{3,2,1,0:T(8,128)(2,1)}, bf16[2,1,256,256]{3,2,1,0:T(8,128)(2,1)S(1)}, u32[]{:S(2)}, u32[]{:S(2)}) collective-permute-start(bf16[2,1,256,256]{3,2,1,0:T(8,128)(2,1)} %right_own.1), channel_id=1, source_target_pairs={{0,1},{1,0},{2,3},{3,2},{4,5},{5,4},{6,7},{7,6},{8,9},{9,8},{10,11... | collective-permute-start | bytes 786440 | tf_op jit(solution)/shard_map/ppermute | solution.py:133
  0.5 14.6 %collective-permute-start = (bf16[2,1,256,256]{3,2,1,0:T(8,128)(2,1)}, bf16[2,1,256,256]{3,2,1,0:T(8,128)(2,1)S(1)}, u32[]{:S(2)}, u32[]{:S(2)}) collective-permute-start(bf16[2,1,256,256]{3,2,1,0:T(8,128)(2,1)} %right_own.1), channel_id=1, source_target_pairs={{0,2},{2,4},{4,6},{6,8},{8,10},{10,12},{12,14},{14,16},{16,18},{18... | collective-permute-start | bytes 786440 | tf_op jit(solution)/shard_map/ppermute | solution.py:129
  3.5 2.3 %collective-permute-start.1 = (s32[2]{0:T(128)}, s32[2]{0:T(128)S(1)}, u32[]{:S(2)}, u32[]{:S(2)}) collective-permute-start(s32[2]{0:T(128)} %op_own.1), channel_id=1, source_target_pairs={{0,1},{1,0},{2,3},{3,2},{4,5},{5,4},{6,7},{7,6},{8,9},{9,8},{10,11... | collective-permute-start | bytes 32 | tf_op jit(solution)/shard_map/ppermute | solution.py:134
  5.1 10.8 %collective-permute-start.4 = (bf16[528,256]{1,0:T(8,128)(2,1)S(1)}, bf16[528,256]{1,0:T(8,128)(2,1)S(1)}, u32[]{:S(2)}, u32[]{:S(2)}) collective-permute-start(bf16[528,256]{1,0:T(8,128)(2,1)S(1)} %concatenate.3), channel_id=1, source_target_pairs={{2,0},{4,2},{6,4},{8,6},{10,8},{12,10},{14,12},{16,14},{18,16},{20... | collective-permute-start | bytes 811016 | tf_op jit(solution)/shard_map/ppermute | solution.py:130
  5.7 1.0 %copy-start = (bf16[2,1,256,256]{3,2,1,0:T(8,128)(2,1)S(1)}, bf16[2,1,256,256]{3,2,1,0:T(8,128)(2,1)}, u32[]{:S(2)}) copy-start(bf16[2,1,256,256]{3,2,1,0:T(8,128)(2,1)} %right_own.1) | copy-start | bytes 786436
  6.7 1.6 %copy-start.1 = (bf16[4,1,4,256,256]{4,3,2,1,0:T(8,128)(2,1)S(1)}, bf16[4,1,4,256,256]{4,3,2,1,0:T(8,128)(2,1)}, u32[]{:S(2)}) copy-start(bf16[4,1,4,256,256]{4,3,2,1,0:T(8,128)(2,1)} %psi.1) | copy-start | bytes 6291460
  8.3 0.9 %copy-start.2 = (bf16[2,1,256,256]{3,2,1,0:T(8,128)(2,1)S(1)}, bf16[2,1,256,256]{3,2,1,0:T(8,128)(2,1)}, u32[]{:S(2)}) copy-start(bf16[2,1,256,256]{3,2,1,0:T(8,128)(2,1)} %left_own.1) | copy-start | bytes 786436
  9.2 0.7 %copy-start.3 = (s32[2]{0:T(128)S(1)}, s32[2]{0:T(128)}, u32[]{:S(2)}) copy-start(s32[2]{0:T(128)} %op_own.1) | copy-start | bytes 28
  15.1 1.5 %collective-permute-start.5 = (bf16[512,256]{1,0:T(8,128)(2,1)S(1)}, bf16[512,256]{1,0:T(8,128)(2,1)S(1)}, u32[]{:S(2)}, u32[]{:S(2)}) collective-permute-start(bf16[512,256]{1,0:T(8,128)(2,1)S(1)} %bitcast.8), channel_id=1, source_target_pairs={{0,1},{1,0},{2,3},{3,2},{4,5},{5,4},{6,7},{7,6},{8,9},{9,8},{10,11... | collective-permute-start | bytes 786440 | tf_op jit(solution)/shard_map/ppermute | solution.py:198
  16.7 2.0 %collective-permute-start.6 = (bf16[528,256]{1,0:T(8,128)(2,1)S(1)}, bf16[528,256]{1,0:T(8,128)(2,1)S(1)}, u32[]{:S(2)}, u32[]{:S(2)}) collective-permute-start(bf16[528,256]{1,0:T(8,128)(2,1)S(1)} %collective-permute-done.4.right_own), channel_id=1, source_target_pairs={{0,1},{1,0},{2,3},{3,2},{4,5},{5,4},{6,7},{7,6},{8,9},{9,8},{10,11... | collective-permute-start | bytes 811016 | tf_op jit(solution)/shard_map/ppermute | solution.py:200

commit v2 on v1

v2 whole, which is shorter than its diff:
```python
import jax
import jax.numpy as jnp
from jax import lax
from jax.experimental import pallas as pl
from jax.experimental.pallas import tpu as pltpu
from jax.sharding import PartitionSpec as P

FLIP = 2
COEFFICIENTS = (
    (1.0, 1.0, 1.0, 1.0),
    (0.25, -0.25, -0.25, 0.25),
    (0.0, 0.5, 0.5, 0.0),
    (0.5, 0.5, -0.5, -0.5),
    (0.5, -0.5, 0.5, -0.5),
)
VMEM_LIMIT = 16 * 1024 * 1024
CENTRE_LIMIT = 50 * 1024 * 1024
VMEM = pl.BlockSpec(memory_space=pltpu.VMEM)
SMEM = pl.BlockSpec(memory_space=pltpu.SMEM)
HBM = pl.BlockSpec(memory_space=pltpu.HBM)


def coefficient(op, p):
    value = jnp.float32(COEFFICIENTS[-1][p])
    for kind in range(len(COEFFICIENTS) - 1):
        value = jnp.where(op == kind, jnp.float32(COEFFICIENTS[kind][p]), value)
    return value


def times_transpose(a, b):
    return lax.dot_general(a, b, (((1,), (1,)), ((), ())), preferred_element_type=jnp.float32)


def below_is_a():
    return lax.axis_index("term") == 0 if lax.axis_size("term") == 2 else True


def centre_kernel(pos, psi, left_own, left_other, right_own, right_other, sigma, rim, kept_row,
                  psi_buf, left_buf, right_buf, lefts, centre, out_buf, psi_sem, env_sem, out_sem):
    nvec = psi.shape[0]
    own, half, size = left_own.shape[0], sigma.shape[3], psi.shape[4]
    terms = own + left_other.shape[0]
    envs = [
        pltpu.make_async_copy(left_own.at[:, 0], left_buf, env_sem.at[0]),
        pltpu.make_async_copy(right_own.at[:, 0], right_buf, env_sem.at[1]),
    ]
    loads = [pltpu.make_async_copy(psi.at[v, 0], psi_buf.at[v], psi_sem.at[v]) for v in range(nvec)]
    for copy in [envs[0]] + loads + [envs[1]]:
        copy.start()
    first_row = pl.multiple_of(lax.axis_index("term") * half, half)
    slot_of_3 = jnp.where(below_is_a(), 0, 1)
    kept = pos[0]
    ops = [pos[1 + t] for t in range(terms)]
    kept_row[...] = jnp.full(kept_row.shape, kept, jnp.float32)
    envs[0].wait()
    for t in range(own):
        lefts[pl.ds(t * half, half), :] = left_buf[t, pl.ds(first_row, half), :]
    for t in range(own, terms):
        lefts[pl.ds(t * half, half), :] = left_other[t - own, 0, pl.ds(first_row, half), :]
    for v in range(nvec):
        loads[v].wait()
        for q in range(4):
            lifted = jnp.dot(lefts[...], psi_buf[v, q], preferred_element_type=jnp.float32)
            for t in range(terms):
                part = lifted[t * half:(t + 1) * half]
                if q in (0, 3):
                    slot = slot_of_3 if q == 3 else 1 - slot_of_3
                    block = (part * coefficient(ops[t], q)).astype(jnp.bfloat16)
                    rim[slot, t, pl.ds(v * half, half), :] = block
                else:
                    flipped = ops[t] == FLIP
                    factor = jnp.where(flipped, coefficient(ops[t], 3 - q), coefficient(ops[t], q))
                    slot = jnp.where(flipped, 2 - q, q - 1)
                    block = (part * factor).astype(jnp.bfloat16)
                    centre[t, pl.ds((slot * nvec + v) * half, half), :] = block
    rows = lax.broadcasted_iota(jnp.int32, (half, size), 0) + first_row
    keep = (rows < kept) & (lax.broadcasted_iota(jnp.int32, (half, size), 1) < kept)
    envs[1].wait()
    stores = []
    for slot in range(2):
        total = None
        for t in range(terms):
            right = right_buf[t] if t < own else right_other[t - own, 0]
            part = times_transpose(centre[t, pl.ds(slot * nvec * half, nvec * half), :], right)
            total = part if total is None else total + part
        for v in range(nvec):
            out_buf[slot, v] = jnp.where(keep, total[v * half:(v + 1) * half], 0.0)
        stores.append(
            pltpu.make_async_copy(out_buf.at[slot], sigma.at[:, 0, slot + 1], out_sem.at[slot])
        )
        stores[-1].start()
    for store in stores:
        store.wait()


def sum_terms(rim, which, first, blocks, count, rows, total=None):
    size = rim.shape[-1]
    for k in range(count):
        product = times_transpose(rim[which, first + k, rows, :], blocks[k * size:(k + 1) * size])
        total = product if total is None else total + product
    return total


def state_mask(which, kept_row, note, half):
    is_below = (which == 0) == below_is_a()
    me = lax.axis_index("sector")
    there = jnp.where(is_below, me, lax.axis_size("sector") - 1 - me) > 0
    shape = (half, kept_row.shape[1])
    rows = lax.broadcasted_iota(jnp.int32, shape, 0) + lax.axis_index("term") * half
    cols = lax.broadcasted_iota(jnp.int32, shape, 1)
    keep = (rows.astype(jnp.float32) < kept_row[0:1, :]) & there
    return keep & (cols.astype(jnp.float32) < note[0:1, :]), jnp.where(is_below, 3, 0)


def own_rim_kernel(rim, own_a, own_b, part_a, part_b):
    count, rows = own_a.shape[0] // rim.shape[-1], pl.ds(0, rim.shape[2])
    part_a[...] = sum_terms(rim, 0, 0, own_a, count, rows)
    part_b[...] = sum_terms(rim, 1, 0, own_b, count, rows)


def last_rim_kernel(kept_row, note_a, note_b, rim, other_a, other_b, part_a, part_b, sigma_in, sigma,
                    out_buf, out_sem):
    _, nvec, half, size = out_buf.shape
    count, groups = other_a.shape[0] // size, out_sem.shape[1]
    first, per_group = rim.shape[1] - count, nvec // groups
    stores = []
    for which, note, blocks, part in ((0, note_a, other_a, part_a), (1, note_b, other_b, part_b)):
        keep, state = state_mask(which, kept_row, note, half)
        for group in range(groups):
            rows = pl.ds(group * per_group * half, per_group * half)
            total = sum_terms(rim, which, first, blocks, count, rows, part[rows, :])
            for j in range(per_group):
                out_buf[which, group * per_group + j] = jnp.where(
                    keep, total[j * half:(j + 1) * half], 0.0
                )
            vectors = pl.ds(group * per_group, per_group)
            store = pltpu.make_async_copy(
                out_buf.at[which, vectors], sigma.at[vectors, 0, state], out_sem.at[which, group]
            )
            store.start()
            stores.append(store)
    for store in stores:
        store.wait()


def note_of(kept_rows, size):
    return jnp.broadcast_to(kept_rows.astype(jnp.float32)[:, None], (8, size))


def two_core_cycle(sectors):
    up = [(2 * i, 2 * i + 2) for i in range(sectors - 1)]
    down = [(2 * i + 3, 2 * i + 1) for i in range(sectors - 1)]
    return up + [(2 * sectors - 2, 2 * sectors - 1)] + down + [(1, 0)]


def shards(psi, left_env, right_env, op_index, kept_rows):
    sectors, cores = lax.axis_size("sector"), lax.axis_size("term")
    nvec, size = psi.shape[0], psi.shape[-1]
    half = size // cores
    terms = left_env.shape[0] * cores
    swap = [(0, 1), (1, 0)]

    if cores == 2:
        cycle = two_core_cycle(sectors)
        reverse = [(b, a) for a, b in cycle]
        own_a = lax.ppermute(right_env, ("sector", "term"), cycle)
        own_b = lax.ppermute(right_env, ("sector", "term"), reverse)
        note_a = lax.ppermute(note_of(kept_rows, size), ("sector", "term"), cycle)
        left_own, right_own, op_own = left_env, right_env, op_index
        left_other = lax.ppermute(left_env, "term", swap)
        right_other = lax.ppermute(right_env, "term", swap)
        op_other = lax.ppermute(op_index, "term", swap)
    else:
        forward = [(i, i + 1) for i in range(sectors - 1)]
        backward = [(b, a) for a, b in forward]
        gathered = [lax.all_gather(x, "term", tiled=True) for x in (left_env, right_env, op_index)]
        (left_own, left_other), (right_own, right_other), (op_own, op_other) = [
            jnp.split(x, 2) for x in gathered
        ]

        def neighbour(pairs):
            blocks = lax.all_gather(lax.ppermute(right_env, "sector", pairs), "term", tiled=True)
            note = lax.ppermute(note_of(kept_rows, size), "sector", pairs)
            return *jnp.split(blocks, 2), note

        own_a, other_a, note_a = neighbour(forward)
        own_b, other_b, note_b = neighbour(backward)

    pos = jnp.concatenate([kept_rows, op_own, op_other])
    sigma_shape = jax.ShapeDtypeStruct((nvec, 1, 4, half, size), jnp.float32)
    rim_shape = jax.ShapeDtypeStruct((2, terms, nvec * half, size), jnp.bfloat16)
    part_shape = jax.ShapeDtypeStruct((nvec * half, size), jnp.float32)
    kept_shape = jax.ShapeDtypeStruct((8, size), jnp.float32)
    params = pltpu.CompilerParams(vmem_limit_bytes=VMEM_LIMIT)

    groups = 2 if nvec % 2 == 0 else 1
    sigma, rim, kept_row = pl.pallas_call(
        centre_kernel,
        out_shape=(sigma_shape, rim_shape, kept_shape),
        in_specs=[SMEM, HBM, HBM, VMEM, HBM, VMEM],
        out_specs=(HBM, VMEM, VMEM),
        scratch_shapes=[
            pltpu.VMEM((nvec, 4, size, size), jnp.bfloat16),
            pltpu.VMEM((left_own.shape[0], size, size), jnp.bfloat16),
            pltpu.VMEM((right_own.shape[0], size, size), jnp.bfloat16),
            pltpu.VMEM((terms * half, size), jnp.bfloat16),
            pltpu.VMEM((terms, 2 * nvec * half, size), jnp.bfloat16),
            pltpu.VMEM((2, nvec, half, size), jnp.float32),
            pltpu.SemaphoreType.DMA((nvec,)),
            pltpu.SemaphoreType.DMA((2,)),
            pltpu.SemaphoreType.DMA((2,)),
        ],
        compiler_params=pltpu.CompilerParams(vmem_limit_bytes=CENTRE_LIMIT),
        name="centre",
    )(pos, psi, left_own, left_other, right_own, right_other)

    own_a, own_b, note_a, sigma, rim = lax.optimization_barrier((own_a, own_b, note_a, sigma, rim))
    if cores == 2:
        other_b = lax.ppermute(own_a, "term", swap)
        other_a = lax.ppermute(own_b, "term", swap)
        note_b = lax.ppermute(note_a, "term", swap)
    own_a, own_b, other_a, other_b = [
        x.reshape(-1, size) for x in (own_a, own_b, other_a, other_b)
    ]
    part_a, part_b = pl.pallas_call(
        own_rim_kernel,
        out_shape=(part_shape, part_shape),
        in_specs=[VMEM] * 3,
        out_specs=(VMEM, VMEM),
        compiler_params=params,
        name="own_rim",
    )(rim, own_a, own_b)
    return pl.pallas_call(
        last_rim_kernel,
        out_shape=sigma_shape,
        in_specs=[VMEM] * 8 + [HBM],
        out_specs=HBM,
        scratch_shapes=[
            pltpu.VMEM((2, nvec, half, size), jnp.float32),
            pltpu.SemaphoreType.DMA((2, groups)),
        ],
        input_output_aliases={8: 0},
        compiler_params=params,
        name="last_rim",
    )(kept_row, note_a, note_b, rim, other_a, other_b, part_a, part_b, sigma)


def solution(mesh):
    in_specs = (
        P(None, "sector", None, None, None),
        P("term", "sector", None, None),
        P("term", "sector", None, None),
        P("term"),
        P("sector"),
    )
    out_specs = P(None, "sector", None, "term", None)
    return jax.shard_map(shards, mesh=mesh, in_specs=in_specs, out_specs=out_specs, check_vma=False)
```

time: 20.7 us -> 19.5 us (0.942)
  starting transfers between devices: 4.28 us -> 7.86 us
  local copies, waits for them, and re-layouts: 5.19 us -> 1.9 us
  waiting for transfers between devices: 2.57 us -> 1.18 us
  other arithmetic: 0 us -> 0.73 us
  Pallas kernels: 7.68 us -> 6.95 us
    ppermute x1 -> x3, starting transfers between devices: 0.56 us -> 3.81 us  [the longest x1 2.92 us: shards(): note_a = lax.ppermute(note_of(kept_rows, size), ('sector', 'term'), cycle)]
    unnamed x8 -> x4, local copies, waits for them, and re-layouts: 4.14 us -> 1.9 us
    ppermute x1, waiting for transfers between devices: 1.16 us -> 0.01 us  [shards(): own_a = lax.ppermute(right_env, ('sector', 'term'), cycle)]
    concatenate x1 -> x0, local copies, waits for them, and re-layouts: 0.97 us -> none  [with_note(): return jnp.concatenate([blocks.reshape(-1, size), note], 0)]
    ppermute x1, starting transfers between devices: 0.14 us -> 0.98 us  [shards(): other_a = lax.ppermute(own_b, 'term', swap)]
    concatenate x0 -> x1, other arithmetic: none -> 0.73 us  [shards(): pos = jnp.concatenate([kept_rows, op_own, op_other])]
    pallas_call x3, Pallas kernels: 7.68 us -> 6.95 us  [the longest x1 5.15 us: shards(): pl.pallas_call(centre_kernel, out_shape=(sigma_shape, rim_shape, kept_sha...]
    ppermute x1, waiting for transfers between devices: 0.73 us -> 0.01 us  [shards(): other_b = lax.ppermute(own_a, 'term', swap)]
  transfers between devices with their start and end apart: 7 -> 9, of which waited for: 3 -> 2; matrix products, arithmetic and copies ran while one was open for 5% -> 4% of each run, Pallas kernels for 29% -> 29%
where the time goes in v2:
time: 19.5 us; the launch traced here: 19.3 us
  starting transfers between devices  7.86 us (40%)
  Pallas kernels  6.95 us (36%)
  local copies, waits for them, and re-layouts  1.9 us (10%)
  waiting for transfers between devices  1.18 us (6%)
  other arithmetic  0.73 us (4%)
  between operations  0.71 us (4%)
    pallas_call x1, Pallas kernels, shards(): pl.pallas_call(centre_kernel, out_shape=(sigma_shape, rim_shape, kept_sha...  5.15 us
    ppermute x1, starting transfers between devices, shards(): note_a = lax.ppermute(note_of(kept_rows, size), ('sector', 'term'), cycle)  2.92 us
    ppermute x1, starting transfers between devices, shards(): own_a = lax.ppermute(right_env, ('sector', 'term'), cycle)  2.49 us
    unnamed x4, local copies, waits for them, and re-layouts  1.9 us
    pallas_call x1, Pallas kernels, shards(): pl.pallas_call(last_rim_kernel, out_shape=sigma_shape, in_specs=[VMEM] *...  1.34 us
    ppermute x1, starting transfers between devices, shards(): other_a = lax.ppermute(own_b, 'term', swap)  0.98 us
    concatenate x1, other arithmetic, shards(): pos = jnp.concatenate([kept_rows, op_own, op_other])  0.73 us
    ppermute x1, waiting for transfers between devices, shards(): op_other = lax.ppermute(op_index, 'term', swap)  0.6 us
  transfers between devices with their start and end apart: 9, of which 2 were waited for; matrix products, arithmetic and copies ran while one was open for 4% of the time, Pallas kernels for 29%

profile of v2, /device:TPU:0, one launch (start us, length us, event | category | flops | bytes accessed | tf_op | source)
XLA Modules:
  0.0 19.3 jit_solution(201447961198463250)
XLA Ops:
  0.0 0.5 %collective-permute-start.1 = (bf16[2,1,256,256]{3,2,1,0:T(8,128)(2,1)}, bf16[2,1,256,256]{3,2,1,0:T(8,128)(2,1)S(1)}, u32[]{:S(2)}, u32[]{:S(2)}) collective-permute-start(bf16[2,1,256,256]{3,2,1,0:T(8,128)(2,1)} %left_own.1), channel_id=1, source_target_pairs={{0,1},{1,0},{2,3},{3,2},{4,5},{5,4},{6,7},{7,6},{8,9},{9,8},{10,11... | collective-permute-start | bytes 786440 | tf_op jit(solution)/shard_map/ppermute | solution.py:170
  0.5 0.1 collective-permute-start.2
  0.5 0.5 %collective-permute-start.4 = (bf16[2,1,256,256]{3,2,1,0:T(8,128)(2,1)}, bf16[2,1,256,256]{3,2,1,0:T(8,128)(2,1)S(1)}, u32[]{:S(2)}, u32[]{:S(2)}) collective-permute-start(bf16[2,1,256,256]{3,2,1,0:T(8,128)(2,1)} %right_own.1), channel_id=1, source_target_pairs={{2,0},{4,2},{6,4},{8,6},{10,8},{12,10},{14,12},{16,14},{18,16},{20... | collective-permute-start | bytes 786440 | tf_op jit(solution)/shard_map/ppermute | solution.py:167
  1.0 2.5 %collective-permute-start.3 = (bf16[2,1,256,256]{3,2,1,0:T(8,128)(2,1)}, bf16[2,1,256,256]{3,2,1,0:T(8,128)(2,1)S(1)}, u32[]{:S(2)}, u32[]{:S(2)}) collective-permute-start(bf16[2,1,256,256]{3,2,1,0:T(8,128)(2,1)} %right_own.1), channel_id=1, source_target_pairs={{0,2},{2,4},{4,6},{6,8},{8,10},{10,12},{12,14},{14,16},{16,18},{18... | collective-permute-start | bytes 786440 | tf_op jit(solution)/shard_map/ppermute | solution.py:166
  3.5 0.0 collective-permute-start
  4.1 0.6 %collective-permute-done = s32[2]{0:T(128)S(1)} collective-permute-done((s32[2]{0:T(128)}, s32[2]{0:T(128)S(1)}, u32[]{:S(2)}, u32[]{:S(2)}) %collective-permute-start) | collective-permute-done | bytes 40 | tf_op jit(solution)/shard_map/ppermute | solution.py:172
  4.7 2.9 %collective-permute-start.5 = (f32[8,256]{1,0:T(8,128)S(1)}, f32[8,256]{1,0:T(8,128)S(1)}, u32[]{:S(2)}, u32[]{:S(2)}) collective-permute-start(f32[8,256]{1,0:T(8,128)S(1)} %broadcast_in_dim.9), channel_id=1, source_target_pairs={{0,2},{2,4},{4,6},{6,8},{8,10},{10,12},{12,14},{14,16},{16,18},{18... | collective-permute-start | bytes 24584 | tf_op jit(solution)/shard_map/ppermute | solution.py:168
  7.6 0.7 %pad_add_fusion.pos = s32[5]{0:T(128)S(1)} fusion(s32[2]{0:T(128)S(1)} %collective-permute-done, s32[2]{0:T(128)} %param.8, s32[1]{0:T(128)S(6)} %copy.8), kind=kLoop, calls=%fused_computation | loop fusion | flops 10 | bytes 40 | tf_op jit(solution)/shard_map/concatenate | solution.py:189
  8.4 0.0 collective-permute-done.1.left_other
  8.4 0.0 collective-permute-done.2.right_other
  8.4 0.0 copy-start
  8.4 0.9 %copy-done = bf16[2,1,256,256]{3,2,1,0:T(8,128)(2,1)S(1)} copy-done((bf16[2,1,256,256]{3,2,1,0:T(8,128)(2,1)S(1)}, bf16[2,1,256,256]{3,2,1,0:T(8,128)(2,1)}, u32[]{:S(2)}) %copy-start) | copy-done | bytes 262168
  9.3 0.0 copy-start.1
  9.3 0.9 %copy-done.1 = bf16[2,1,256,256]{3,2,1,0:T(8,128)(2,1)S(1)} copy-done((bf16[2,1,256,256]{3,2,1,0:T(8,128)(2,1)S(1)}, bf16[2,1,256,256]{3,2,1,0:T(8,128)(2,1)}, u32[]{:S(2)}) %copy-start.1) | copy-done | bytes 262168
  10.3 5.1 %centre.1 = (f32[4,1,4,128,256]{4,3,2,1,0:T(8,128)}, bf16[2,4,512,256]{3,2,1,0:T(8,128)(2,1)S(1)}, f32[8,256]{1,0:T(8,128)S(1)}) custom-call(s32[5]{0:T(128)S(1)} %pad_add_fusion.pos, bf16[4,1,4,256,256]{4,3,2,1,0:T(8,128)(2,1)} %psi.1, bf16[2,1,256,256]{3,2,1,0:T(8,128)(2,1)S(1)} %copy-done, bf16[2,1,256,256]{3,2,1,0:T(8,128)(2,1)S(1)} %collective-permute-done.1.left_other, ...), custom_call_target="tpu_custom_call" | custom-call | tf_op jit(solution)/shard_map/centre/pallas_call | solution.py:197
  15.4 0.0 collective-permute-done.5.note_a
  15.4 0.0 collective-permute-done.4
  15.5 0.0 collective-permute-done.3
  15.5 1.0 %collective-permute-start.7 = (bf16[2,1,256,256]{3,2,1,0:T(8,128)(2,1)S(1)}, bf16[2,1,256,256]{3,2,1,0:T(8,128)(2,1)S(1)}, u32[]{:S(2)}, u32[]{:S(2)}) collective-permute-start(bf16[2,1,256,256]{3,2,1,0:T(8,128)(2,1)S(1)} %collective-permute-done.4), channel_id=1, source_target_pairs={{0,1},{1,0},{2,3},{3,2},{4,5},{5,4},{6,7},{7,6},{8,9},{9,8},{10,11... | collective-permute-start | bytes 786440 | tf_op jit(solution)/shard_map/ppermute | solution.py:220
  16.4 0.1 collective-permute-start.8
  16.5 0.4 %collective-permute-start.6 = (f32[8,256]{1,0:T(8,128)S(1)}, f32[8,256]{1,0:T(8,128)S(1)}, u32[]{:S(2)}, u32[]{:S(2)}) collective-permute-start(f32[8,256]{1,0:T(8,128)S(1)} %collective-permute-done.5.note_a), channel_id=1, source_target_pairs={{0,1},{1,0},{2,3},{3,2},{4,5},{5,4},{6,7},{7,6},{8,9},{9,8},{10,11... | collective-permute-start | bytes 24584 | tf_op jit(solution)/shard_map/ppermute | solution.py:221
  17.0 0.5 %own_rim.1 = (f32[512,256]{1,0:T(8,128)S(1)}, f32[512,256]{1,0:T(8,128)S(1)}) custom-call(bf16[2,4,512,256]{3,2,1,0:T(8,128)(2,1)S(1)} %get-tuple-element.19.rim, bf16[512,256]{1,0:T(8,128)(2,1)S(1)} %bitcast.6, bf16[512,256]{1,0:T(8,128)(2,1)S(1)} %bitcast.5), custom_call_target="tpu_custom_call" | custom-call | tf_op jit(solution)/shard_map/own_rim/pallas_call | solution.py:225
  17.4 0.6 %collective-permute-done.6.note_b = f32[8,256]{1,0:T(8,128)S(1)} collective-permute-done((f32[8,256]{1,0:T(8,128)S(1)}, f32[8,256]{1,0:T(8,128)S(1)}, u32[]{:S(2)}, u32[]{:S(2)}) %collective-permute-start.6) | collective-permute-done | bytes 8224 | tf_op jit(solution)/shard_map/ppermute | solution.py:221
  18.0 0.0 collective-permute-done.7
  18.0 0.0 collective-permute-done.8
  18.0 1.3 %last_rim.1 = f32[4,1,4,128,256]{4,3,2,1,0:T(8,128)} custom-call(f32[8,256]{1,0:T(8,128)S(1)} %get-tuple-element.15.kept_row, f32[8,256]{1,0:T(8,128)S(1)} %collective-permute-done.5.note_a, f32[8,256]{1,0:T(8,128)S(1)} %collective-permute-done.6.note_b, bf16[2,4,512,256]{3,2,1,0:T(8,128)(2,1)S(1)} %get-tuple-element.19.rim, ...), custom_call_target="tpu_custom_call", output_to_operand_aliasing={{}: (8, {})} | custom-call | tf_op jit(solution)/shard_map/last_rim/pallas_call | solution.py:233
  (1 shorter events, 0.0 us)
Async XLA Ops:
  0.0 8.4 %collective-permute-start.1 = (bf16[2,1,256,256]{3,2,1,0:T(8,128)(2,1)}, bf16[2,1,256,256]{3,2,1,0:T(8,128)(2,1)S(1)}, u32[]{:S(2)}, u32[]{:S(2)}) collective-permute-start(bf16[2,1,256,256]{3,2,1,0:T(8,128)(2,1)} %left_own.1), channel_id=1, source_target_pairs={{0,1},{1,0},{2,3},{3,2},{4,5},{5,4},{6,7},{7,6},{8,9},{9,8},{10,11... | collective-permute-start | bytes 786440 | tf_op jit(solution)/shard_map/ppermute | solution.py:170
  0.5 7.9 %collective-permute-start.2 = (bf16[2,1,256,256]{3,2,1,0:T(8,128)(2,1)}, bf16[2,1,256,256]{3,2,1,0:T(8,128)(2,1)S(1)}, u32[]{:S(2)}, u32[]{:S(2)}) collective-permute-start(bf16[2,1,256,256]{3,2,1,0:T(8,128)(2,1)} %right_own.1), channel_id=1, source_target_pairs={{0,1},{1,0},{2,3},{3,2},{4,5},{5,4},{6,7},{7,6},{8,9},{9,8},{10,11... | collective-permute-start | bytes 786440 | tf_op jit(solution)/shard_map/ppermute | solution.py:171
  0.5 14.9 %collective-permute-start.4 = (bf16[2,1,256,256]{3,2,1,0:T(8,128)(2,1)}, bf16[2,1,256,256]{3,2,1,0:T(8,128)(2,1)S(1)}, u32[]{:S(2)}, u32[]{:S(2)}) collective-permute-start(bf16[2,1,256,256]{3,2,1,0:T(8,128)(2,1)} %right_own.1), channel_id=1, source_target_pairs={{2,0},{4,2},{6,4},{8,6},{10,8},{12,10},{14,12},{16,14},{18,16},{20... | collective-permute-start | bytes 786440 | tf_op jit(solution)/shard_map/ppermute | solution.py:167
  1.0 14.5 %collective-permute-start.3 = (bf16[2,1,256,256]{3,2,1,0:T(8,128)(2,1)}, bf16[2,1,256,256]{3,2,1,0:T(8,128)(2,1)S(1)}, u32[]{:S(2)}, u32[]{:S(2)}) collective-permute-start(bf16[2,1,256,256]{3,2,1,0:T(8,128)(2,1)} %right_own.1), channel_id=1, source_target_pairs={{0,2},{2,4},{4,6},{6,8},{8,10},{10,12},{12,14},{14,16},{16,18},{18... | collective-permute-start | bytes 786440 | tf_op jit(solution)/shard_map/ppermute | solution.py:166
  3.5 1.3 %collective-permute-start = (s32[2]{0:T(128)}, s32[2]{0:T(128)S(1)}, u32[]{:S(2)}, u32[]{:S(2)}) collective-permute-start(s32[2]{0:T(128)} %param.8), channel_id=1, source_target_pairs={{0,1},{1,0},{2,3},{3,2},{4,5},{5,4},{6,7},{7,6},{8,9},{9,8},{10,11... | collective-permute-start | bytes 32 | tf_op jit(solution)/shard_map/ppermute | solution.py:172
  4.7 10.7 %collective-permute-start.5 = (f32[8,256]{1,0:T(8,128)S(1)}, f32[8,256]{1,0:T(8,128)S(1)}, u32[]{:S(2)}, u32[]{:S(2)}) collective-permute-start(f32[8,256]{1,0:T(8,128)S(1)} %broadcast_in_dim.9), channel_id=1, source_target_pairs={{0,2},{2,4},{4,6},{6,8},{8,10},{10,12},{12,14},{14,16},{16,18},{18... | collective-permute-start | bytes 24584 | tf_op jit(solution)/shard_map/ppermute | solution.py:168
  8.4 1.0 %copy-start = (bf16[2,1,256,256]{3,2,1,0:T(8,128)(2,1)S(1)}, bf16[2,1,256,256]{3,2,1,0:T(8,128)(2,1)}, u32[]{:S(2)}) copy-start(bf16[2,1,256,256]{3,2,1,0:T(8,128)(2,1)} %left_own.1) | copy-start | bytes 786436
  9.3 0.9 %copy-start.1 = (bf16[2,1,256,256]{3,2,1,0:T(8,128)(2,1)S(1)}, bf16[2,1,256,256]{3,2,1,0:T(8,128)(2,1)}, u32[]{:S(2)}) copy-start(bf16[2,1,256,256]{3,2,1,0:T(8,128)(2,1)} %right_own.1) | copy-start | bytes 786436
  15.5 2.5 %collective-permute-start.7 = (bf16[2,1,256,256]{3,2,1,0:T(8,128)(2,1)S(1)}, bf16[2,1,256,256]{3,2,1,0:T(8,128)(2,1)S(1)}, u32[]{:S(2)}, u32[]{:S(2)}) collective-permute-start(bf16[2,1,256,256]{3,2,1,0:T(8,128)(2,1)S(1)} %collective-permute-done.4), channel_id=1, source_target_pairs={{0,1},{1,0},{2,3},{3,2},{4,5},{5,4},{6,7},{7,6},{8,9},{9,8},{10,11... | collective-permute-start | bytes 786440 | tf_op jit(solution)/shard_map/ppermute | solution.py:220
  16.4 1.6 %collective-permute-start.8 = (bf16[2,1,256,256]{3,2,1,0:T(8,128)(2,1)S(1)}, bf16[2,1,256,256]{3,2,1,0:T(8,128)(2,1)S(1)}, u32[]{:S(2)}, u32[]{:S(2)}) collective-permute-start(bf16[2,1,256,256]{3,2,1,0:T(8,128)(2,1)S(1)} %collective-permute-done.3), channel_id=1, source_target_pairs={{0,1},{1,0},{2,3},{3,2},{4,5},{5,4},{6,7},{7,6},{8,9},{9,8},{10,11... | collective-permute-start | bytes 786440 | tf_op jit(solution)/shard_map/ppermute | solution.py:219
  16.5 1.5 %collective-permute-start.6 = (f32[8,256]{1,0:T(8,128)S(1)}, f32[8,256]{1,0:T(8,128)S(1)}, u32[]{:S(2)}, u32[]{:S(2)}) collective-permute-start(f32[8,256]{1,0:T(8,128)S(1)} %collective-permute-done.5.note_a), channel_id=1, source_target_pairs={{0,1},{1,0},{2,3},{3,2},{4,5},{5,4},{6,7},{7,6},{8,9},{9,8},{10,11... | collective-permute-start | bytes 24584 | tf_op jit(solution)/shard_map/ppermute | solution.py:221

commit v3 on v2

v3 whole, which is shorter than its diff:
```python
import jax
import jax.numpy as jnp
from jax import lax
from jax.experimental import pallas as pl
from jax.experimental.pallas import tpu as pltpu
from jax.sharding import PartitionSpec as P

FLIP = 2
COEFFICIENTS = (
    (1.0, 1.0, 1.0, 1.0),
    (0.25, -0.25, -0.25, 0.25),
    (0.0, 0.5, 0.5, 0.0),
    (0.5, 0.5, -0.5, -0.5),
    (0.5, -0.5, 0.5, -0.5),
)
VMEM_LIMIT = 16 * 1024 * 1024
CENTRE_LIMIT = 50 * 1024 * 1024
PACK_LIMIT = 54579 * 1024
VMEM = pl.BlockSpec(memory_space=pltpu.VMEM)
HBM = pl.BlockSpec(memory_space=pltpu.HBM)


def coefficient(op, p):
    value = jnp.full_like(op, COEFFICIENTS[-1][p])
    for kind in range(len(COEFFICIENTS) - 1):
        value = jnp.where(op == kind, COEFFICIENTS[kind][p], value)
    return value


def times_transpose(a, b):
    return lax.dot_general(a, b, (((1,), (1,)), ((), ())), preferred_element_type=jnp.float32)


def below_is_a():
    return lax.axis_index("term") == 0 if lax.axis_size("term") == 2 else True


def info_rows(terms):
    return 8 * pl.cdiv(1 + terms, 8)


def info_of(kept, ops, terms, size):
    rows = lax.broadcasted_iota(jnp.int32, (info_rows(terms), size), 0)
    info = jnp.where(rows == 0, kept[0], 0)
    for t in range(terms):
        info = jnp.where(rows == 1 + t, ops[t], info)
    return info.astype(jnp.float32)


def pack_kernel(kept, ops, left, right, info, mine, theirs, *refs):
    *blocks, kept_buf, ops_buf, sems = refs
    terms, half, size = mine.shape
    core = lax.axis_index("term")
    scalars = [
        pltpu.make_async_copy(kept, kept_buf, sems.at[0]),
        pltpu.make_async_copy(ops, ops_buf, sems.at[1]),
    ]
    copies = [
        pltpu.make_async_copy(
            left.at[:, 0, pl.ds(pl.multiple_of(who * half, half), half)], rows, sems.at[2 + k]
        )
        for k, (who, rows) in enumerate(((core, mine), (1 - core, theirs)))
    ]
    for t, block in enumerate(blocks):
        copies.append(pltpu.make_async_copy(right.at[t, 0], block, sems.at[4 + t]))
    for copy in scalars + copies:
        copy.start()
    for copy in scalars:
        copy.wait()
    info[...] = info_of(kept_buf, ops_buf, terms, size)
    for copy in copies:
        copy.wait()


def pack(kept, ops, left, right, half):
    terms, size = left.shape[0], left.shape[-1]
    rows = jax.ShapeDtypeStruct((terms, half, size), left.dtype)
    block = jax.ShapeDtypeStruct((size, size), right.dtype)
    info, mine, theirs, *blocks = pl.pallas_call(
        pack_kernel,
        out_shape=(jax.ShapeDtypeStruct((info_rows(terms), size), jnp.float32), rows, rows)
        + (block,) * terms,
        in_specs=[HBM] * 4,
        out_specs=(VMEM,) * (3 + terms),
        scratch_shapes=[
            pltpu.SMEM(kept.shape, kept.dtype),
            pltpu.SMEM(ops.shape, ops.dtype),
            pltpu.SemaphoreType.DMA((4 + terms,)),
        ],
        compiler_params=pltpu.CompilerParams(vmem_limit_bytes=PACK_LIMIT),
        name="pack",
    )(kept, ops, left, right)
    return info, mine, theirs, blocks


def centre_kernel(psi, info_own, info_other, left_own, left_other, *refs):
    (*rights, sigma, rim, psi_buf, lefts, centre, out_buf, psi_sem, out_sem) = refs
    nvec, half, size = psi.shape[0], sigma.shape[3], psi.shape[4]
    own, terms = left_own.shape[0], len(rights)
    loads = [pltpu.make_async_copy(psi.at[v, 0], psi_buf.at[v], psi_sem.at[v]) for v in range(nvec)]
    for copy in loads:
        copy.start()
    for t in range(terms):
        source, k = (left_own, t) if t < own else (left_other, t - own)
        lefts[pl.ds(t * half, half), :] = source[k]
    slot_of_3 = jnp.where(below_is_a(), 0, 1)
    ops = [info_own[1 + t:2 + t] if t < own else info_other[1 + t - own:2 + t - own]
           for t in range(terms)]
    factors = [[coefficient(op, p) for p in range(4)] for op in ops]
    flips = [op == FLIP for op in ops]
    rows = lax.broadcasted_iota(jnp.int32, (half, size), 0) + lax.axis_index("term") * half
    cols = lax.broadcasted_iota(jnp.int32, (half, size), 1)
    keep = jnp.maximum(rows, cols).astype(jnp.float32) < info_own[0:1]
    groups = out_sem.shape[1]
    per_group = nvec // groups
    stores = []
    for group in range(groups):
        for j in range(per_group):
            v = group * per_group + j
            loads[v].wait()
            lifted = [
                jnp.dot(lefts[...], psi_buf[v, q], preferred_element_type=jnp.float32)
                for q in range(4)
            ]
            for t in range(terms):
                part = [x[t * half:(t + 1) * half] for x in lifted]
                factor = factors[t]
                for q in (0, 3):
                    slot = slot_of_3 if q == 3 else 1 - slot_of_3
                    rim[slot, t, pl.ds(v * half, half), :] = (part[q] * factor[q]).astype(rim.dtype)
                for p in (1, 2):
                    source = jnp.where(flips[t], part[3 - p], part[p])
                    centre[p - 1, t, pl.ds(j * half, half), :] = (source * factor[p]).astype(
                        centre.dtype
                    )
        for slot in range(2):
            total = None
            for t in range(terms):
                part = times_transpose(centre[slot, t], rights[t][...])
                total = part if total is None else total + part
            for j in range(per_group):
                out_buf[slot, group * per_group + j] = jnp.where(
                    keep, total[j * half:(j + 1) * half], 0.0
                )
            vectors = pl.ds(group * per_group, per_group)
            store = pltpu.make_async_copy(
                out_buf.at[slot, vectors], sigma.at[vectors, 0, slot + 1], out_sem.at[slot, group]
            )
            store.start()
            stores.append(store)
    for store in stores:
        store.wait()


def sum_terms(rim, which, first, blocks, count, rows, total=None):
    size = rim.shape[-1]
    for k in range(count):
        product = times_transpose(rim[which, first + k, rows, :], blocks[k * size:(k + 1) * size])
        total = product if total is None else total + product
    return total


def state_mask(which, info, note, half):
    is_below = (which == 0) == below_is_a()
    me = lax.axis_index("sector")
    there = jnp.where(is_below, me, lax.axis_size("sector") - 1 - me) > 0
    shape = (half, info.shape[1])
    rows = lax.broadcasted_iota(jnp.int32, shape, 0) + lax.axis_index("term") * half
    cols = lax.broadcasted_iota(jnp.int32, shape, 1)
    keep = (rows.astype(jnp.float32) < info[0:1, :]) & there
    return keep & (cols.astype(jnp.float32) < note[0:1, :]), jnp.where(is_below, 3, 0)


def own_rim_kernel(rim, own_a, own_b, part_a, part_b):
    count, rows = own_a.shape[0] // rim.shape[-1], pl.ds(0, rim.shape[2])
    part_a[...] = sum_terms(rim, 0, 0, own_a, count, rows)
    part_b[...] = sum_terms(rim, 1, 0, own_b, count, rows)


def last_rim_kernel(info, note_a, note_b, rim, other_a, other_b, part_a, part_b, sigma_in, sigma,
                    out_buf, out_sem):
    _, nvec, half, size = out_buf.shape
    count, groups = other_a.shape[0] // size, out_sem.shape[1]
    first, per_group = rim.shape[1] - count, nvec // groups
    stores = []
    for which, note, blocks, part in ((0, note_a, other_a, part_a), (1, note_b, other_b, part_b)):
        keep, state = state_mask(which, info, note, half)
        for group in range(groups):
            rows = pl.ds(group * per_group * half, per_group * half)
            total = sum_terms(rim, which, first, blocks, count, rows, part[rows, :])
            for j in range(per_group):
                out_buf[which, group * per_group + j] = jnp.where(
                    keep, total[j * half:(j + 1) * half], 0.0
                )
            vectors = pl.ds(group * per_group, per_group)
            store = pltpu.make_async_copy(
                out_buf.at[which, vectors], sigma.at[vectors, 0, state], out_sem.at[which, group]
            )
            store.start()
            stores.append(store)
    for store in stores:
        store.wait()


def two_core_cycle(sectors):
    up = [(2 * i, 2 * i + 2) for i in range(sectors - 1)]
    down = [(2 * i + 3, 2 * i + 1) for i in range(sectors - 1)]
    return up + [(2 * sectors - 2, 2 * sectors - 1)] + down + [(1, 0)]


def shards(psi, left_env, right_env, op_index, kept_rows):
    sectors, cores = lax.axis_size("sector"), lax.axis_size("term")
    nvec, size = psi.shape[0], psi.shape[-1]
    half = size // cores
    terms = left_env.shape[0] * cores
    swap = [(0, 1), (1, 0)]

    if cores == 2:
        cycle = two_core_cycle(sectors)
        reverse = [(b, a) for a, b in cycle]
        own_a = lax.ppermute(right_env, ("sector", "term"), cycle)
        own_b = lax.ppermute(right_env, ("sector", "term"), reverse)
        info_own, left_own, left_sent, rights = pack(
            kept_rows, op_index, left_env, right_env, half
        )
        left_other = lax.ppermute(left_sent, "term", swap)
        info_other = lax.ppermute(info_own, "term", swap)
        rights += [lax.ppermute(x, "term", swap) for x in rights]
        note_a = lax.ppermute(info_own, ("sector", "term"), cycle)
    else:
        forward = [(i, i + 1) for i in range(sectors - 1)]
        backward = [(b, a) for a, b in forward]
        gathered = [lax.all_gather(x, "term", tiled=True) for x in (left_env, right_env, op_index)]
        rows = lax.dynamic_slice_in_dim(gathered[0][:, 0], lax.axis_index("term") * half, half, 1)
        left_own, left_other = jnp.split(rows, 2)
        info_own, info_other = [
            info_of(kept_rows, ops, terms // 2, size) for ops in jnp.split(gathered[2], 2)
        ]
        rights = list(gathered[1][:, 0])

        def neighbour(pairs):
            blocks = lax.all_gather(lax.ppermute(right_env, "sector", pairs), "term", tiled=True)
            return *jnp.split(blocks, 2), lax.ppermute(info_own, "sector", pairs)

        own_a, other_a, note_a = neighbour(forward)
        own_b, other_b, note_b = neighbour(backward)

    sigma_shape = jax.ShapeDtypeStruct((nvec, 1, 4, half, size), jnp.float32)
    rim_shape = jax.ShapeDtypeStruct((2, terms, nvec * half, size), jnp.bfloat16)
    part_shape = jax.ShapeDtypeStruct((nvec * half, size), jnp.float32)
    params = pltpu.CompilerParams(vmem_limit_bytes=VMEM_LIMIT)

    groups = 2 if nvec % 2 == 0 else 1
    sigma, rim = pl.pallas_call(
        centre_kernel,
        out_shape=(sigma_shape, rim_shape),
        in_specs=[HBM] + [VMEM] * (4 + terms),
        out_specs=(HBM, VMEM),
        scratch_shapes=[
            pltpu.VMEM((nvec, 4, size, size), jnp.bfloat16),
            pltpu.VMEM((terms * half, size), jnp.bfloat16),
            pltpu.VMEM((2, terms, nvec // groups * half, size), jnp.bfloat16),
            pltpu.VMEM((2, nvec, half, size), jnp.float32),
            pltpu.SemaphoreType.DMA((nvec,)),
            pltpu.SemaphoreType.DMA((2, groups)),
        ],
        compiler_params=pltpu.CompilerParams(vmem_limit_bytes=CENTRE_LIMIT),
        name="centre",
    )(psi, info_own, info_other, left_own, left_other, *rights)

    own_a, own_b, note_a, sigma, rim = lax.optimization_barrier((own_a, own_b, note_a, sigma, rim))
    if cores == 2:
        other_b = lax.ppermute(own_a, "term", swap)
        other_a = lax.ppermute(own_b, "term", swap)
        note_b = lax.ppermute(note_a, "term", swap)
    own_a, own_b, other_a, other_b = [
        x.reshape(-1, size) for x in (own_a, own_b, other_a, other_b)
    ]
    part_a, part_b = pl.pallas_call(
        own_rim_kernel,
        out_shape=(part_shape, part_shape),
        in_specs=[VMEM] * 3,
        out_specs=(VMEM, VMEM),
        compiler_params=params,
        name="own_rim",
    )(rim, own_a, own_b)
    return pl.pallas_call(
        last_rim_kernel,
        out_shape=sigma_shape,
        in_specs=[VMEM] * 8 + [HBM],
        out_specs=HBM,
        scratch_shapes=[
            pltpu.VMEM((2, nvec, half, size), jnp.float32),
            pltpu.SemaphoreType.DMA((2, groups)),
        ],
        input_output_aliases={8: 0},
        compiler_params=params,
        name="last_rim",
    )(info_own, note_a, note_b, rim, other_a, other_b, part_a, part_b, sigma)


def solution(mesh):
    in_specs = (
        P(None, "sector", None, None, None),
        P("term", "sector", None, None),
        P("term", "sector", None, None),
        P("term"),
        P("sector"),
    )
    out_specs = P(None, "sector", None, "term", None)
    return jax.shard_map(shards, mesh=mesh, in_specs=in_specs, out_specs=out_specs, check_vma=False)
```

time: 19.5 us -> 19 us (0.974)
  local copies, waits for them, and re-layouts: 1.9 us -> 0.65 us
  other arithmetic: 0.73 us -> 0 us
  starting transfers between devices: 7.86 us -> 8.58 us
  waiting for transfers between devices: 1.18 us -> 1.7 us
  Pallas kernels: 6.95 us -> 7.2 us
    unnamed x4 -> x2, local copies, waits for them, and re-layouts: 1.9 us -> 0.65 us
    concatenate x1 -> x0, other arithmetic: 0.73 us -> none  [shards(): pos = jnp.concatenate([kept_rows, op_own, op_other])]
    ppermute x4 -> x5, waiting for transfers between devices: 0.61 us -> 1.12 us  [the longest x1 0.58 us: shards(): info_other = lax.ppermute(info_own, 'term', swap)]
    ppermute x1, starting transfers between devices: 0.98 us -> 1.4 us  [shards(): other_a = lax.ppermute(own_b, 'term', swap)]
    ppermute x4 -> x5, starting transfers between devices: 3.43 us -> 3.73 us  [the longest x1 2.92 us: shards(): note_a = lax.ppermute(info_own, ('sector', 'term'), cycle)]
    pallas_call x1 -> x2, Pallas kernels: 5.15 us -> 5.39 us  [the longest x1 4.25 us: shards(): pl.pallas_call(centre_kernel, out_shape=(sigma_shape, rim_shape), in_spec...]
  transfers between devices with their start and end apart: 9 -> 10, of which waited for: 2 -> 4; matrix products, arithmetic and copies ran while one was open for 4% -> 0% of each run, Pallas kernels for 29% -> 31%
where the time goes in v3:
time: 19 us; the launch traced here: 18.8 us
  starting transfers between devices  8.58 us (45%)
  Pallas kernels  7.2 us (38%)
  waiting for transfers between devices  1.7 us (9%)
  between operations  0.7 us (4%)
  local copies, waits for them, and re-layouts  0.65 us (3%)
    pallas_call x1, Pallas kernels, shards(): pl.pallas_call(centre_kernel, out_shape=(sigma_shape, rim_shape), in_spec...  4.25 us
    ppermute x1, starting transfers between devices, shards(): note_a = lax.ppermute(info_own, ('sector', 'term'), cycle)  2.92 us
    ppermute x1, starting transfers between devices, shards(): own_a = lax.ppermute(right_env, ('sector', 'term'), cycle)  2.49 us
    ppermute x1, starting transfers between devices, shards(): other_a = lax.ppermute(own_b, 'term', swap)  1.4 us
    pallas_call x1, Pallas kernels, shards(): pl.pallas_call(last_rim_kernel, out_shape=sigma_shape, in_specs=[VMEM] *...  1.34 us
    pallas_call x1, Pallas kernels, pack(): pl.pallas_call(pack_kernel, out_shape=(jax.ShapeDtypeStruct((info_rows(te...  1.15 us
    unnamed x2, local copies, waits for them, and re-layouts  0.65 us
    ppermute x1, waiting for transfers between devices, shards(): info_other = lax.ppermute(info_own, 'term', swap)  0.58 us
  transfers between devices with their start and end apart: 10, of which 4 were waited for; matrix products, arithmetic and copies ran while one was open for 0% of the time, Pallas kernels for 31%

profile of v3, /device:TPU:0, one launch (start us, length us, event | category | flops | bytes accessed | tf_op | source)
XLA Modules:
  0.0 18.8 jit_solution(8750962796308645241)
XLA Ops:
  0.0 0.5 %collective-permute-start.1 = (bf16[2,1,256,256]{3,2,1,0:T(8,128)(2,1)}, bf16[2,1,256,256]{3,2,1,0:T(8,128)(2,1)S(1)}, u32[]{:S(2)}, u32[]{:S(2)}) collective-permute-start(bf16[2,1,256,256]{3,2,1,0:T(8,128)(2,1)} %right.1), channel_id=1, source_target_pairs={{2,0},{4,2},{6,4},{8,6},{10,8},{12,10},{14,12},{16,14},{18,16},{20... | collective-permute-start | bytes 786440 | tf_op jit(solution)/shard_map/ppermute | solution.py:222
  0.5 2.5 %collective-permute-start = (bf16[2,1,256,256]{3,2,1,0:T(8,128)(2,1)}, bf16[2,1,256,256]{3,2,1,0:T(8,128)(2,1)S(1)}, u32[]{:S(2)}, u32[]{:S(2)}) collective-permute-start(bf16[2,1,256,256]{3,2,1,0:T(8,128)(2,1)} %right.1), channel_id=1, source_target_pairs={{0,2},{2,4},{4,6},{6,8},{8,10},{10,12},{12,14},{14,16},{16,18},{18... | collective-permute-start | bytes 786440 | tf_op jit(solution)/shard_map/ppermute | solution.py:221
  3.6 0.0 copy-start
  3.6 0.6 %copy-done = s32[2]{0:T(128)S(1)} copy-done((s32[2]{0:T(128)S(1)}, s32[2]{0:T(128)}, u32[]{:S(2)}) %copy-start) | copy-done | bytes 32
  4.3 1.1 %pack.1 = (f32[8,256]{1,0:T(8,128)S(1)}, bf16[2,128,256]{2,1,0:T(8,128)(2,1)S(1)}, bf16[2,128,256]{2,1,0:T(8,128)(2,1)S(1)}, bf16[256,256]{1,0:T(8,128)(2,1)S(1)}, bf16[256,256]{1,0:T(8,128)(2,1)S(1)}) custom-call(s32[1]{0:T(128)S(6)} %copy.8.kept, s32[2]{0:T(128)S(1)} %copy-done, bf16[2,1,256,256]{3,2,1,0:T(8,128)(2,1)} %left.1, bf16[2,1,256,256]{3,2,1,0:T(8,128)(2,1)} %right.1), custom_call_target="tpu_custom_call" | custom-call | tf_op jit(solution)/shard_map/pack/pallas_call | solution.py:79
  5.4 0.1 collective-permute-start.3
  5.5 0.5 %collective-permute-start.4 = (bf16[2,128,256]{2,1,0:T(8,128)(2,1)S(1)}, bf16[2,128,256]{2,1,0:T(8,128)(2,1)S(1)}, u32[]{:S(2)}, u32[]{:S(2)}) collective-permute-start(bf16[2,128,256]{2,1,0:T(8,128)(2,1)S(1)} %get-tuple-element.21), channel_id=1, source_target_pairs={{0,1},{1,0},{2,3},{3,2},{4,5},{5,4},{6,7},{7,6},{8,9},{9,8},{10,11... | collective-permute-start | bytes 393224 | tf_op jit(solution)/shard_map/ppermute | solution.py:226
  6.0 0.1 collective-permute-start.5
  6.1 0.6 %collective-permute-done.3.info_other = f32[8,256]{1,0:T(8,128)S(1)} collective-permute-done((f32[8,256]{1,0:T(8,128)S(1)}, f32[8,256]{1,0:T(8,128)S(1)}, u32[]{:S(2)}, u32[]{:S(2)}) %collective-permute-start.3) | collective-permute-done | bytes 8224 | tf_op jit(solution)/shard_map/ppermute | solution.py:227
  6.6 0.2 collective-permute-start.6
  6.8 0.2 collective-permute-done.4.left_other
  7.0 2.9 %collective-permute-start.2 = (f32[8,256]{1,0:T(8,128)S(1)}, f32[8,256]{1,0:T(8,128)S(1)}, u32[]{:S(2)}, u32[]{:S(2)}) collective-permute-start(f32[8,256]{1,0:T(8,128)S(1)} %get-tuple-element.19.info_own.info), channel_id=1, source_target_pairs={{0,2},{2,4},{4,6},{6,8},{8,10},{10,12},{12,14},{14,16},{16,18},{18... | collective-permute-start | bytes 24584 | tf_op jit(solution)/shard_map/ppermute | solution.py:229
  9.9 0.0 collective-permute-done.5.refs_2_
  9.9 0.0 collective-permute-done.6.refs_3_
  9.9 4.2 %centre.1 = (f32[4,1,4,128,256]{4,3,2,1,0:T(8,128)}, bf16[2,4,512,256]{3,2,1,0:T(8,128)(2,1)S(1)}) custom-call(bf16[4,1,4,256,256]{4,3,2,1,0:T(8,128)(2,1)} %psi.1, f32[8,256]{1,0:T(8,128)S(1)} %get-tuple-element.19.info_own.info, f32[8,256]{1,0:T(8,128)S(1)} %collective-permute-done.3.info_other, bf16[2,128,256]{2,1,0:T(8,128)(2,1)S(1)} %get-tuple-element.20.left_own, ...), custom_call_target="tpu_custom_call" | custom-call | tf_op jit(solution)/shard_map/centre/pallas_call | solution.py:254
  14.2 0.4 %collective-permute-done.2.note_a = f32[8,256]{1,0:T(8,128)S(1)} collective-permute-done((f32[8,256]{1,0:T(8,128)S(1)}, f32[8,256]{1,0:T(8,128)S(1)}, u32[]{:S(2)}, u32[]{:S(2)}) %collective-permute-start.2) | collective-permute-done | bytes 8224 | tf_op jit(solution)/shard_map/ppermute | solution.py:229
  14.5 0.0 collective-permute-done.1
  14.5 0.0 collective-permute-done
  14.5 1.4 %collective-permute-start.8 = (bf16[2,1,256,256]{3,2,1,0:T(8,128)(2,1)S(1)}, bf16[2,1,256,256]{3,2,1,0:T(8,128)(2,1)S(1)}, u32[]{:S(2)}, u32[]{:S(2)}) collective-permute-start(bf16[2,1,256,256]{3,2,1,0:T(8,128)(2,1)S(1)} %collective-permute-done.1), channel_id=1, source_target_pairs={{0,1},{1,0},{2,3},{3,2},{4,5},{5,4},{6,7},{7,6},{8,9},{9,8},{10,11... | collective-permute-start | bytes 786440 | tf_op jit(solution)/shard_map/ppermute | solution.py:274
  15.9 0.1 collective-permute-start.9
  16.0 0.4 %collective-permute-start.7 = (f32[8,256]{1,0:T(8,128)S(1)}, f32[8,256]{1,0:T(8,128)S(1)}, u32[]{:S(2)}, u32[]{:S(2)}) collective-permute-start(f32[8,256]{1,0:T(8,128)S(1)} %collective-permute-done.2.note_a), channel_id=1, source_target_pairs={{0,1},{1,0},{2,3},{3,2},{4,5},{5,4},{6,7},{7,6},{8,9},{9,8},{10,11... | collective-permute-start | bytes 24584 | tf_op jit(solution)/shard_map/ppermute | solution.py:275
  16.4 0.5 %own_rim.1 = (f32[512,256]{1,0:T(8,128)S(1)}, f32[512,256]{1,0:T(8,128)S(1)}) custom-call(bf16[2,4,512,256]{3,2,1,0:T(8,128)(2,1)S(1)} %get-tuple-element.27.rim, bf16[512,256]{1,0:T(8,128)(2,1)S(1)} %bitcast.5, bf16[512,256]{1,0:T(8,128)(2,1)S(1)} %bitcast.4), custom_call_target="tpu_custom_call" | custom-call | tf_op jit(solution)/shard_map/own_rim/pallas_call | solution.py:279
  16.9 0.6 %collective-permute-done.7.note_b = f32[8,256]{1,0:T(8,128)S(1)} collective-permute-done((f32[8,256]{1,0:T(8,128)S(1)}, f32[8,256]{1,0:T(8,128)S(1)}, u32[]{:S(2)}, u32[]{:S(2)}) %collective-permute-start.7) | collective-permute-done | bytes 8224 | tf_op jit(solution)/shard_map/ppermute | solution.py:275
  17.5 0.0 collective-permute-done.8
  17.5 0.0 collective-permute-done.9
  17.5 1.3 %last_rim.1 = f32[4,1,4,128,256]{4,3,2,1,0:T(8,128)} custom-call(f32[8,256]{1,0:T(8,128)S(1)} %get-tuple-element.19.info_own.info, f32[8,256]{1,0:T(8,128)S(1)} %collective-permute-done.2.note_a, f32[8,256]{1,0:T(8,128)S(1)} %collective-permute-done.7.note_b, bf16[2,4,512,256]{3,2,1,0:T(8,128)(2,1)S(1)} %get-tuple-element.27.rim, ...), custom_call_target="tpu_custom_call", output_to_operand_aliasing={{}: (8, {})} | custom-call | tf_op jit(solution)/shard_map/last_rim/pallas_call | solution.py:287
Async XLA Ops:
  0.0 14.5 %collective-permute-start.1 = (bf16[2,1,256,256]{3,2,1,0:T(8,128)(2,1)}, bf16[2,1,256,256]{3,2,1,0:T(8,128)(2,1)S(1)}, u32[]{:S(2)}, u32[]{:S(2)}) collective-permute-start(bf16[2,1,256,256]{3,2,1,0:T(8,128)(2,1)} %right.1), channel_id=1, source_target_pairs={{2,0},{4,2},{6,4},{8,6},{10,8},{12,10},{14,12},{16,14},{18,16},{20... | collective-permute-start | bytes 786440 | tf_op jit(solution)/shard_map/ppermute | solution.py:222
  0.5 14.1 %collective-permute-start = (bf16[2,1,256,256]{3,2,1,0:T(8,128)(2,1)}, bf16[2,1,256,256]{3,2,1,0:T(8,128)(2,1)S(1)}, u32[]{:S(2)}, u32[]{:S(2)}) collective-permute-start(bf16[2,1,256,256]{3,2,1,0:T(8,128)(2,1)} %right.1), channel_id=1, source_target_pairs={{0,2},{2,4},{4,6},{6,8},{8,10},{10,12},{12,14},{14,16},{16,18},{18... | collective-permute-start | bytes 786440 | tf_op jit(solution)/shard_map/ppermute | solution.py:221
  3.6 0.7 %copy-start = (s32[2]{0:T(128)S(1)}, s32[2]{0:T(128)}, u32[]{:S(2)}) copy-start(s32[2]{0:T(128)} %ops.1) | copy-start | bytes 28
  5.4 1.2 %collective-permute-start.3 = (f32[8,256]{1,0:T(8,128)S(1)}, f32[8,256]{1,0:T(8,128)S(1)}, u32[]{:S(2)}, u32[]{:S(2)}) collective-permute-start(f32[8,256]{1,0:T(8,128)S(1)} %get-tuple-element.19.info_own.info), channel_id=1, source_target_pairs={{0,1},{1,0},{2,3},{3,2},{4,5},{5,4},{6,7},{7,6},{8,9},{9,8},{10,11... | collective-permute-start | bytes 24584 | tf_op jit(solution)/shard_map/ppermute | solution.py:227
  5.5 1.5 %collective-permute-start.4 = (bf16[2,128,256]{2,1,0:T(8,128)(2,1)S(1)}, bf16[2,128,256]{2,1,0:T(8,128)(2,1)S(1)}, u32[]{:S(2)}, u32[]{:S(2)}) collective-permute-start(bf16[2,128,256]{2,1,0:T(8,128)(2,1)S(1)} %get-tuple-element.21), channel_id=1, source_target_pairs={{0,1},{1,0},{2,3},{3,2},{4,5},{5,4},{6,7},{7,6},{8,9},{9,8},{10,11... | collective-permute-start | bytes 393224 | tf_op jit(solution)/shard_map/ppermute | solution.py:226
  6.0 3.9 %collective-permute-start.5 = (bf16[256,256]{1,0:T(8,128)(2,1)S(1)}, bf16[256,256]{1,0:T(8,128)(2,1)S(1)}, u32[]{:S(2)}, u32[]{:S(2)}) collective-permute-start(bf16[256,256]{1,0:T(8,128)(2,1)S(1)} %get-tuple-element.22.refs_0_), channel_id=1, source_target_pairs={{0,1},{1,0},{2,3},{3,2},{4,5},{5,4},{6,7},{7,6},{8,9},{9,8},{10,11... | collective-permute-start | bytes 393224 | tf_op jit(solution)/shard_map/ppermute | solution.py:228
  6.6 3.3 %collective-permute-start.6 = (bf16[256,256]{1,0:T(8,128)(2,1)S(1)}, bf16[256,256]{1,0:T(8,128)(2,1)S(1)}, u32[]{:S(2)}, u32[]{:S(2)}) collective-permute-start(bf16[256,256]{1,0:T(8,128)(2,1)S(1)} %get-tuple-element.23.refs_1_), channel_id=1, source_target_pairs={{0,1},{1,0},{2,3},{3,2},{4,5},{5,4},{6,7},{7,6},{8,9},{9,8},{10,11... | collective-permute-start | bytes 393224 | tf_op jit(solution)/shard_map/ppermute | solution.py:228
  7.0 7.6 %collective-permute-start.2 = (f32[8,256]{1,0:T(8,128)S(1)}, f32[8,256]{1,0:T(8,128)S(1)}, u32[]{:S(2)}, u32[]{:S(2)}) collective-permute-start(f32[8,256]{1,0:T(8,128)S(1)} %get-tuple-element.19.info_own.info), channel_id=1, source_target_pairs={{0,2},{2,4},{4,6},{6,8},{8,10},{10,12},{12,14},{14,16},{16,18},{18... | collective-permute-start | bytes 24584 | tf_op jit(solution)/shard_map/ppermute | solution.py:229
  14.5 3.0 %collective-permute-start.8 = (bf16[2,1,256,256]{3,2,1,0:T(8,128)(2,1)S(1)}, bf16[2,1,256,256]{3,2,1,0:T(8,128)(2,1)S(1)}, u32[]{:S(2)}, u32[]{:S(2)}) collective-permute-start(bf16[2,1,256,256]{3,2,1,0:T(8,128)(2,1)S(1)} %collective-permute-done.1), channel_id=1, source_target_pairs={{0,1},{1,0},{2,3},{3,2},{4,5},{5,4},{6,7},{7,6},{8,9},{9,8},{10,11... | collective-permute-start | bytes 786440 | tf_op jit(solution)/shard_map/ppermute | solution.py:274
  15.9 1.6 %collective-permute-start.9 = (bf16[2,1,256,256]{3,2,1,0:T(8,128)(2,1)S(1)}, bf16[2,1,256,256]{3,2,1,0:T(8,128)(2,1)S(1)}, u32[]{:S(2)}, u32[]{:S(2)}) collective-permute-start(bf16[2,1,256,256]{3,2,1,0:T(8,128)(2,1)S(1)} %collective-permute-done), channel_id=1, source_target_pairs={{0,1},{1,0},{2,3},{3,2},{4,5},{5,4},{6,7},{7,6},{8,9},{9,8},{10,11... | collective-permute-start | bytes 786440 | tf_op jit(solution)/shard_map/ppermute | solution.py:273
  16.0 1.5 %collective-permute-start.7 = (f32[8,256]{1,0:T(8,128)S(1)}, f32[8,256]{1,0:T(8,128)S(1)}, u32[]{:S(2)}, u32[]{:S(2)}) collective-permute-start(f32[8,256]{1,0:T(8,128)S(1)} %collective-permute-done.2.note_a), channel_id=1, source_target_pairs={{0,1},{1,0},{2,3},{3,2},{4,5},{5,4},{6,7},{7,6},{8,9},{9,8},{10,11... | collective-permute-start | bytes 24584 | tf_op jit(solution)/shard_map/ppermute | solution.py:275

commit v4 on v3

--- a/solution.py
+++ b/solution.py
@@ -32,7 +32,7 @@
 
 
 def below_is_a():
-    return lax.axis_index("term") == 0 if lax.axis_size("term") == 2 else True
+    return lax.axis_index("term") == 1 if lax.axis_size("term") == 2 else True
 
 
 def info_rows(terms):
@@ -218,15 +218,15 @@
     if cores == 2:
         cycle = two_core_cycle(sectors)
         reverse = [(b, a) for a, b in cycle]
-        own_a = lax.ppermute(right_env, ("sector", "term"), cycle)
-        own_b = lax.ppermute(right_env, ("sector", "term"), reverse)
+        own_a = lax.ppermute(right_env, ("sector", "term"), reverse)
+        own_b = lax.ppermute(right_env, ("sector", "term"), cycle)
         info_own, left_own, left_sent, rights = pack(
             kept_rows, op_index, left_env, right_env, half
         )
         left_other = lax.ppermute(left_sent, "term", swap)
         info_other = lax.ppermute(info_own, "term", swap)
         rights += [lax.ppermute(x, "term", swap) for x in rights]
-        note_a = lax.ppermute(info_own, ("sector", "term"), cycle)
+        note_a = lax.ppermute(info_own, ("sector", "term"), reverse)
     else:
         forward = [(i, i + 1) for i in range(sectors - 1)]
         backward = [(b, a) for a, b in forward]

time: 19 us -> 18.7 us (0.984)
  starting transfers between devices: 8.58 us -> 4.69 us
  waiting for transfers between devices: 1.7 us -> 5.28 us
    ppermute x3, waiting for transfers between devices: 0.38 us -> 3.01 us  [the longest x1 3 us: shards(): note_a = lax.ppermute(info_own, ('sector', 'term'), reverse)]
    ppermute x3, starting transfers between devices: 5.86 us -> 3.3 us  [the longest x1 2.94 us: shards(): own_b = lax.ppermute(right_env, ('sector', 'term'), cycle)]
    ppermute x1, starting transfers between devices: 1.4 us -> 0.01 us  [shards(): other_a = lax.ppermute(own_b, 'term', swap)]
    ppermute x2, waiting for transfers between devices: 0.01 us -> 0.66 us  [shards(): rights += [lax.ppermute(x, 'term', swap) for x in rights]]
    ppermute x1, starting transfers between devices: 0.07 us -> 0.5 us  [shards(): other_b = lax.ppermute(own_a, 'term', swap)]
    ppermute x1, starting transfers between devices: 0.44 us -> 0.07 us  [shards(): note_b = lax.ppermute(note_a, 'term', swap)]
    ppermute x1, waiting for transfers between devices: 0.57 us -> 0.87 us  [shards(): note_b = lax.ppermute(note_a, 'term', swap)]
  transfers between devices with their start and end apart: 10 -> 10, of which waited for: 4 -> 5; matrix products, arithmetic and copies ran while one was open for 0% -> 0% of each run, Pallas kernels for 31% -> 32%
where the time goes in v4:
time: 18.7 us; the launch traced here: 18.5 us
  Pallas kernels  7.2 us (39%)
  waiting for transfers between devices  5.28 us (28%)
  starting transfers between devices  4.69 us (25%)
  between operations  0.71 us (4%)
  local copies, waits for them, and re-layouts  0.65 us (3%)
    pallas_call x1, Pallas kernels, shards(): pl.pallas_call(centre_kernel, out_shape=(sigma_shape, rim_shape), in_spec...  4.24 us
    ppermute x1, waiting for transfers between devices, shards(): note_a = lax.ppermute(info_own, ('sector', 'term'), reverse)  3 us
    ppermute x1, starting transfers between devices, shards(): own_b = lax.ppermute(right_env, ('sector', 'term'), cycle)  2.94 us
    pallas_call x1, Pallas kernels, shards(): pl.pallas_call(last_rim_kernel, out_shape=sigma_shape, in_specs=[VMEM] *...  1.34 us
    pallas_call x1, Pallas kernels, pack(): pl.pallas_call(pack_kernel, out_shape=(jax.ShapeDtypeStruct((info_rows(te...  1.15 us
    ppermute x1, waiting for transfers between devices, shards(): note_b = lax.ppermute(note_a, 'term', swap)  0.87 us
    ppermute x2, waiting for transfers between devices, shards(): rights += [lax.ppermute(x, 'term', swap) for x in rights]  0.66 us
    unnamed x2, local copies, waits for them, and re-layouts  0.65 us
  transfers between devices with their start and end apart: 10, of which 5 were waited for; matrix products, arithmetic and copies ran while one was open for 0% of the time, Pallas kernels for 32%

profile of v4, /device:TPU:0, one launch (start us, length us, event | category | flops | bytes accessed | tf_op | source)
XLA Modules:
  0.0 18.5 jit_solution(14723801646345352723)
XLA Ops:
  0.0 2.9 %collective-permute-start.1 = (bf16[2,1,256,256]{3,2,1,0:T(8,128)(2,1)}, bf16[2,1,256,256]{3,2,1,0:T(8,128)(2,1)S(1)}, u32[]{:S(2)}, u32[]{:S(2)}) collective-permute-start(bf16[2,1,256,256]{3,2,1,0:T(8,128)(2,1)} %right.1), channel_id=1, source_target_pairs={{0,2},{2,4},{4,6},{6,8},{8,10},{10,12},{12,14},{14,16},{16,18},{18... | collective-permute-start | bytes 786440 | tf_op jit(solution)/shard_map/ppermute | solution.py:222
  2.9 0.0 collective-permute-start
  3.6 0.0 copy-start
  3.6 0.6 %copy-done = s32[2]{0:T(128)S(1)} copy-done((s32[2]{0:T(128)S(1)}, s32[2]{0:T(128)}, u32[]{:S(2)}) %copy-start) | copy-done | bytes 32
  4.3 1.1 %pack.1 = (f32[8,256]{1,0:T(8,128)S(1)}, bf16[2,128,256]{2,1,0:T(8,128)(2,1)S(1)}, bf16[2,128,256]{2,1,0:T(8,128)(2,1)S(1)}, bf16[256,256]{1,0:T(8,128)(2,1)S(1)}, bf16[256,256]{1,0:T(8,128)(2,1)S(1)}) custom-call(s32[1]{0:T(128)S(6)} %copy.8.kept, s32[2]{0:T(128)S(1)} %copy-done, bf16[2,1,256,256]{3,2,1,0:T(8,128)(2,1)} %left.1, bf16[2,1,256,256]{3,2,1,0:T(8,128)(2,1)} %right.1), custom_call_target="tpu_custom_call" | custom-call | tf_op jit(solution)/shard_map/pack/pallas_call | solution.py:79
  5.4 0.1 collective-permute-start.3
  5.5 0.5 %collective-permute-start.4 = (bf16[2,128,256]{2,1,0:T(8,128)(2,1)S(1)}, bf16[2,128,256]{2,1,0:T(8,128)(2,1)S(1)}, u32[]{:S(2)}, u32[]{:S(2)}) collective-permute-start(bf16[2,128,256]{2,1,0:T(8,128)(2,1)S(1)} %get-tuple-element.21), channel_id=1, source_target_pairs={{0,1},{1,0},{2,3},{3,2},{4,5},{5,4},{6,7},{7,6},{8,9},{9,8},{10,11... | collective-permute-start | bytes 393224 | tf_op jit(solution)/shard_map/ppermute | solution.py:226
  6.0 0.1 collective-permute-start.5
  6.1 0.6 %collective-permute-done.3.info_other = f32[8,256]{1,0:T(8,128)S(1)} collective-permute-done((f32[8,256]{1,0:T(8,128)S(1)}, f32[8,256]{1,0:T(8,128)S(1)}, u32[]{:S(2)}, u32[]{:S(2)}) %collective-permute-start.3) | collective-permute-done | bytes 8224 | tf_op jit(solution)/shard_map/ppermute | solution.py:227
  6.6 0.2 collective-permute-start.6
  6.8 0.2 collective-permute-done.4.left_other
  7.0 0.4 %collective-permute-start.2 = (f32[8,256]{1,0:T(8,128)S(1)}, f32[8,256]{1,0:T(8,128)S(1)}, u32[]{:S(2)}, u32[]{:S(2)}) collective-permute-start(f32[8,256]{1,0:T(8,128)S(1)} %get-tuple-element.19.info_own.info), channel_id=1, source_target_pairs={{2,0},{4,2},{6,4},{8,6},{10,8},{12,10},{14,12},{16,14},{18,16},{20... | collective-permute-start | bytes 24584 | tf_op jit(solution)/shard_map/ppermute | solution.py:229
  7.3 0.0 collective-permute-done.5.refs_2_
  7.3 0.7 %collective-permute-done.6.refs_3_ = bf16[256,256]{1,0:T(8,128)(2,1)S(1)} collective-permute-done((bf16[256,256]{1,0:T(8,128)(2,1)S(1)}, bf16[256,256]{1,0:T(8,128)(2,1)S(1)}, u32[]{:S(2)}, u32[]{:S(2)}) %collective-permute-start.6) | collective-permute-done | bytes 131104 | tf_op jit(solution)/shard_map/ppermute | solution.py:228
  8.0 4.2 %centre.1 = (f32[4,1,4,128,256]{4,3,2,1,0:T(8,128)}, bf16[2,4,512,256]{3,2,1,0:T(8,128)(2,1)S(1)}) custom-call(bf16[4,1,4,256,256]{4,3,2,1,0:T(8,128)(2,1)} %psi.1, f32[8,256]{1,0:T(8,128)S(1)} %get-tuple-element.19.info_own.info, f32[8,256]{1,0:T(8,128)S(1)} %collective-permute-done.3.info_other, bf16[2,128,256]{2,1,0:T(8,128)(2,1)S(1)} %get-tuple-element.20.left_own, ...), custom_call_target="tpu_custom_call" | custom-call | tf_op jit(solution)/shard_map/centre/pallas_call | solution.py:254
  12.2 3.0 %collective-permute-done.2.note_a = f32[8,256]{1,0:T(8,128)S(1)} collective-permute-done((f32[8,256]{1,0:T(8,128)S(1)}, f32[8,256]{1,0:T(8,128)S(1)}, u32[]{:S(2)}, u32[]{:S(2)}) %collective-permute-start.2) | collective-permute-done | bytes 8224 | tf_op jit(solution)/shard_map/ppermute | solution.py:229
  15.2 0.0 collective-permute-done.1
  15.2 0.0 collective-permute-done
  15.3 0.0 collective-permute-start.8
  15.3 0.5 %collective-permute-start.9 = (bf16[2,1,256,256]{3,2,1,0:T(8,128)(2,1)S(1)}, bf16[2,1,256,256]{3,2,1,0:T(8,128)(2,1)S(1)}, u32[]{:S(2)}, u32[]{:S(2)}) collective-permute-start(bf16[2,1,256,256]{3,2,1,0:T(8,128)(2,1)S(1)} %collective-permute-done), channel_id=1, source_target_pairs={{0,1},{1,0},{2,3},{3,2},{4,5},{5,4},{6,7},{7,6},{8,9},{9,8},{10,11... | collective-permute-start | bytes 786440 | tf_op jit(solution)/shard_map/ppermute | solution.py:273
  15.8 0.1 collective-permute-start.7
  15.8 0.5 %own_rim.1 = (f32[512,256]{1,0:T(8,128)S(1)}, f32[512,256]{1,0:T(8,128)S(1)}) custom-call(bf16[2,4,512,256]{3,2,1,0:T(8,128)(2,1)S(1)} %get-tuple-element.27.rim, bf16[512,256]{1,0:T(8,128)(2,1)S(1)} %bitcast.5, bf16[512,256]{1,0:T(8,128)(2,1)S(1)} %bitcast.4), custom_call_target="tpu_custom_call" | custom-call | tf_op jit(solution)/shard_map/own_rim/pallas_call | solution.py:279
  16.3 0.9 %collective-permute-done.7.note_b = f32[8,256]{1,0:T(8,128)S(1)} collective-permute-done((f32[8,256]{1,0:T(8,128)S(1)}, f32[8,256]{1,0:T(8,128)S(1)}, u32[]{:S(2)}, u32[]{:S(2)}) %collective-permute-start.7) | collective-permute-done | bytes 8224 | tf_op jit(solution)/shard_map/ppermute | solution.py:275
  17.2 0.0 collective-permute-done.8
  17.2 0.0 collective-permute-done.9
  17.2 1.3 %last_rim.1 = f32[4,1,4,128,256]{4,3,2,1,0:T(8,128)} custom-call(f32[8,256]{1,0:T(8,128)S(1)} %get-tuple-element.19.info_own.info, f32[8,256]{1,0:T(8,128)S(1)} %collective-permute-done.2.note_a, f32[8,256]{1,0:T(8,128)S(1)} %collective-permute-done.7.note_b, bf16[2,4,512,256]{3,2,1,0:T(8,128)(2,1)S(1)} %get-tuple-element.27.rim, ...), custom_call_target="tpu_custom_call", output_to_operand_aliasing={{}: (8, {})} | custom-call | tf_op jit(solution)/shard_map/last_rim/pallas_call | solution.py:287
Async XLA Ops:
  0.0 15.2 %collective-permute-start.1 = (bf16[2,1,256,256]{3,2,1,0:T(8,128)(2,1)}, bf16[2,1,256,256]{3,2,1,0:T(8,128)(2,1)S(1)}, u32[]{:S(2)}, u32[]{:S(2)}) collective-permute-start(bf16[2,1,256,256]{3,2,1,0:T(8,128)(2,1)} %right.1), channel_id=1, source_target_pairs={{0,2},{2,4},{4,6},{6,8},{8,10},{10,12},{12,14},{14,16},{16,18},{18... | collective-permute-start | bytes 786440 | tf_op jit(solution)/shard_map/ppermute | solution.py:222
  2.9 12.3 %collective-permute-start = (bf16[2,1,256,256]{3,2,1,0:T(8,128)(2,1)}, bf16[2,1,256,256]{3,2,1,0:T(8,128)(2,1)S(1)}, u32[]{:S(2)}, u32[]{:S(2)}) collective-permute-start(bf16[2,1,256,256]{3,2,1,0:T(8,128)(2,1)} %right.1), channel_id=1, source_target_pairs={{2,0},{4,2},{6,4},{8,6},{10,8},{12,10},{14,12},{16,14},{18,16},{20... | collective-permute-start | bytes 786440 | tf_op jit(solution)/shard_map/ppermute | solution.py:221
  3.6 0.7 %copy-start = (s32[2]{0:T(128)S(1)}, s32[2]{0:T(128)}, u32[]{:S(2)}) copy-start(s32[2]{0:T(128)} %ops.1) | copy-start | bytes 28
  5.4 1.2 %collective-permute-start.3 = (f32[8,256]{1,0:T(8,128)S(1)}, f32[8,256]{1,0:T(8,128)S(1)}, u32[]{:S(2)}, u32[]{:S(2)}) collective-permute-start(f32[8,256]{1,0:T(8,128)S(1)} %get-tuple-element.19.info_own.info), channel_id=1, source_target_pairs={{0,1},{1,0},{2,3},{3,2},{4,5},{5,4},{6,7},{7,6},{8,9},{9,8},{10,11... | collective-permute-start | bytes 24584 | tf_op jit(solution)/shard_map/ppermute | solution.py:227
  5.5 1.5 %collective-permute-start.4 = (bf16[2,128,256]{2,1,0:T(8,128)(2,1)S(1)}, bf16[2,128,256]{2,1,0:T(8,128)(2,1)S(1)}, u32[]{:S(2)}, u32[]{:S(2)}) collective-permute-start(bf16[2,128,256]{2,1,0:T(8,128)(2,1)S(1)} %get-tuple-element.21), channel_id=1, source_target_pairs={{0,1},{1,0},{2,3},{3,2},{4,5},{5,4},{6,7},{7,6},{8,9},{9,8},{10,11... | collective-permute-start | bytes 393224 | tf_op jit(solution)/shard_map/ppermute | solution.py:226
  6.0 1.4 %collective-permute-start.5 = (bf16[256,256]{1,0:T(8,128)(2,1)S(1)}, bf16[256,256]{1,0:T(8,128)(2,1)S(1)}, u32[]{:S(2)}, u32[]{:S(2)}) collective-permute-start(bf16[256,256]{1,0:T(8,128)(2,1)S(1)} %get-tuple-element.22.refs_0_), channel_id=1, source_target_pairs={{0,1},{1,0},{2,3},{3,2},{4,5},{5,4},{6,7},{7,6},{8,9},{9,8},{10,11... | collective-permute-start | bytes 393224 | tf_op jit(solution)/shard_map/ppermute | solution.py:228
  6.6 1.3 %collective-permute-start.6 = (bf16[256,256]{1,0:T(8,128)(2,1)S(1)}, bf16[256,256]{1,0:T(8,128)(2,1)S(1)}, u32[]{:S(2)}, u32[]{:S(2)}) collective-permute-start(bf16[256,256]{1,0:T(8,128)(2,1)S(1)} %get-tuple-element.23.refs_1_), channel_id=1, source_target_pairs={{0,1},{1,0},{2,3},{3,2},{4,5},{5,4},{6,7},{7,6},{8,9},{9,8},{10,11... | collective-permute-start | bytes 393224 | tf_op jit(solution)/shard_map/ppermute | solution.py:228
  7.0 8.3 %collective-permute-start.2 = (f32[8,256]{1,0:T(8,128)S(1)}, f32[8,256]{1,0:T(8,128)S(1)}, u32[]{:S(2)}, u32[]{:S(2)}) collective-permute-start(f32[8,256]{1,0:T(8,128)S(1)} %get-tuple-element.19.info_own.info), channel_id=1, source_target_pairs={{2,0},{4,2},{6,4},{8,6},{10,8},{12,10},{14,12},{16,14},{18,16},{20... | collective-permute-start | bytes 24584 | tf_op jit(solution)/shard_map/ppermute | solution.py:229
  15.3 1.9 %collective-permute-start.8 = (bf16[2,1,256,256]{3,2,1,0:T(8,128)(2,1)S(1)}, bf16[2,1,256,256]{3,2,1,0:T(8,128)(2,1)S(1)}, u32[]{:S(2)}, u32[]{:S(2)}) collective-permute-start(bf16[2,1,256,256]{3,2,1,0:T(8,128)(2,1)S(1)} %collective-permute-done.1), channel_id=1, source_target_pairs={{0,1},{1,0},{2,3},{3,2},{4,5},{5,4},{6,7},{7,6},{8,9},{9,8},{10,11... | collective-permute-start | bytes 786440 | tf_op jit(solution)/shard_map/ppermute | solution.py:274
  15.3 1.9 %collective-permute-start.9 = (bf16[2,1,256,256]{3,2,1,0:T(8,128)(2,1)S(1)}, bf16[2,1,256,256]{3,2,1,0:T(8,128)(2,1)S(1)}, u32[]{:S(2)}, u32[]{:S(2)}) collective-permute-start(bf16[2,1,256,256]{3,2,1,0:T(8,128)(2,1)S(1)} %collective-permute-done), channel_id=1, source_target_pairs={{0,1},{1,0},{2,3},{3,2},{4,5},{5,4},{6,7},{7,6},{8,9},{9,8},{10,11... | collective-permute-start | bytes 786440 | tf_op jit(solution)/shard_map/ppermute | solution.py:273
  15.8 1.4 %collective-permute-start.7 = (f32[8,256]{1,0:T(8,128)S(1)}, f32[8,256]{1,0:T(8,128)S(1)}, u32[]{:S(2)}, u32[]{:S(2)}) collective-permute-start(f32[8,256]{1,0:T(8,128)S(1)} %collective-permute-done.2.note_a), channel_id=1, source_target_pairs={{0,1},{1,0},{2,3},{3,2},{4,5},{5,4},{6,7},{7,6},{8,9},{9,8},{10,11... | collective-permute-start | bytes 24584 | tf_op jit(solution)/shard_map/ppermute | solution.py:275

commit v5 on v4

--- a/solution.py
+++ b/solution.py
@@ -32,7 +32,7 @@
 
 
 def below_is_a():
-    return lax.axis_index("term") == 1 if lax.axis_size("term") == 2 else True
+    return lax.axis_index("sector") % 2 == 0 if lax.axis_size("term") == 2 else True
 
 
 def info_rows(terms):
@@ -168,26 +168,33 @@
     rows = lax.broadcasted_iota(jnp.int32, shape, 0) + lax.axis_index("term") * half
     cols = lax.broadcasted_iota(jnp.int32, shape, 1)
     keep = (rows.astype(jnp.float32) < info[0:1, :]) & there
-    return keep & (cols.astype(jnp.float32) < note[0:1, :]), jnp.where(is_below, 3, 0)
-
-
-def own_rim_kernel(rim, own_a, own_b, part_a, part_b):
-    count, rows = own_a.shape[0] // rim.shape[-1], pl.ds(0, rim.shape[2])
-    part_a[...] = sum_terms(rim, 0, 0, own_a, count, rows)
-    part_b[...] = sum_terms(rim, 1, 0, own_b, count, rows)
-
-
-def last_rim_kernel(info, note_a, note_b, rim, other_a, other_b, part_a, part_b, sigma_in, sigma,
-                    out_buf, out_sem):
+    return keep & (cols.astype(jnp.float32) < note), jnp.where(is_below, 3, 0)
+
+
+def middle_kernel(rim, own_a, own_b, other_b, part_a, part_b):
+    own, other = own_b.shape[0] // rim.shape[-1], other_b.shape[0] // rim.shape[-1]
+    rows = pl.ds(0, rim.shape[2])
+    part_b[...] = sum_terms(
+        rim, 1, own, other_b, other, rows, sum_terms(rim, 1, 0, own_b, own, rows)
+    )
+    part_a[...] = sum_terms(rim, 0, 0, own_a, own, rows)
+
+
+def last_kernel(info, note, note_other, rim, other_a, part_a, part_b, sigma_in, sigma, out_buf, out_sem):
     _, nvec, half, size = out_buf.shape
     count, groups = other_a.shape[0] // size, out_sem.shape[1]
     first, per_group = rim.shape[1] - count, nvec // groups
+    direct = (lax.axis_index("term") == 0) == below_is_a()
+    notes = note[0:1, :], note_other[0:1, :]
+    note_a, note_b = jnp.where(direct, *notes), jnp.where(direct, *notes[::-1])
     stores = []
-    for which, note, blocks, part in ((0, note_a, other_a, part_a), (1, note_b, other_b, part_b)):
+    for which, note, part in ((1, note_b, part_b), (0, note_a, part_a)):
         keep, state = state_mask(which, info, note, half)
         for group in range(groups):
             rows = pl.ds(group * per_group * half, per_group * half)
-            total = sum_terms(rim, which, first, blocks, count, rows, part[rows, :])
+            total = part[rows, :]
+            if which == 0:
+                total = sum_terms(rim, 0, first, other_a, count, rows, total)
             for j in range(per_group):
                 out_buf[which, group * per_group + j] = jnp.where(
                     keep, total[j * half:(j + 1) * half], 0.0
@@ -208,6 +215,17 @@
     return up + [(2 * sectors - 2, 2 * sectors - 1)] + down + [(1, 0)]
 
 
+def pair_exchange(sectors, first):
+    pairs = []
+    for sector in range(sectors):
+        low = sector if (sector - first) % 2 == 0 else sector - 1
+        alone = low < 0 or low + 1 >= sectors
+        for core in range(2):
+            target = 2 * sector + 1 - core if alone else 2 * (2 * low + 1 - sector) + core
+            pairs.append((2 * sector + core, target))
+    return pairs
+
+
 def shards(psi, left_env, right_env, op_index, kept_rows):
     sectors, cores = lax.axis_size("sector"), lax.axis_size("term")
     nvec, size = psi.shape[0], psi.shape[-1]
@@ -217,16 +235,15 @@
 
     if cores == 2:
         cycle = two_core_cycle(sectors)
-        reverse = [(b, a) for a, b in cycle]
-        own_a = lax.ppermute(right_env, ("sector", "term"), reverse)
-        own_b = lax.ppermute(right_env, ("sector", "term"), cycle)
+        own_b = lax.ppermute(right_env, ("sector", "term"), pair_exchange(sectors, 0))
+        own_a = lax.ppermute(right_env, ("sector", "term"), pair_exchange(sectors, 1))
         info_own, left_own, left_sent, rights = pack(
             kept_rows, op_index, left_env, right_env, half
         )
         left_other = lax.ppermute(left_sent, "term", swap)
         info_other = lax.ppermute(info_own, "term", swap)
         rights += [lax.ppermute(x, "term", swap) for x in rights]
-        note_a = lax.ppermute(info_own, ("sector", "term"), reverse)
+        note = lax.ppermute(info_own, ("sector", "term"), cycle)
     else:
         forward = [(i, i + 1) for i in range(sectors - 1)]
         backward = [(b, a) for a, b in forward]
@@ -242,8 +259,8 @@
             blocks = lax.all_gather(lax.ppermute(right_env, "sector", pairs), "term", tiled=True)
             return *jnp.split(blocks, 2), lax.ppermute(info_own, "sector", pairs)
 
-        own_a, other_a, note_a = neighbour(forward)
-        own_b, other_b, note_b = neighbour(backward)
+        own_a, other_a, note = neighbour(forward)
+        own_b, other_b, note_other = neighbour(backward)
 
     sigma_shape = jax.ShapeDtypeStruct((nvec, 1, 4, half, size), jnp.float32)
     rim_shape = jax.ShapeDtypeStruct((2, terms, nvec * half, size), jnp.bfloat16)
@@ -268,35 +285,34 @@
         name="centre",
     )(psi, info_own, info_other, left_own, left_other, *rights)
 
-    own_a, own_b, note_a, sigma, rim = lax.optimization_barrier((own_a, own_b, note_a, sigma, rim))
+    own_a, own_b = own_a.reshape(-1, size), own_b.reshape(-1, size)
+    own_b, sigma, rim = lax.optimization_barrier((own_b, sigma, rim))
+    own_a, note, sigma = lax.optimization_barrier((own_a, note, sigma))
     if cores == 2:
-        other_b = lax.ppermute(own_a, "term", swap)
-        other_a = lax.ppermute(own_b, "term", swap)
-        note_b = lax.ppermute(note_a, "term", swap)
-    own_a, own_b, other_a, other_b = [
-        x.reshape(-1, size) for x in (own_a, own_b, other_a, other_b)
-    ]
+        other_b = lax.ppermute(own_b, "term", swap)
+        other_a = lax.ppermute(own_a, "term", swap)
+        note_other = lax.ppermute(note, "term", swap)
     part_a, part_b = pl.pallas_call(
-        own_rim_kernel,
+        middle_kernel,
         out_shape=(part_shape, part_shape),
-        in_specs=[VMEM] * 3,
+        in_specs=[VMEM] * 4,
         out_specs=(VMEM, VMEM),
         compiler_params=params,
-        name="own_rim",
-    )(rim, own_a, own_b)
+        name="middle",
+    )(rim, own_a, own_b, other_b.reshape(-1, size))
     return pl.pallas_call(
-        last_rim_kernel,
+        last_kernel,
         out_shape=sigma_shape,
-        in_specs=[VMEM] * 8 + [HBM],
+        in_specs=[VMEM] * 7 + [HBM],
         out_specs=HBM,
         scratch_shapes=[
             pltpu.VMEM((2, nvec, half, size), jnp.float32),
             pltpu.SemaphoreType.DMA((2, groups)),
         ],
-        input_output_aliases={8: 0},
+        input_output_aliases={7: 0},
         compiler_params=params,
-        name="last_rim",
-    )(info_own, note_a, note_b, rim, other_a, other_b, part_a, part_b, sigma)
+        name="last",
+    )(info_own, note, note_other, rim, other_a.reshape(-1, size), part_a, part_b, sigma)
 
 
 def solution(mesh):

time: 18.7 us -> 18.2 us (0.973)
  waiting for transfers between devices: 5.28 us -> 1.77 us
  starting transfers between devices: 4.69 us -> 7.57 us
    ppermute x6, waiting for transfers between devices: 3.88 us -> 1.27 us  [the longest x1 0.94 us: shards(): other_b = lax.ppermute(own_b, 'term', swap)]
    ppermute x6, starting transfers between devices: 3.88 us -> 6.14 us  [the longest x1 2.94 us: shards(): lax.ppermute(right_env, ('sector', 'term'), pair_exchange(sectors, 0))]
    ppermute x2, waiting for transfers between devices: 0.66 us -> 0.01 us  [shards(): rights += [lax.ppermute(x, 'term', swap) for x in rights]]
    ppermute x2, starting transfers between devices: 0.24 us -> 0.78 us  [shards(): rights += [lax.ppermute(x, 'term', swap) for x in rights]]
    ppermute x1, starting transfers between devices: 0.07 us -> 0.57 us  [shards(): info_other = lax.ppermute(info_own, 'term', swap)]
    ppermute x1, starting transfers between devices: 0.5 us -> 0.08 us  [shards(): left_other = lax.ppermute(left_sent, 'term', swap)]
    ppermute x1, waiting for transfers between devices: 0.58 us -> 0.32 us  [shards(): info_other = lax.ppermute(info_own, 'term', swap)]
  transfers between devices with their start and end apart: 10 -> 10, of which waited for: 5 -> 4; matrix products, arithmetic and copies ran while one was open for 0% -> 0% of each run, Pallas kernels for 32% -> 34%
where the time goes in v5:
time: 18.2 us; the launch traced here: 17.9 us
  starting transfers between devices  7.57 us (42%)
  Pallas kernels  7.25 us (40%)
  waiting for transfers between devices  1.77 us (10%)
  between operations  0.71 us (4%)
  local copies, waits for them, and re-layouts  0.65 us (4%)
    pallas_call x1, Pallas kernels, shards(): pl.pallas_call(centre_kernel, out_shape=(sigma_shape, rim_shape), in_spec...  4.25 us
    ppermute x1, starting transfers between devices, shards(): lax.ppermute(right_env, ('sector', 'term'), pair_exchange(sectors, 0))  2.94 us
    ppermute x1, starting transfers between devices, shards(): note = lax.ppermute(info_own, ('sector', 'term'), cycle)  2.62 us
    pallas_call x1, Pallas kernels, shards(): pl.pallas_call(last_kernel, out_shape=sigma_shape, in_specs=[VMEM] * 7 +...  1.25 us
    pallas_call x1, Pallas kernels, pack(): pl.pallas_call(pack_kernel, out_shape=(jax.ShapeDtypeStruct((info_rows(te...  1.15 us
    ppermute x1, waiting for transfers between devices, shards(): other_b = lax.ppermute(own_b, 'term', swap)  0.94 us
    ppermute x2, starting transfers between devices, shards(): rights += [lax.ppermute(x, 'term', swap) for x in rights]  0.78 us
    unnamed x2, local copies, waits for them, and re-layouts  0.65 us
  transfers between devices with their start and end apart: 10, of which 4 were waited for; matrix products, arithmetic and copies ran while one was open for 0% of the time, Pallas kernels for 34%

profile of v5, /device:TPU:0, one launch (start us, length us, event | category | flops | bytes accessed | tf_op | source)
XLA Modules:
  0.0 17.9 jit_solution(4081229352931801345)
XLA Ops:
  0.0 2.9 %collective-permute-start.2 = (bf16[2,1,256,256]{3,2,1,0:T(8,128)(2,1)}, bf16[2,1,256,256]{3,2,1,0:T(8,128)(2,1)S(1)}, u32[]{:S(2)}, u32[]{:S(2)}) collective-permute-start(bf16[2,1,256,256]{3,2,1,0:T(8,128)(2,1)} %right.1), channel_id=1, source_target_pairs={{0,2},{1,3},{2,0},{3,1},{4,6},{5,7},{6,4},{7,5},{8,10},{9,11},{10,... | collective-permute-start | bytes 786440 | tf_op jit(solution)/shard_map/ppermute | solution.py:238
  2.9 0.0 collective-permute-start
  3.6 0.0 copy-start
  3.6 0.6 %copy-done = s32[2]{0:T(128)S(1)} copy-done((s32[2]{0:T(128)S(1)}, s32[2]{0:T(128)}, u32[]{:S(2)}) %copy-start) | copy-done | bytes 32
  4.3 1.1 %pack.1 = (f32[8,256]{1,0:T(8,128)S(1)}, bf16[2,128,256]{2,1,0:T(8,128)(2,1)S(1)}, bf16[2,128,256]{2,1,0:T(8,128)(2,1)S(1)}, bf16[256,256]{1,0:T(8,128)(2,1)S(1)}, bf16[256,256]{1,0:T(8,128)(2,1)S(1)}) custom-call(s32[1]{0:T(128)S(6)} %copy.8.kept, s32[2]{0:T(128)S(1)} %copy-done, bf16[2,1,256,256]{3,2,1,0:T(8,128)(2,1)} %left.1, bf16[2,1,256,256]{3,2,1,0:T(8,128)(2,1)} %right.1), custom_call_target="tpu_custom_call" | custom-call | tf_op jit(solution)/shard_map/pack/pallas_call | solution.py:79
  5.4 0.6 %collective-permute-start.3 = (f32[8,256]{1,0:T(8,128)S(1)}, f32[8,256]{1,0:T(8,128)S(1)}, u32[]{:S(2)}, u32[]{:S(2)}) collective-permute-start(f32[8,256]{1,0:T(8,128)S(1)} %get-tuple-element.20.info_own.info), channel_id=1, source_target_pairs={{0,1},{1,0},{2,3},{3,2},{4,5},{5,4},{6,7},{7,6},{8,9},{9,8},{10,11... | collective-permute-start | bytes 24584 | tf_op jit(solution)/shard_map/ppermute | solution.py:244
  6.0 0.1 collective-permute-start.4
  6.1 0.4 %collective-permute-start.5 = (bf16[256,256]{1,0:T(8,128)(2,1)S(1)}, bf16[256,256]{1,0:T(8,128)(2,1)S(1)}, u32[]{:S(2)}, u32[]{:S(2)}) collective-permute-start(bf16[256,256]{1,0:T(8,128)(2,1)S(1)} %get-tuple-element.23.refs_0_), channel_id=1, source_target_pairs={{0,1},{1,0},{2,3},{3,2},{4,5},{5,4},{6,7},{7,6},{8,9},{9,8},{10,11... | collective-permute-start | bytes 393224 | tf_op jit(solution)/shard_map/ppermute | solution.py:245
  6.5 0.3 %collective-permute-done.3.info_other = f32[8,256]{1,0:T(8,128)S(1)} collective-permute-done((f32[8,256]{1,0:T(8,128)S(1)}, f32[8,256]{1,0:T(8,128)S(1)}, u32[]{:S(2)}, u32[]{:S(2)}) %collective-permute-start.3) | collective-permute-done | bytes 8224 | tf_op jit(solution)/shard_map/ppermute | solution.py:244
  6.8 0.3 %collective-permute-start.6 = (bf16[256,256]{1,0:T(8,128)(2,1)S(1)}, bf16[256,256]{1,0:T(8,128)(2,1)S(1)}, u32[]{:S(2)}, u32[]{:S(2)}) collective-permute-start(bf16[256,256]{1,0:T(8,128)(2,1)S(1)} %get-tuple-element.24.refs_1_), channel_id=1, source_target_pairs={{0,1},{1,0},{2,3},{3,2},{4,5},{5,4},{6,7},{7,6},{8,9},{9,8},{10,11... | collective-permute-start | bytes 393224 | tf_op jit(solution)/shard_map/ppermute | solution.py:245
  7.2 0.2 collective-permute-done.4.left_other
  7.3 2.6 %collective-permute-start.1 = (f32[8,256]{1,0:T(8,128)S(1)}, f32[8,256]{1,0:T(8,128)S(1)}, u32[]{:S(2)}, u32[]{:S(2)}) collective-permute-start(f32[8,256]{1,0:T(8,128)S(1)} %get-tuple-element.20.info_own.info), channel_id=1, source_target_pairs={{0,2},{2,4},{4,6},{6,8},{8,10},{10,12},{12,14},{14,16},{16,18},{18... | collective-permute-start | bytes 24584 | tf_op jit(solution)/shard_map/ppermute | solution.py:246
  9.9 0.0 collective-permute-done.5.refs_2_
  10.0 0.0 collective-permute-done.6.refs_3_
  10.0 4.2 %centre.1 = (f32[4,1,4,128,256]{4,3,2,1,0:T(8,128)}, bf16[2,4,512,256]{3,2,1,0:T(8,128)(2,1)S(1)}) custom-call(bf16[4,1,4,256,256]{4,3,2,1,0:T(8,128)(2,1)} %psi.1, f32[8,256]{1,0:T(8,128)S(1)} %get-tuple-element.20.info_own.info, f32[8,256]{1,0:T(8,128)S(1)} %collective-permute-done.3.info_other, bf16[2,128,256]{2,1,0:T(8,128)(2,1)S(1)} %get-tuple-element.21.left_own, ...), custom_call_target="tpu_custom_call" | custom-call | tf_op jit(solution)/shard_map/centre/pallas_call | solution.py:271
  14.2 0.3 %collective-permute-done.2 = bf16[2,1,256,256]{3,2,1,0:T(8,128)(2,1)S(1)} collective-permute-done((bf16[2,1,256,256]{3,2,1,0:T(8,128)(2,1)}, bf16[2,1,256,256]{3,2,1,0:T(8,128)(2,1)S(1)}, u32[]{:S(2)}, u32[]{:S(2)}) %collective-permute-start.2) | collective-permute-done | bytes 262176 | tf_op jit(solution)/shard_map/ppermute | solution.py:238
  14.5 0.0 collective-permute-start.9
  14.5 0.0 collective-permute-done.1.note
  14.5 0.0 collective-permute-done
  14.5 0.5 %collective-permute-start.8 = (bf16[512,256]{1,0:T(8,128)(2,1)S(1)}, bf16[512,256]{1,0:T(8,128)(2,1)S(1)}, u32[]{:S(2)}, u32[]{:S(2)}) collective-permute-start(bf16[512,256]{1,0:T(8,128)(2,1)S(1)} %bitcast.2), channel_id=1, source_target_pairs={{0,1},{1,0},{2,3},{3,2},{4,5},{5,4},{6,7},{7,6},{8,9},{9,8},{10,11... | collective-permute-start | bytes 786440 | tf_op jit(solution)/shard_map/ppermute | solution.py:293
  15.0 0.1 collective-permute-start.7
  15.1 0.9 %collective-permute-done.9.other_b = bf16[512,256]{1,0:T(8,128)(2,1)S(1)} collective-permute-done((bf16[512,256]{1,0:T(8,128)(2,1)S(1)}, bf16[512,256]{1,0:T(8,128)(2,1)S(1)}, u32[]{:S(2)}, u32[]{:S(2)}) %collective-permute-start.9) | collective-permute-done | bytes 262176 | tf_op jit(solution)/shard_map/ppermute | solution.py:292
  16.1 0.6 %middle.1 = (f32[512,256]{1,0:T(8,128)S(1)}, f32[512,256]{1,0:T(8,128)S(1)}) custom-call(bf16[2,4,512,256]{3,2,1,0:T(8,128)(2,1)S(1)} %get-tuple-element.29.rim, bf16[512,256]{1,0:T(8,128)(2,1)S(1)} %bitcast.3, bf16[512,256]{1,0:T(8,128)(2,1)S(1)} %bitcast.5, bf16[512,256]{1,0:T(8,128)(2,1)S(1)} %collective-permute-done.9.other_b), custom_call_target="tpu_custom_call" | custom-call | tf_op jit(solution)/shard_map/middle/pallas_call | solution.py:295
  16.7 0.0 collective-permute-done.7.note_other
  16.7 0.0 collective-permute-done.8.other_a
  16.7 1.2 %last.1 = f32[4,1,4,128,256]{4,3,2,1,0:T(8,128)} custom-call(f32[8,256]{1,0:T(8,128)S(1)} %get-tuple-element.20.info_own.info, f32[8,256]{1,0:T(8,128)S(1)} %collective-permute-done.1.note, f32[8,256]{1,0:T(8,128)S(1)} %collective-permute-done.7.note_other, bf16[2,4,512,256]{3,2,1,0:T(8,128)(2,1)S(1)} %get-tuple-element.29.rim, ...), custom_call_target="tpu_custom_call", output_to_operand_aliasing={{}: (7, {})} | custom-call | tf_op jit(solution)/shard_map/last/pallas_call | solution.py:303
Async XLA Ops:
  0.0 14.5 %collective-permute-start.2 = (bf16[2,1,256,256]{3,2,1,0:T(8,128)(2,1)}, bf16[2,1,256,256]{3,2,1,0:T(8,128)(2,1)S(1)}, u32[]{:S(2)}, u32[]{:S(2)}) collective-permute-start(bf16[2,1,256,256]{3,2,1,0:T(8,128)(2,1)} %right.1), channel_id=1, source_target_pairs={{0,2},{1,3},{2,0},{3,1},{4,6},{5,7},{6,4},{7,5},{8,10},{9,11},{10,... | collective-permute-start | bytes 786440 | tf_op jit(solution)/shard_map/ppermute | solution.py:238
  2.9 11.6 %collective-permute-start = (bf16[2,1,256,256]{3,2,1,0:T(8,128)(2,1)}, bf16[2,1,256,256]{3,2,1,0:T(8,128)(2,1)S(1)}, u32[]{:S(2)}, u32[]{:S(2)}) collective-permute-start(bf16[2,1,256,256]{3,2,1,0:T(8,128)(2,1)} %right.1), channel_id=1, source_target_pairs={{0,1},{1,0},{2,4},{3,5},{4,2},{5,3},{6,8},{7,9},{8,6},{9,7},{10,12... | collective-permute-start | bytes 786440 | tf_op jit(solution)/shard_map/ppermute | solution.py:239
  3.6 0.7 %copy-start = (s32[2]{0:T(128)S(1)}, s32[2]{0:T(128)}, u32[]{:S(2)}) copy-start(s32[2]{0:T(128)} %ops.1) | copy-start | bytes 28
  5.4 1.4 %collective-permute-start.3 = (f32[8,256]{1,0:T(8,128)S(1)}, f32[8,256]{1,0:T(8,128)S(1)}, u32[]{:S(2)}, u32[]{:S(2)}) collective-permute-start(f32[8,256]{1,0:T(8,128)S(1)} %get-tuple-element.20.info_own.info), channel_id=1, source_target_pairs={{0,1},{1,0},{2,3},{3,2},{4,5},{5,4},{6,7},{7,6},{8,9},{9,8},{10,11... | collective-permute-start | bytes 24584 | tf_op jit(solution)/shard_map/ppermute | solution.py:244
  6.0 1.3 %collective-permute-start.4 = (bf16[2,128,256]{2,1,0:T(8,128)(2,1)S(1)}, bf16[2,128,256]{2,1,0:T(8,128)(2,1)S(1)}, u32[]{:S(2)}, u32[]{:S(2)}) collective-permute-start(bf16[2,128,256]{2,1,0:T(8,128)(2,1)S(1)} %get-tuple-element.22), channel_id=1, source_target_pairs={{0,1},{1,0},{2,3},{3,2},{4,5},{5,4},{6,7},{7,6},{8,9},{9,8},{10,11... | collective-permute-start | bytes 393224 | tf_op jit(solution)/shard_map/ppermute | solution.py:243
  6.1 3.9 %collective-permute-start.5 = (bf16[256,256]{1,0:T(8,128)(2,1)S(1)}, bf16[256,256]{1,0:T(8,128)(2,1)S(1)}, u32[]{:S(2)}, u32[]{:S(2)}) collective-permute-start(bf16[256,256]{1,0:T(8,128)(2,1)S(1)} %get-tuple-element.23.refs_0_), channel_id=1, source_target_pairs={{0,1},{1,0},{2,3},{3,2},{4,5},{5,4},{6,7},{7,6},{8,9},{9,8},{10,11... | collective-permute-start | bytes 393224 | tf_op jit(solution)/shard_map/ppermute | solution.py:245
  6.8 3.1 %collective-permute-start.6 = (bf16[256,256]{1,0:T(8,128)(2,1)S(1)}, bf16[256,256]{1,0:T(8,128)(2,1)S(1)}, u32[]{:S(2)}, u32[]{:S(2)}) collective-permute-start(bf16[256,256]{1,0:T(8,128)(2,1)S(1)} %get-tuple-element.24.refs_1_), channel_id=1, source_target_pairs={{0,1},{1,0},{2,3},{3,2},{4,5},{5,4},{6,7},{7,6},{8,9},{9,8},{10,11... | collective-permute-start | bytes 393224 | tf_op jit(solution)/shard_map/ppermute | solution.py:245
  7.3 7.2 %collective-permute-start.1 = (f32[8,256]{1,0:T(8,128)S(1)}, f32[8,256]{1,0:T(8,128)S(1)}, u32[]{:S(2)}, u32[]{:S(2)}) collective-permute-start(f32[8,256]{1,0:T(8,128)S(1)} %get-tuple-element.20.info_own.info), channel_id=1, source_target_pairs={{0,2},{2,4},{4,6},{6,8},{8,10},{10,12},{12,14},{14,16},{16,18},{18... | collective-permute-start | bytes 24584 | tf_op jit(solution)/shard_map/ppermute | solution.py:246
  14.5 1.5 %collective-permute-start.9 = (bf16[512,256]{1,0:T(8,128)(2,1)S(1)}, bf16[512,256]{1,0:T(8,128)(2,1)S(1)}, u32[]{:S(2)}, u32[]{:S(2)}) collective-permute-start(bf16[512,256]{1,0:T(8,128)(2,1)S(1)} %bitcast.4), channel_id=1, source_target_pairs={{0,1},{1,0},{2,3},{3,2},{4,5},{5,4},{6,7},{7,6},{8,9},{9,8},{10,11... | collective-permute-start | bytes 786440 | tf_op jit(solution)/shard_map/ppermute | solution.py:292
  14.5 2.1 %collective-permute-start.8 = (bf16[512,256]{1,0:T(8,128)(2,1)S(1)}, bf16[512,256]{1,0:T(8,128)(2,1)S(1)}, u32[]{:S(2)}, u32[]{:S(2)}) collective-permute-start(bf16[512,256]{1,0:T(8,128)(2,1)S(1)} %bitcast.2), channel_id=1, source_target_pairs={{0,1},{1,0},{2,3},{3,2},{4,5},{5,4},{6,7},{7,6},{8,9},{9,8},{10,11... | collective-permute-start | bytes 786440 | tf_op jit(solution)/shard_map/ppermute | solution.py:293
  15.0 1.6 %collective-permute-start.7 = (f32[8,256]{1,0:T(8,128)S(1)}, f32[8,256]{1,0:T(8,128)S(1)}, u32[]{:S(2)}, u32[]{:S(2)}) collective-permute-start(f32[8,256]{1,0:T(8,128)S(1)} %collective-permute-done.1.note), channel_id=1, source_target_pairs={{0,1},{1,0},{2,3},{3,2},{4,5},{5,4},{6,7},{7,6},{8,9},{9,8},{10,11... | collective-permute-start | bytes 24584 | tf_op jit(solution)/shard_map/ppermute | solution.py:294

commit v6 on v5

--- a/solution.py
+++ b/solution.py
@@ -184,7 +184,7 @@
     _, nvec, half, size = out_buf.shape
     count, groups = other_a.shape[0] // size, out_sem.shape[1]
     first, per_group = rim.shape[1] - count, nvec // groups
-    direct = (lax.axis_index("term") == 0) == below_is_a()
+    direct = (lax.axis_index("term") == 0) == below_is_a() if lax.axis_size("term") == 2 else True
     notes = note[0:1, :], note_other[0:1, :]
     note_a, note_b = jnp.where(direct, *notes), jnp.where(direct, *notes[::-1])
     stores = []

time: 18.2 us -> 18.2 us (level)
  no operation moved by 1% of the time
where the time goes in v6:
time: 18.2 us; the launch traced here: 17.9 us
  starting transfers between devices  7.57 us (42%)
  Pallas kernels  7.25 us (40%)
  waiting for transfers between devices  1.77 us (10%)
  between operations  0.71 us (4%)
  local copies, waits for them, and re-layouts  0.65 us (4%)
    pallas_call x1, Pallas kernels, shards(): pl.pallas_call(centre_kernel, out_shape=(sigma_shape, rim_shape), in_spec...  4.25 us
    ppermute x1, starting transfers between devices, shards(): lax.ppermute(right_env, ('sector', 'term'), pair_exchange(sectors, 0))  2.94 us
    ppermute x1, starting transfers between devices, shards(): note = lax.ppermute(info_own, ('sector', 'term'), cycle)  2.62 us
    pallas_call x1, Pallas kernels, shards(): pl.pallas_call(last_kernel, out_shape=sigma_shape, in_specs=[VMEM] * 7 +...  1.25 us
    pallas_call x1, Pallas kernels, pack(): pl.pallas_call(pack_kernel, out_shape=(jax.ShapeDtypeStruct((info_rows(te...  1.15 us
    ppermute x1, waiting for transfers between devices, shards(): other_b = lax.ppermute(own_b, 'term', swap)  0.94 us
    ppermute x2, starting transfers between devices, shards(): rights += [lax.ppermute(x, 'term', swap) for x in rights]  0.78 us
    unnamed x2, local copies, waits for them, and re-layouts  0.65 us
  transfers between devices with their start and end apart: 10, of which 4 were waited for; matrix products, arithmetic and copies ran while one was open for 0% of the time, Pallas kernels for 34%

profile of v6, /device:TPU:0, one launch (start us, length us, event | category | flops | bytes accessed | tf_op | source)
XLA Modules:
  0.0 17.9 jit_solution(4081229352931801345)
XLA Ops:
  0.0 2.9 %collective-permute-start.2 = (bf16[2,1,256,256]{3,2,1,0:T(8,128)(2,1)}, bf16[2,1,256,256]{3,2,1,0:T(8,128)(2,1)S(1)}, u32[]{:S(2)}, u32[]{:S(2)}) collective-permute-start(bf16[2,1,256,256]{3,2,1,0:T(8,128)(2,1)} %right.1), channel_id=1, source_target_pairs={{0,2},{1,3},{2,0},{3,1},{4,6},{5,7},{6,4},{7,5},{8,10},{9,11},{10,... | collective-permute-start | bytes 786440 | tf_op jit(solution)/shard_map/ppermute | solution.py:238
  2.9 0.0 collective-permute-start
  3.6 0.0 copy-start
  3.6 0.6 %copy-done = s32[2]{0:T(128)S(1)} copy-done((s32[2]{0:T(128)S(1)}, s32[2]{0:T(128)}, u32[]{:S(2)}) %copy-start) | copy-done | bytes 32
  4.3 1.1 %pack.1 = (f32[8,256]{1,0:T(8,128)S(1)}, bf16[2,128,256]{2,1,0:T(8,128)(2,1)S(1)}, bf16[2,128,256]{2,1,0:T(8,128)(2,1)S(1)}, bf16[256,256]{1,0:T(8,128)(2,1)S(1)}, bf16[256,256]{1,0:T(8,128)(2,1)S(1)}) custom-call(s32[1]{0:T(128)S(6)} %copy.8.kept, s32[2]{0:T(128)S(1)} %copy-done, bf16[2,1,256,256]{3,2,1,0:T(8,128)(2,1)} %left.1, bf16[2,1,256,256]{3,2,1,0:T(8,128)(2,1)} %right.1), custom_call_target="tpu_custom_call" | custom-call | tf_op jit(solution)/shard_map/pack/pallas_call | solution.py:79
  5.4 0.6 %collective-permute-start.3 = (f32[8,256]{1,0:T(8,128)S(1)}, f32[8,256]{1,0:T(8,128)S(1)}, u32[]{:S(2)}, u32[]{:S(2)}) collective-permute-start(f32[8,256]{1,0:T(8,128)S(1)} %get-tuple-element.20.info_own.info), channel_id=1, source_target_pairs={{0,1},{1,0},{2,3},{3,2},{4,5},{5,4},{6,7},{7,6},{8,9},{9,8},{10,11... | collective-permute-start | bytes 24584 | tf_op jit(solution)/shard_map/ppermute | solution.py:244
  6.0 0.1 collective-permute-start.4
  6.1 0.4 %collective-permute-start.5 = (bf16[256,256]{1,0:T(8,128)(2,1)S(1)}, bf16[256,256]{1,0:T(8,128)(2,1)S(1)}, u32[]{:S(2)}, u32[]{:S(2)}) collective-permute-start(bf16[256,256]{1,0:T(8,128)(2,1)S(1)} %get-tuple-element.23.refs_0_), channel_id=1, source_target_pairs={{0,1},{1,0},{2,3},{3,2},{4,5},{5,4},{6,7},{7,6},{8,9},{9,8},{10,11... | collective-permute-start | bytes 393224 | tf_op jit(solution)/shard_map/ppermute | solution.py:245
  6.5 0.3 %collective-permute-done.3.info_other = f32[8,256]{1,0:T(8,128)S(1)} collective-permute-done((f32[8,256]{1,0:T(8,128)S(1)}, f32[8,256]{1,0:T(8,128)S(1)}, u32[]{:S(2)}, u32[]{:S(2)}) %collective-permute-start.3) | collective-permute-done | bytes 8224 | tf_op jit(solution)/shard_map/ppermute | solution.py:244
  6.8 0.3 %collective-permute-start.6 = (bf16[256,256]{1,0:T(8,128)(2,1)S(1)}, bf16[256,256]{1,0:T(8,128)(2,1)S(1)}, u32[]{:S(2)}, u32[]{:S(2)}) collective-permute-start(bf16[256,256]{1,0:T(8,128)(2,1)S(1)} %get-tuple-element.24.refs_1_), channel_id=1, source_target_pairs={{0,1},{1,0},{2,3},{3,2},{4,5},{5,4},{6,7},{7,6},{8,9},{9,8},{10,11... | collective-permute-start | bytes 393224 | tf_op jit(solution)/shard_map/ppermute | solution.py:245
  7.2 0.2 collective-permute-done.4.left_other
  7.3 2.6 %collective-permute-start.1 = (f32[8,256]{1,0:T(8,128)S(1)}, f32[8,256]{1,0:T(8,128)S(1)}, u32[]{:S(2)}, u32[]{:S(2)}) collective-permute-start(f32[8,256]{1,0:T(8,128)S(1)} %get-tuple-element.20.info_own.info), channel_id=1, source_target_pairs={{0,2},{2,4},{4,6},{6,8},{8,10},{10,12},{12,14},{14,16},{16,18},{18... | collective-permute-start | bytes 24584 | tf_op jit(solution)/shard_map/ppermute | solution.py:246
  9.9 0.0 collective-permute-done.5.refs_2_
  10.0 0.0 collective-permute-done.6.refs_3_
  10.0 4.2 %centre.1 = (f32[4,1,4,128,256]{4,3,2,1,0:T(8,128)}, bf16[2,4,512,256]{3,2,1,0:T(8,128)(2,1)S(1)}) custom-call(bf16[4,1,4,256,256]{4,3,2,1,0:T(8,128)(2,1)} %psi.1, f32[8,256]{1,0:T(8,128)S(1)} %get-tuple-element.20.info_own.info, f32[8,256]{1,0:T(8,128)S(1)} %collective-permute-done.3.info_other, bf16[2,128,256]{2,1,0:T(8,128)(2,1)S(1)} %get-tuple-element.21.left_own, ...), custom_call_target="tpu_custom_call" | custom-call | tf_op jit(solution)/shard_map/centre/pallas_call | solution.py:271
  14.2 0.3 %collective-permute-done.2 = bf16[2,1,256,256]{3,2,1,0:T(8,128)(2,1)S(1)} collective-permute-done((bf16[2,1,256,256]{3,2,1,0:T(8,128)(2,1)}, bf16[2,1,256,256]{3,2,1,0:T(8,128)(2,1)S(1)}, u32[]{:S(2)}, u32[]{:S(2)}) %collective-permute-start.2) | collective-permute-done | bytes 262176 | tf_op jit(solution)/shard_map/ppermute | solution.py:238
  14.5 0.0 collective-permute-start.9
  14.5 0.0 collective-permute-done.1.note
  14.5 0.0 collective-permute-done
  14.5 0.5 %collective-permute-start.8 = (bf16[512,256]{1,0:T(8,128)(2,1)S(1)}, bf16[512,256]{1,0:T(8,128)(2,1)S(1)}, u32[]{:S(2)}, u32[]{:S(2)}) collective-permute-start(bf16[512,256]{1,0:T(8,128)(2,1)S(1)} %bitcast.2), channel_id=1, source_target_pairs={{0,1},{1,0},{2,3},{3,2},{4,5},{5,4},{6,7},{7,6},{8,9},{9,8},{10,11... | collective-permute-start | bytes 786440 | tf_op jit(solution)/shard_map/ppermute | solution.py:293
  15.0 0.1 collective-permute-start.7
  15.1 0.9 %collective-permute-done.9.other_b = bf16[512,256]{1,0:T(8,128)(2,1)S(1)} collective-permute-done((bf16[512,256]{1,0:T(8,128)(2,1)S(1)}, bf16[512,256]{1,0:T(8,128)(2,1)S(1)}, u32[]{:S(2)}, u32[]{:S(2)}) %collective-permute-start.9) | collective-permute-done | bytes 262176 | tf_op jit(solution)/shard_map/ppermute | solution.py:292
  16.1 0.6 %middle.1 = (f32[512,256]{1,0:T(8,128)S(1)}, f32[512,256]{1,0:T(8,128)S(1)}) custom-call(bf16[2,4,512,256]{3,2,1,0:T(8,128)(2,1)S(1)} %get-tuple-element.29.rim, bf16[512,256]{1,0:T(8,128)(2,1)S(1)} %bitcast.3, bf16[512,256]{1,0:T(8,128)(2,1)S(1)} %bitcast.5, bf16[512,256]{1,0:T(8,128)(2,1)S(1)} %collective-permute-done.9.other_b), custom_call_target="tpu_custom_call" | custom-call | tf_op jit(solution)/shard_map/middle/pallas_call | solution.py:295
  16.7 0.0 collective-permute-done.7.note_other
  16.7 0.0 collective-permute-done.8.other_a
  16.7 1.2 %last.1 = f32[4,1,4,128,256]{4,3,2,1,0:T(8,128)} custom-call(f32[8,256]{1,0:T(8,128)S(1)} %get-tuple-element.20.info_own.info, f32[8,256]{1,0:T(8,128)S(1)} %collective-permute-done.1.note, f32[8,256]{1,0:T(8,128)S(1)} %collective-permute-done.7.note_other, bf16[2,4,512,256]{3,2,1,0:T(8,128)(2,1)S(1)} %get-tuple-element.29.rim, ...), custom_call_target="tpu_custom_call", output_to_operand_aliasing={{}: (7, {})} | custom-call | tf_op jit(solution)/shard_map/last/pallas_call | solution.py:303
Async XLA Ops:
  0.0 14.5 %collective-permute-start.2 = (bf16[2,1,256,256]{3,2,1,0:T(8,128)(2,1)}, bf16[2,1,256,256]{3,2,1,0:T(8,128)(2,1)S(1)}, u32[]{:S(2)}, u32[]{:S(2)}) collective-permute-start(bf16[2,1,256,256]{3,2,1,0:T(8,128)(2,1)} %right.1), channel_id=1, source_target_pairs={{0,2},{1,3},{2,0},{3,1},{4,6},{5,7},{6,4},{7,5},{8,10},{9,11},{10,... | collective-permute-start | bytes 786440 | tf_op jit(solution)/shard_map/ppermute | solution.py:238
  2.9 11.6 %collective-permute-start = (bf16[2,1,256,256]{3,2,1,0:T(8,128)(2,1)}, bf16[2,1,256,256]{3,2,1,0:T(8,128)(2,1)S(1)}, u32[]{:S(2)}, u32[]{:S(2)}) collective-permute-start(bf16[2,1,256,256]{3,2,1,0:T(8,128)(2,1)} %right.1), channel_id=1, source_target_pairs={{0,1},{1,0},{2,4},{3,5},{4,2},{5,3},{6,8},{7,9},{8,6},{9,7},{10,12... | collective-permute-start | bytes 786440 | tf_op jit(solution)/shard_map/ppermute | solution.py:239
  3.6 0.7 %copy-start = (s32[2]{0:T(128)S(1)}, s32[2]{0:T(128)}, u32[]{:S(2)}) copy-start(s32[2]{0:T(128)} %ops.1) | copy-start | bytes 28
  5.4 1.4 %collective-permute-start.3 = (f32[8,256]{1,0:T(8,128)S(1)}, f32[8,256]{1,0:T(8,128)S(1)}, u32[]{:S(2)}, u32[]{:S(2)}) collective-permute-start(f32[8,256]{1,0:T(8,128)S(1)} %get-tuple-element.20.info_own.info), channel_id=1, source_target_pairs={{0,1},{1,0},{2,3},{3,2},{4,5},{5,4},{6,7},{7,6},{8,9},{9,8},{10,11... | collective-permute-start | bytes 24584 | tf_op jit(solution)/shard_map/ppermute | solution.py:244
  6.0 1.3 %collective-permute-start.4 = (bf16[2,128,256]{2,1,0:T(8,128)(2,1)S(1)}, bf16[2,128,256]{2,1,0:T(8,128)(2,1)S(1)}, u32[]{:S(2)}, u32[]{:S(2)}) collective-permute-start(bf16[2,128,256]{2,1,0:T(8,128)(2,1)S(1)} %get-tuple-element.22), channel_id=1, source_target_pairs={{0,1},{1,0},{2,3},{3,2},{4,5},{5,4},{6,7},{7,6},{8,9},{9,8},{10,11... | collective-permute-start | bytes 393224 | tf_op jit(solution)/shard_map/ppermute | solution.py:243
  6.1 3.9 %collective-permute-start.5 = (bf16[256,256]{1,0:T(8,128)(2,1)S(1)}, bf16[256,256]{1,0:T(8,128)(2,1)S(1)}, u32[]{:S(2)}, u32[]{:S(2)}) collective-permute-start(bf16[256,256]{1,0:T(8,128)(2,1)S(1)} %get-tuple-element.23.refs_0_), channel_id=1, source_target_pairs={{0,1},{1,0},{2,3},{3,2},{4,5},{5,4},{6,7},{7,6},{8,9},{9,8},{10,11... | collective-permute-start | bytes 393224 | tf_op jit(solution)/shard_map/ppermute | solution.py:245
  6.8 3.1 %collective-permute-start.6 = (bf16[256,256]{1,0:T(8,128)(2,1)S(1)}, bf16[256,256]{1,0:T(8,128)(2,1)S(1)}, u32[]{:S(2)}, u32[]{:S(2)}) collective-permute-start(bf16[256,256]{1,0:T(8,128)(2,1)S(1)} %get-tuple-element.24.refs_1_), channel_id=1, source_target_pairs={{0,1},{1,0},{2,3},{3,2},{4,5},{5,4},{6,7},{7,6},{8,9},{9,8},{10,11... | collective-permute-start | bytes 393224 | tf_op jit(solution)/shard_map/ppermute | solution.py:245
  7.3 7.2 %collective-permute-start.1 = (f32[8,256]{1,0:T(8,128)S(1)}, f32[8,256]{1,0:T(8,128)S(1)}, u32[]{:S(2)}, u32[]{:S(2)}) collective-permute-start(f32[8,256]{1,0:T(8,128)S(1)} %get-tuple-element.20.info_own.info), channel_id=1, source_target_pairs={{0,2},{2,4},{4,6},{6,8},{8,10},{10,12},{12,14},{14,16},{16,18},{18... | collective-permute-start | bytes 24584 | tf_op jit(solution)/shard_map/ppermute | solution.py:246
  14.5 1.5 %collective-permute-start.9 = (bf16[512,256]{1,0:T(8,128)(2,1)S(1)}, bf16[512,256]{1,0:T(8,128)(2,1)S(1)}, u32[]{:S(2)}, u32[]{:S(2)}) collective-permute-start(bf16[512,256]{1,0:T(8,128)(2,1)S(1)} %bitcast.4), channel_id=1, source_target_pairs={{0,1},{1,0},{2,3},{3,2},{4,5},{5,4},{6,7},{7,6},{8,9},{9,8},{10,11... | collective-permute-start | bytes 786440 | tf_op jit(solution)/shard_map/ppermute | solution.py:292
  14.5 2.1 %collective-permute-start.8 = (bf16[512,256]{1,0:T(8,128)(2,1)S(1)}, bf16[512,256]{1,0:T(8,128)(2,1)S(1)}, u32[]{:S(2)}, u32[]{:S(2)}) collective-permute-start(bf16[512,256]{1,0:T(8,128)(2,1)S(1)} %bitcast.2), channel_id=1, source_target_pairs={{0,1},{1,0},{2,3},{3,2},{4,5},{5,4},{6,7},{7,6},{8,9},{9,8},{10,11... | collective-permute-start | bytes 786440 | tf_op jit(solution)/shard_map/ppermute | solution.py:293
  15.0 1.6 %collective-permute-start.7 = (f32[8,256]{1,0:T(8,128)S(1)}, f32[8,256]{1,0:T(8,128)S(1)}, u32[]{:S(2)}, u32[]{:S(2)}) collective-permute-start(f32[8,256]{1,0:T(8,128)S(1)} %collective-permute-done.1.note), channel_id=1, source_target_pairs={{0,1},{1,0},{2,3},{3,2},{4,5},{5,4},{6,7},{7,6},{8,9},{9,8},{10,11... | collective-permute-start | bytes 24584 | tf_op jit(solution)/shard_map/ppermute | solution.py:294

commit v7 on v6

--- a/solution.py
+++ b/solution.py
@@ -6,6 +6,7 @@
 from jax.sharding import PartitionSpec as P
 
 FLIP = 2
+NOTE = 128
 COEFFICIENTS = (
     (1.0, 1.0, 1.0, 1.0),
     (0.25, -0.25, -0.25, 0.25),
@@ -47,7 +48,7 @@
     return info.astype(jnp.float32)
 
 
-def pack_kernel(kept, ops, left, right, info, mine, theirs, *refs):
+def pack_kernel(kept, ops, left, right, info, note, mine, theirs, *refs):
     *blocks, kept_buf, ops_buf, sems = refs
     terms, half, size = mine.shape
     core = lax.axis_index("term")
@@ -68,6 +69,7 @@
     for copy in scalars:
         copy.wait()
     info[...] = info_of(kept_buf, ops_buf, terms, size)
+    note[...] = info[0:8, 0:NOTE]
     for copy in copies:
         copy.wait()
 
@@ -76,12 +78,13 @@
     terms, size = left.shape[0], left.shape[-1]
     rows = jax.ShapeDtypeStruct((terms, half, size), left.dtype)
     block = jax.ShapeDtypeStruct((size, size), right.dtype)
-    info, mine, theirs, *blocks = pl.pallas_call(
+    info, note, mine, theirs, *blocks = pl.pallas_call(
         pack_kernel,
-        out_shape=(jax.ShapeDtypeStruct((info_rows(terms), size), jnp.float32), rows, rows)
+        out_shape=(jax.ShapeDtypeStruct((info_rows(terms), size), jnp.float32),
+                   jax.ShapeDtypeStruct((8, NOTE), jnp.float32), rows, rows)
         + (block,) * terms,
         in_specs=[HBM] * 4,
-        out_specs=(VMEM,) * (3 + terms),
+        out_specs=(VMEM,) * (4 + terms),
         scratch_shapes=[
             pltpu.SMEM(kept.shape, kept.dtype),
             pltpu.SMEM(ops.shape, ops.dtype),
@@ -90,7 +93,7 @@
         compiler_params=pltpu.CompilerParams(vmem_limit_bytes=PACK_LIMIT),
         name="pack",
     )(kept, ops, left, right)
-    return info, mine, theirs, blocks
+    return info, note, mine, theirs, blocks
 
 
 def centre_kernel(psi, info_own, info_other, left_own, left_other, *refs):
@@ -171,21 +174,27 @@
     return keep & (cols.astype(jnp.float32) < note), jnp.where(is_below, 3, 0)
 
 
-def middle_kernel(rim, own_a, own_b, other_b, part_a, part_b):
-    own, other = own_b.shape[0] // rim.shape[-1], other_b.shape[0] // rim.shape[-1]
-    rows = pl.ds(0, rim.shape[2])
-    part_b[...] = sum_terms(
-        rim, 1, own, other_b, other, rows, sum_terms(rim, 1, 0, own_b, own, rows)
-    )
-    part_a[...] = sum_terms(rim, 0, 0, own_a, own, rows)
+def crossed():
+    return lax.axis_size("term") == 2
+
+
+def own_kernel(rim, own_a, own_b, part_a, part_b):
+    count, rows = own_b.shape[0] // rim.shape[-1], pl.ds(0, rim.shape[2])
+    part_a[...] = sum_terms(rim, 0, count if crossed() else 0, own_a, count, rows)
+    part_b[...] = sum_terms(rim, 1, 0, own_b, count, rows)
+
+
+def other_kernel(rim, other_b, part_in, part_b):
+    count, rows = other_b.shape[0] // rim.shape[-1], pl.ds(0, rim.shape[2])
+    part_b[...] = sum_terms(rim, 1, rim.shape[1] - count, other_b, count, rows, part_in[...])
 
 
 def last_kernel(info, note, note_other, rim, other_a, part_a, part_b, sigma_in, sigma, out_buf, out_sem):
     _, nvec, half, size = out_buf.shape
     count, groups = other_a.shape[0] // size, out_sem.shape[1]
-    first, per_group = rim.shape[1] - count, nvec // groups
+    first, per_group = 0 if crossed() else rim.shape[1] - count, nvec // groups
     direct = (lax.axis_index("term") == 0) == below_is_a() if lax.axis_size("term") == 2 else True
-    notes = note[0:1, :], note_other[0:1, :]
+    notes = [jnp.concatenate([x[0:1, :]] * (size // NOTE), 1) for x in (note, note_other)]
     note_a, note_b = jnp.where(direct, *notes), jnp.where(direct, *notes[::-1])
     stores = []
     for which, note, part in ((1, note_b, part_b), (0, note_a, part_a)):
@@ -215,13 +224,13 @@
     return up + [(2 * sectors - 2, 2 * sectors - 1)] + down + [(1, 0)]
 
 
-def pair_exchange(sectors, first):
+def pair_exchange(sectors, first, cross):
     pairs = []
     for sector in range(sectors):
         low = sector if (sector - first) % 2 == 0 else sector - 1
         alone = low < 0 or low + 1 >= sectors
         for core in range(2):
-            target = 2 * sector + 1 - core if alone else 2 * (2 * low + 1 - sector) + core
+            target = 2 * sector + 1 - core if alone else 2 * (2 * low + 1 - sector) + (core ^ cross)
             pairs.append((2 * sector + core, target))
     return pairs
 
@@ -235,15 +244,15 @@
 
     if cores == 2:
         cycle = two_core_cycle(sectors)
-        own_b = lax.ppermute(right_env, ("sector", "term"), pair_exchange(sectors, 0))
-        own_a = lax.ppermute(right_env, ("sector", "term"), pair_exchange(sectors, 1))
-        info_own, left_own, left_sent, rights = pack(
+        own_b = lax.ppermute(right_env, ("sector", "term"), pair_exchange(sectors, 0, 0))
+        own_a = lax.ppermute(right_env, ("sector", "term"), pair_exchange(sectors, 1, 1))
+        info_own, note, left_own, left_sent, rights = pack(
             kept_rows, op_index, left_env, right_env, half
         )
         left_other = lax.ppermute(left_sent, "term", swap)
         info_other = lax.ppermute(info_own, "term", swap)
         rights += [lax.ppermute(x, "term", swap) for x in rights]
-        note = lax.ppermute(info_own, ("sector", "term"), cycle)
+        note = lax.ppermute(note, ("sector", "term"), cycle)
     else:
         forward = [(i, i + 1) for i in range(sectors - 1)]
         backward = [(b, a) for a, b in forward]
@@ -257,7 +266,7 @@
 
         def neighbour(pairs):
             blocks = lax.all_gather(lax.ppermute(right_env, "sector", pairs), "term", tiled=True)
-            return *jnp.split(blocks, 2), lax.ppermute(info_own, "sector", pairs)
+            return *jnp.split(blocks, 2), lax.ppermute(info_own[0:8, 0:NOTE], "sector", pairs)
 
         own_a, other_a, note = neighbour(forward)
         own_b, other_b, note_other = neighbour(backward)
@@ -293,13 +302,22 @@
         other_a = lax.ppermute(own_a, "term", swap)
         note_other = lax.ppermute(note, "term", swap)
     part_a, part_b = pl.pallas_call(
-        middle_kernel,
+        own_kernel,
         out_shape=(part_shape, part_shape),
-        in_specs=[VMEM] * 4,
+        in_specs=[VMEM] * 3,
         out_specs=(VMEM, VMEM),
         compiler_params=params,
-        name="middle",
-    )(rim, own_a, own_b, other_b.reshape(-1, size))
+        name="own",
+    )(rim, own_a, own_b)
+    part_b = pl.pallas_call(
+        other_kernel,
+        out_shape=part_shape,
+        in_specs=[VMEM] * 3,
+        out_specs=VMEM,
+        input_output_aliases={2: 0},
+        compiler_params=params,
+        name="other",
+    )(rim, other_b.reshape(-1, size), part_b)
     return pl.pallas_call(
         last_kernel,
         out_shape=sigma_shape,

time: 18.2 us -> 17.8 us (0.978)
  waiting for transfers between devices: 1.77 us -> 1.28 us
  Pallas kernels: 7.25 us -> 7.49 us
    ppermute x1, waiting for transfers between devices: 0.94 us -> 0.47 us  [shards(): other_b = lax.ppermute(own_b, 'term', swap)]
    pallas_call x1 -> x2, Pallas kernels: 0.6 us -> 0.87 us  [the longest x1 0.46 us: shards(): pl.pallas_call(own_kernel, out_shape=(part_shape, part_shape), in_specs=[...]
  transfers between devices with their start and end apart: 10 -> 10, of which waited for: 4 -> 4; matrix products, arithmetic and copies ran while one was open for 0% -> 0% of each run, Pallas kernels for 34% -> 35%
where the time goes in v7:
time: 17.8 us; the launch traced here: 17.7 us
  starting transfers between devices  7.54 us (42%)
  Pallas kernels  7.49 us (42%)
  waiting for transfers between devices  1.28 us (7%)
  between operations  0.71 us (4%)
  local copies, waits for them, and re-layouts  0.65 us (4%)
    pallas_call x1, Pallas kernels, shards(): pl.pallas_call(centre_kernel, out_shape=(sigma_shape, rim_shape), in_spec...  4.25 us
    ppermute x1, starting transfers between devices, shards(): lax.ppermute(right_env, ('sector', 'term'), pair_exchange(sectors, 0, 0))  2.94 us
    ppermute x1, starting transfers between devices, shards(): note = lax.ppermute(note, ('sector', 'term'), cycle)  2.59 us
    pallas_call x1, Pallas kernels, shards(): pl.pallas_call(last_kernel, out_shape=sigma_shape, in_specs=[VMEM] * 7 +...  1.23 us
    pallas_call x1, Pallas kernels, pack(): pl.pallas_call(pack_kernel, out_shape=(jax.ShapeDtypeStruct((info_rows(te...  1.15 us
    ppermute x2, starting transfers between devices, shards(): rights += [lax.ppermute(x, 'term', swap) for x in rights]  0.78 us
    unnamed x2, local copies, waits for them, and re-layouts  0.65 us
    ppermute x1, starting transfers between devices, shards(): info_other = lax.ppermute(info_own, 'term', swap)  0.57 us
  transfers between devices with their start and end apart: 10, of which 4 were waited for; matrix products, arithmetic and copies ran while one was open for 0% of the time, Pallas kernels for 35%

profile of v7, /device:TPU:0, one launch (start us, length us, event | category | flops | bytes accessed | tf_op | source)
XLA Modules:
  0.0 17.7 jit_solution(11445457743213162480)
XLA Ops:
  0.0 2.9 %collective-permute-start.2 = (bf16[2,1,256,256]{3,2,1,0:T(8,128)(2,1)}, bf16[2,1,256,256]{3,2,1,0:T(8,128)(2,1)S(1)}, u32[]{:S(2)}, u32[]{:S(2)}) collective-permute-start(bf16[2,1,256,256]{3,2,1,0:T(8,128)(2,1)} %right.1), channel_id=1, source_target_pairs={{0,2},{1,3},{2,0},{3,1},{4,6},{5,7},{6,4},{7,5},{8,10},{9,11},{10,... | collective-permute-start | bytes 786440 | tf_op jit(solution)/shard_map/ppermute | solution.py:247
  2.9 0.0 collective-permute-start
  3.6 0.0 copy-start
  3.6 0.6 %copy-done = s32[2]{0:T(128)S(1)} copy-done((s32[2]{0:T(128)S(1)}, s32[2]{0:T(128)}, u32[]{:S(2)}) %copy-start) | copy-done | bytes 32
  4.3 1.1 %pack.1 = (f32[8,256]{1,0:T(8,128)S(1)}, f32[8,128]{1,0:T(8,128)S(1)}, bf16[2,128,256]{2,1,0:T(8,128)(2,1)S(1)}, bf16[2,128,256]{2,1,0:T(8,128)(2,1)S(1)}, bf16[...) custom-call(s32[1]{0:T(128)S(6)} %copy.10.kept, s32[2]{0:T(128)S(1)} %copy-done, bf16[2,1,256,256]{3,2,1,0:T(8,128)(2,1)} %left.1, ...), custom_call_target="tpu_custom_call" | custom-call | tf_op jit(solution)/shard_map/pack/pallas_call | solution.py:81
  5.4 0.6 %collective-permute-start.3 = (f32[8,256]{1,0:T(8,128)S(1)}, f32[8,256]{1,0:T(8,128)S(1)}, u32[]{:S(2)}, u32[]{:S(2)}) collective-permute-start(f32[8,256]{1,0:T(8,128)S(1)} %get-tuple-element.21.info_own.info), channel_id=1, source_target_pairs={{0,1},{1,0},{2,3},{3,2},{4,5},{5,4},{6,7},{7,6},{8,9},{9,8},{10,11... | collective-permute-start | bytes 24584 | tf_op jit(solution)/shard_map/ppermute | solution.py:253
  6.0 0.1 collective-permute-start.4
  6.1 0.4 %collective-permute-start.5 = (bf16[256,256]{1,0:T(8,128)(2,1)S(1)}, bf16[256,256]{1,0:T(8,128)(2,1)S(1)}, u32[]{:S(2)}, u32[]{:S(2)}) collective-permute-start(bf16[256,256]{1,0:T(8,128)(2,1)S(1)} %get-tuple-element.25.refs_0_), channel_id=1, source_target_pairs={{0,1},{1,0},{2,3},{3,2},{4,5},{5,4},{6,7},{7,6},{8,9},{9,8},{10,11... | collective-permute-start | bytes 393224 | tf_op jit(solution)/shard_map/ppermute | solution.py:254
  6.5 0.3 %collective-permute-done.3.info_other = f32[8,256]{1,0:T(8,128)S(1)} collective-permute-done((f32[8,256]{1,0:T(8,128)S(1)}, f32[8,256]{1,0:T(8,128)S(1)}, u32[]{:S(2)}, u32[]{:S(2)}) %collective-permute-start.3) | collective-permute-done | bytes 8224 | tf_op jit(solution)/shard_map/ppermute | solution.py:253
  6.8 0.3 %collective-permute-start.6 = (bf16[256,256]{1,0:T(8,128)(2,1)S(1)}, bf16[256,256]{1,0:T(8,128)(2,1)S(1)}, u32[]{:S(2)}, u32[]{:S(2)}) collective-permute-start(bf16[256,256]{1,0:T(8,128)(2,1)S(1)} %get-tuple-element.26.refs_1_), channel_id=1, source_target_pairs={{0,1},{1,0},{2,3},{3,2},{4,5},{5,4},{6,7},{7,6},{8,9},{9,8},{10,11... | collective-permute-start | bytes 393224 | tf_op jit(solution)/shard_map/ppermute | solution.py:254
  7.2 0.2 collective-permute-done.4.left_other
  7.3 2.6 %collective-permute-start.1 = (f32[8,128]{1,0:T(8,128)S(1)}, f32[8,128]{1,0:T(8,128)S(1)}, u32[]{:S(2)}, u32[]{:S(2)}) collective-permute-start(f32[8,128]{1,0:T(8,128)S(1)} %get-tuple-element.22), channel_id=1, source_target_pairs={{0,2},{2,4},{4,6},{6,8},{8,10},{10,12},{12,14},{14,16},{16,18},{18... | collective-permute-start | bytes 12296 | tf_op jit(solution)/shard_map/ppermute | solution.py:255
  9.9 0.0 collective-permute-done.5.refs_2_
  9.9 0.0 collective-permute-done.6.refs_3_
  9.9 4.3 %centre.1 = (f32[4,1,4,128,256]{4,3,2,1,0:T(8,128)}, bf16[2,4,512,256]{3,2,1,0:T(8,128)(2,1)S(1)}) custom-call(bf16[4,1,4,256,256]{4,3,2,1,0:T(8,128)(2,1)} %psi.1, f32[8,256]{1,0:T(8,128)S(1)} %get-tuple-element.21.info_own.info, f32[8,256]{1,0:T(8,128)S(1)} %collective-permute-done.3.info_other, bf16[2,128,256]{2,1,0:T(8,128)(2,1)S(1)} %get-tuple-element.23.left_own, ...), custom_call_target="tpu_custom_call" | custom-call | tf_op jit(solution)/shard_map/centre/pallas_call | solution.py:280
  14.2 0.3 %collective-permute-done.2 = bf16[2,1,256,256]{3,2,1,0:T(8,128)(2,1)S(1)} collective-permute-done((bf16[2,1,256,256]{3,2,1,0:T(8,128)(2,1)}, bf16[2,1,256,256]{3,2,1,0:T(8,128)(2,1)S(1)}, u32[]{:S(2)}, u32[]{:S(2)}) %collective-permute-start.2) | collective-permute-done | bytes 262176 | tf_op jit(solution)/shard_map/ppermute | solution.py:247
  14.5 0.0 collective-permute-start.9
  14.5 0.0 collective-permute-done.1.note
  14.5 0.0 collective-permute-done
  14.5 0.5 %collective-permute-start.8 = (bf16[512,256]{1,0:T(8,128)(2,1)S(1)}, bf16[512,256]{1,0:T(8,128)(2,1)S(1)}, u32[]{:S(2)}, u32[]{:S(2)}) collective-permute-start(bf16[512,256]{1,0:T(8,128)(2,1)S(1)} %bitcast.2), channel_id=1, source_target_pairs={{0,1},{1,0},{2,3},{3,2},{4,5},{5,4},{6,7},{7,6},{8,9},{9,8},{10,11... | collective-permute-start | bytes 786440 | tf_op jit(solution)/shard_map/ppermute | solution.py:302
  15.0 0.1 collective-permute-start.7
  15.1 0.5 %own.1 = (f32[512,256]{1,0:T(8,128)S(1)}, f32[512,256]{1,0:T(8,128)S(1)}) custom-call(bf16[2,4,512,256]{3,2,1,0:T(8,128)(2,1)S(1)} %get-tuple-element.31.rim, bf16[512,256]{1,0:T(8,128)(2,1)S(1)} %bitcast.3, bf16[512,256]{1,0:T(8,128)(2,1)S(1)} %bitcast.5), custom_call_target="tpu_custom_call" | custom-call | tf_op jit(solution)/shard_map/own/pallas_call | solution.py:304
  15.5 0.5 %collective-permute-done.9.other_b = bf16[512,256]{1,0:T(8,128)(2,1)S(1)} collective-permute-done((bf16[512,256]{1,0:T(8,128)(2,1)S(1)}, bf16[512,256]{1,0:T(8,128)(2,1)S(1)}, u32[]{:S(2)}, u32[]{:S(2)}) %collective-permute-start.9) | collective-permute-done | bytes 262176 | tf_op jit(solution)/shard_map/ppermute | solution.py:301
  16.0 0.4 %other.1.part_b = f32[512,256]{1,0:T(8,128)S(1)} custom-call(bf16[2,4,512,256]{3,2,1,0:T(8,128)(2,1)S(1)} %get-tuple-element.31.rim, bf16[512,256]{1,0:T(8,128)(2,1)S(1)} %collective-permute-done.9.other_b, f32[512,256]{1,0:T(8,128)S(1)} %get-tuple-element.35.part_in), custom_call_target="tpu_custom_call", output_to_operand_aliasing={{}: (2, {})} | custom-call | tf_op jit(solution)/shard_map/other/pallas_call | solution.py:312
  16.4 0.0 collective-permute-done.7.note_other
  16.4 0.0 collective-permute-done.8.other_a
  16.4 1.2 %last.1 = f32[4,1,4,128,256]{4,3,2,1,0:T(8,128)} custom-call(f32[8,256]{1,0:T(8,128)S(1)} %get-tuple-element.21.info_own.info, f32[8,128]{1,0:T(8,128)S(1)} %collective-permute-done.1.note, f32[8,128]{1,0:T(8,128)S(1)} %collective-permute-done.7.note_other, bf16[2,4,512,256]{3,2,1,0:T(8,128)(2,1)S(1)} %get-tuple-element.31.rim, ...), custom_call_target="tpu_custom_call", output_to_operand_aliasing={{}: (7, {})} | custom-call | tf_op jit(solution)/shard_map/last/pallas_call | solution.py:321
Async XLA Ops:
  0.0 14.5 %collective-permute-start.2 = (bf16[2,1,256,256]{3,2,1,0:T(8,128)(2,1)}, bf16[2,1,256,256]{3,2,1,0:T(8,128)(2,1)S(1)}, u32[]{:S(2)}, u32[]{:S(2)}) collective-permute-start(bf16[2,1,256,256]{3,2,1,0:T(8,128)(2,1)} %right.1), channel_id=1, source_target_pairs={{0,2},{1,3},{2,0},{3,1},{4,6},{5,7},{6,4},{7,5},{8,10},{9,11},{10,... | collective-permute-start | bytes 786440 | tf_op jit(solution)/shard_map/ppermute | solution.py:247
  2.9 11.6 %collective-permute-start = (bf16[2,1,256,256]{3,2,1,0:T(8,128)(2,1)}, bf16[2,1,256,256]{3,2,1,0:T(8,128)(2,1)S(1)}, u32[]{:S(2)}, u32[]{:S(2)}) collective-permute-start(bf16[2,1,256,256]{3,2,1,0:T(8,128)(2,1)} %right.1), channel_id=1, source_target_pairs={{0,1},{1,0},{2,5},{3,4},{4,3},{5,2},{6,9},{7,8},{8,7},{9,6},{10,13... | collective-permute-start | bytes 786440 | tf_op jit(solution)/shard_map/ppermute | solution.py:248
  3.6 0.7 %copy-start = (s32[2]{0:T(128)S(1)}, s32[2]{0:T(128)}, u32[]{:S(2)}) copy-start(s32[2]{0:T(128)} %ops.1) | copy-start | bytes 28
  5.4 1.4 %collective-permute-start.3 = (f32[8,256]{1,0:T(8,128)S(1)}, f32[8,256]{1,0:T(8,128)S(1)}, u32[]{:S(2)}, u32[]{:S(2)}) collective-permute-start(f32[8,256]{1,0:T(8,128)S(1)} %get-tuple-element.21.info_own.info), channel_id=1, source_target_pairs={{0,1},{1,0},{2,3},{3,2},{4,5},{5,4},{6,7},{7,6},{8,9},{9,8},{10,11... | collective-permute-start | bytes 24584 | tf_op jit(solution)/shard_map/ppermute | solution.py:253
  6.0 1.3 %collective-permute-start.4 = (bf16[2,128,256]{2,1,0:T(8,128)(2,1)S(1)}, bf16[2,128,256]{2,1,0:T(8,128)(2,1)S(1)}, u32[]{:S(2)}, u32[]{:S(2)}) collective-permute-start(bf16[2,128,256]{2,1,0:T(8,128)(2,1)S(1)} %get-tuple-element.24), channel_id=1, source_target_pairs={{0,1},{1,0},{2,3},{3,2},{4,5},{5,4},{6,7},{7,6},{8,9},{9,8},{10,11... | collective-permute-start | bytes 393224 | tf_op jit(solution)/shard_map/ppermute | solution.py:252
  6.1 3.9 %collective-permute-start.5 = (bf16[256,256]{1,0:T(8,128)(2,1)S(1)}, bf16[256,256]{1,0:T(8,128)(2,1)S(1)}, u32[]{:S(2)}, u32[]{:S(2)}) collective-permute-start(bf16[256,256]{1,0:T(8,128)(2,1)S(1)} %get-tuple-element.25.refs_0_), channel_id=1, source_target_pairs={{0,1},{1,0},{2,3},{3,2},{4,5},{5,4},{6,7},{7,6},{8,9},{9,8},{10,11... | collective-permute-start | bytes 393224 | tf_op jit(solution)/shard_map/ppermute | solution.py:254
  6.8 3.1 %collective-permute-start.6 = (bf16[256,256]{1,0:T(8,128)(2,1)S(1)}, bf16[256,256]{1,0:T(8,128)(2,1)S(1)}, u32[]{:S(2)}, u32[]{:S(2)}) collective-permute-start(bf16[256,256]{1,0:T(8,128)(2,1)S(1)} %get-tuple-element.26.refs_1_), channel_id=1, source_target_pairs={{0,1},{1,0},{2,3},{3,2},{4,5},{5,4},{6,7},{7,6},{8,9},{9,8},{10,11... | collective-permute-start | bytes 393224 | tf_op jit(solution)/shard_map/ppermute | solution.py:254
  7.3 7.2 %collective-permute-start.1 = (f32[8,128]{1,0:T(8,128)S(1)}, f32[8,128]{1,0:T(8,128)S(1)}, u32[]{:S(2)}, u32[]{:S(2)}) collective-permute-start(f32[8,128]{1,0:T(8,128)S(1)} %get-tuple-element.22), channel_id=1, source_target_pairs={{0,2},{2,4},{4,6},{6,8},{8,10},{10,12},{12,14},{14,16},{16,18},{18... | collective-permute-start | bytes 12296 | tf_op jit(solution)/shard_map/ppermute | solution.py:255
  14.5 1.5 %collective-permute-start.9 = (bf16[512,256]{1,0:T(8,128)(2,1)S(1)}, bf16[512,256]{1,0:T(8,128)(2,1)S(1)}, u32[]{:S(2)}, u32[]{:S(2)}) collective-permute-start(bf16[512,256]{1,0:T(8,128)(2,1)S(1)} %bitcast.4), channel_id=1, source_target_pairs={{0,1},{1,0},{2,3},{3,2},{4,5},{5,4},{6,7},{7,6},{8,9},{9,8},{10,11... | collective-permute-start | bytes 786440 | tf_op jit(solution)/shard_map/ppermute | solution.py:301
  14.5 1.9 %collective-permute-start.8 = (bf16[512,256]{1,0:T(8,128)(2,1)S(1)}, bf16[512,256]{1,0:T(8,128)(2,1)S(1)}, u32[]{:S(2)}, u32[]{:S(2)}) collective-permute-start(bf16[512,256]{1,0:T(8,128)(2,1)S(1)} %bitcast.2), channel_id=1, source_target_pairs={{0,1},{1,0},{2,3},{3,2},{4,5},{5,4},{6,7},{7,6},{8,9},{9,8},{10,11... | collective-permute-start | bytes 786440 | tf_op jit(solution)/shard_map/ppermute | solution.py:302
  15.0 1.4 %collective-permute-start.7 = (f32[8,128]{1,0:T(8,128)S(1)}, f32[8,128]{1,0:T(8,128)S(1)}, u32[]{:S(2)}, u32[]{:S(2)}) collective-permute-start(f32[8,128]{1,0:T(8,128)S(1)} %collective-permute-done.1.note), channel_id=1, source_target_pairs={{0,1},{1,0},{2,3},{3,2},{4,5},{5,4},{6,7},{7,6},{8,9},{9,8},{10,11... | collective-permute-start | bytes 12296 | tf_op jit(solution)/shard_map/ppermute | solution.py:303

commit v8 on v7

--- a/solution.py
+++ b/solution.py
@@ -37,11 +37,11 @@
 
 
 def info_rows(terms):
-    return 8 * pl.cdiv(1 + terms, 8)
-
-
-def info_of(kept, ops, terms, size):
-    rows = lax.broadcasted_iota(jnp.int32, (info_rows(terms), size), 0)
+    return 16 * pl.cdiv(1 + terms, 16)
+
+
+def info_of(kept, ops, terms, size, count):
+    rows = lax.broadcasted_iota(jnp.int32, (count, size), 0)
     info = jnp.where(rows == 0, kept[0], 0)
     for t in range(terms):
         info = jnp.where(rows == 1 + t, ops[t], info)
@@ -56,19 +56,23 @@
         pltpu.make_async_copy(kept, kept_buf, sems.at[0]),
         pltpu.make_async_copy(ops, ops_buf, sems.at[1]),
     ]
-    copies = [
-        pltpu.make_async_copy(
-            left.at[:, 0, pl.ds(pl.multiple_of(who * half, half), half)], rows, sems.at[2 + k]
+    first = [pl.multiple_of(who * half, half) for who in (core, 1 - core)]
+    copies = [pltpu.make_async_copy(left.at[:, 0, pl.ds(first[0], half)], mine, sems.at[2])]
+    for t, block in enumerate(blocks):
+        copies.append(
+            pltpu.make_async_copy(
+                left.at[t, 0, pl.ds(first[1], half)],
+                theirs.at[pl.ds(t * half, half)],
+                sems.at[3 + 2 * t],
+            )
         )
-        for k, (who, rows) in enumerate(((core, mine), (1 - core, theirs)))
-    ]
-    for t, block in enumerate(blocks):
-        copies.append(pltpu.make_async_copy(right.at[t, 0], block, sems.at[4 + t]))
+        copies.append(pltpu.make_async_copy(right.at[t, 0], block, sems.at[4 + 2 * t]))
     for copy in scalars + copies:
         copy.start()
     for copy in scalars:
         copy.wait()
-    info[...] = info_of(kept_buf, ops_buf, terms, size)
+    info[...] = info_of(kept_buf, ops_buf, terms, size, info.shape[0])
+    theirs[terms * half:] = info[...].astype(theirs.dtype)
     note[...] = info[0:8, 0:NOTE]
     for copy in copies:
         copy.wait()
@@ -77,18 +81,19 @@
 def pack(kept, ops, left, right, half):
     terms, size = left.shape[0], left.shape[-1]
     rows = jax.ShapeDtypeStruct((terms, half, size), left.dtype)
+    theirs = jax.ShapeDtypeStruct((terms * half + info_rows(terms), size), left.dtype)
     block = jax.ShapeDtypeStruct((size, size), right.dtype)
     info, note, mine, theirs, *blocks = pl.pallas_call(
         pack_kernel,
         out_shape=(jax.ShapeDtypeStruct((info_rows(terms), size), jnp.float32),
-                   jax.ShapeDtypeStruct((8, NOTE), jnp.float32), rows, rows)
+                   jax.ShapeDtypeStruct((8, NOTE), jnp.float32), rows, theirs)
         + (block,) * terms,
         in_specs=[HBM] * 4,
         out_specs=(VMEM,) * (4 + terms),
         scratch_shapes=[
             pltpu.SMEM(kept.shape, kept.dtype),
             pltpu.SMEM(ops.shape, ops.dtype),
-            pltpu.SemaphoreType.DMA((4 + terms,)),
+            pltpu.SemaphoreType.DMA((3 + 2 * terms,)),
         ],
         compiler_params=pltpu.CompilerParams(vmem_limit_bytes=PACK_LIMIT),
         name="pack",
@@ -96,16 +101,18 @@
     return info, note, mine, theirs, blocks
 
 
-def centre_kernel(psi, info_own, info_other, left_own, left_other, *refs):
+def centre_kernel(psi, info_own, left_own, left_other, *refs):
     (*rights, sigma, rim, psi_buf, lefts, centre, out_buf, psi_sem, out_sem) = refs
     nvec, half, size = psi.shape[0], sigma.shape[3], psi.shape[4]
     own, terms = left_own.shape[0], len(rights)
     loads = [pltpu.make_async_copy(psi.at[v, 0], psi_buf.at[v], psi_sem.at[v]) for v in range(nvec)]
     for copy in loads:
         copy.start()
-    for t in range(terms):
-        source, k = (left_own, t) if t < own else (left_other, t - own)
-        lefts[pl.ds(t * half, half), :] = source[k]
+    for t in range(own):
+        lefts[pl.ds(t * half, half), :] = left_own[t]
+    others = (terms - own) * half
+    lefts[pl.ds(own * half, others), :] = left_other[:others]
+    info_other = left_other[others:].astype(jnp.float32)
     slot_of_3 = jnp.where(below_is_a(), 0, 1)
     ops = [info_own[1 + t:2 + t] if t < own else info_other[1 + t - own:2 + t - own]
            for t in range(terms)]
@@ -250,7 +257,6 @@
             kept_rows, op_index, left_env, right_env, half
         )
         left_other = lax.ppermute(left_sent, "term", swap)
-        info_other = lax.ppermute(info_own, "term", swap)
         rights += [lax.ppermute(x, "term", swap) for x in rights]
         note = lax.ppermute(note, ("sector", "term"), cycle)
     else:
@@ -260,8 +266,12 @@
         rows = lax.dynamic_slice_in_dim(gathered[0][:, 0], lax.axis_index("term") * half, half, 1)
         left_own, left_other = jnp.split(rows, 2)
         info_own, info_other = [
-            info_of(kept_rows, ops, terms // 2, size) for ops in jnp.split(gathered[2], 2)
+            info_of(kept_rows, ops, terms // 2, size, info_rows(terms // 2))
+            for ops in jnp.split(gathered[2], 2)
         ]
+        left_other = jnp.concatenate(
+            [left_other.reshape(-1, size), info_other.astype(left_other.dtype)], 0
+        )
         rights = list(gathered[1][:, 0])
 
         def neighbour(pairs):
@@ -280,7 +290,7 @@
     sigma, rim = pl.pallas_call(
         centre_kernel,
         out_shape=(sigma_shape, rim_shape),
-        in_specs=[HBM] + [VMEM] * (4 + terms),
+        in_specs=[HBM] + [VMEM] * (3 + terms),
         out_specs=(HBM, VMEM),
         scratch_shapes=[
             pltpu.VMEM((nvec, 4, size, size), jnp.bfloat16),
@@ -292,7 +302,7 @@
         ],
         compiler_params=pltpu.CompilerParams(vmem_limit_bytes=CENTRE_LIMIT),
         name="centre",
-    )(psi, info_own, info_other, left_own, left_other, *rights)
+    )(psi, info_own, left_own, left_other, *rights)
 
     own_a, own_b = own_a.reshape(-1, size), own_b.reshape(-1, size)
     own_b, sigma, rim = lax.optimization_barrier((own_b, sigma, rim))
@@ -325,7 +335,7 @@
         out_specs=HBM,
         scratch_shapes=[
             pltpu.VMEM((2, nvec, half, size), jnp.float32),
-            pltpu.SemaphoreType.DMA((2, groups)),
+            pltpu.SemaphoreType.DMA((2, 1)),
         ],
         input_output_aliases={7: 0},
         compiler_params=params,

time: 17.8 us -> 17.8 us (level)
  starting transfers between devices: 7.54 us -> 7.19 us
  waiting for transfers between devices: 1.28 us -> 1.61 us
    ppermute x2, waiting for transfers between devices: 0.01 us -> 0.84 us  [shards(): rights += [lax.ppermute(x, 'term', swap) for x in rights]]
    ppermute x1 -> x0, starting transfers between devices: 0.57 us -> none  [shards(): info_other = lax.ppermute(info_own, 'term', swap)]
    ppermute x1, starting transfers between devices: 0.08 us -> 0.57 us  [shards(): left_other = lax.ppermute(left_sent, 'term', swap)]
    ppermute x1 -> x0, waiting for transfers between devices: 0.32 us -> none  [shards(): info_other = lax.ppermute(info_own, 'term', swap)]
    ppermute x2, starting transfers between devices: 0.78 us -> 0.51 us  [shards(): rights += [lax.ppermute(x, 'term', swap) for x in rights]]
  transfers between devices with their start and end apart: 10 -> 9, of which waited for: 4 -> 3; matrix products, arithmetic and copies ran while one was open for 0% -> 0% of each run, Pallas kernels for 35% -> 36%
where the time goes in v8:
time: 17.8 us; the launch traced here: 17.6 us
  Pallas kernels  7.47 us (42%)
  starting transfers between devices  7.19 us (40%)
  waiting for transfers between devices  1.61 us (9%)
  between operations  0.71 us (4%)
  local copies, waits for them, and re-layouts  0.65 us (4%)
    pallas_call x1, Pallas kernels, shards(): pl.pallas_call(centre_kernel, out_shape=(sigma_shape, rim_shape), in_spec...  4.26 us
    ppermute x1, starting transfers between devices, shards(): lax.ppermute(right_env, ('sector', 'term'), pair_exchange(sectors, 0, 0))  2.94 us
    ppermute x1, starting transfers between devices, shards(): note = lax.ppermute(note, ('sector', 'term'), cycle)  2.59 us
    pallas_call x1, Pallas kernels, shards(): pl.pallas_call(last_kernel, out_shape=sigma_shape, in_specs=[VMEM] * 7 +...  1.19 us
    pallas_call x1, Pallas kernels, pack(): pl.pallas_call(pack_kernel, out_shape=(jax.ShapeDtypeStruct((info_rows(te...  1.16 us
    ppermute x2, waiting for transfers between devices, shards(): rights += [lax.ppermute(x, 'term', swap) for x in rights]  0.84 us
    unnamed x2, local copies, waits for them, and re-layouts  0.65 us
    ppermute x1, starting transfers between devices, shards(): left_other = lax.ppermute(left_sent, 'term', swap)  0.57 us
  transfers between devices with their start and end apart: 9, of which 3 were waited for; matrix products, arithmetic and copies ran while one was open for 0% of the time, Pallas kernels for 36%

profile of v8, /device:TPU:0, one launch (start us, length us, event | category | flops | bytes accessed | tf_op | source)
XLA Modules:
  0.0 17.6 jit_solution(14742283050264591250)
XLA Ops:
  0.0 2.9 %collective-permute-start.2 = (bf16[2,1,256,256]{3,2,1,0:T(8,128)(2,1)}, bf16[2,1,256,256]{3,2,1,0:T(8,128)(2,1)S(1)}, u32[]{:S(2)}, u32[]{:S(2)}) collective-permute-start(bf16[2,1,256,256]{3,2,1,0:T(8,128)(2,1)} %right.1), channel_id=1, source_target_pairs={{0,2},{1,3},{2,0},{3,1},{4,6},{5,7},{6,4},{7,5},{8,10},{9,11},{10,... | collective-permute-start | bytes 786440 | tf_op jit(solution)/shard_map/ppermute | solution.py:254
  2.9 0.0 collective-permute-start
  3.6 0.0 copy-start
  3.6 0.6 %copy-done = s32[2]{0:T(128)S(1)} copy-done((s32[2]{0:T(128)S(1)}, s32[2]{0:T(128)}, u32[]{:S(2)}) %copy-start) | copy-done | bytes 32
  4.3 1.2 %pack.1 = (f32[16,256]{1,0:T(8,128)S(1)}, f32[8,128]{1,0:T(8,128)S(1)}, bf16[2,128,256]{2,1,0:T(8,128)(2,1)S(1)}, bf16[272,256]{1,0:T(8,128)(2,1)S(1)}, bf16[256...) custom-call(s32[1]{0:T(128)S(6)} %copy.10.kept, s32[2]{0:T(128)S(1)} %copy-done, bf16[2,1,256,256]{3,2,1,0:T(8,128)(2,1)} %left.1, ...), custom_call_target="tpu_custom_call" | custom-call | tf_op jit(solution)/shard_map/pack/pallas_call | solution.py:86
  5.4 0.6 %collective-permute-start.3 = (bf16[272,256]{1,0:T(8,128)(2,1)S(1)}, bf16[272,256]{1,0:T(8,128)(2,1)S(1)}, u32[]{:S(2)}, u32[]{:S(2)}) collective-permute-start(bf16[272,256]{1,0:T(8,128)(2,1)S(1)} %get-tuple-element.24), channel_id=1, source_target_pairs={{0,1},{1,0},{2,3},{3,2},{4,5},{5,4},{6,7},{7,6},{8,9},{9,8},{10,11... | collective-permute-start | bytes 417800 | tf_op jit(solution)/shard_map/ppermute | solution.py:259
  6.0 0.1 collective-permute-start.4
  6.1 0.4 %collective-permute-start.5 = (bf16[256,256]{1,0:T(8,128)(2,1)S(1)}, bf16[256,256]{1,0:T(8,128)(2,1)S(1)}, u32[]{:S(2)}, u32[]{:S(2)}) collective-permute-start(bf16[256,256]{1,0:T(8,128)(2,1)S(1)} %get-tuple-element.26.refs_1_), channel_id=1, source_target_pairs={{0,1},{1,0},{2,3},{3,2},{4,5},{5,4},{6,7},{7,6},{8,9},{9,8},{10,11... | collective-permute-start | bytes 393224 | tf_op jit(solution)/shard_map/ppermute | solution.py:260
  6.5 0.8 %collective-permute-done.4.refs_2_ = bf16[256,256]{1,0:T(8,128)(2,1)S(1)} collective-permute-done((bf16[256,256]{1,0:T(8,128)(2,1)S(1)}, bf16[256,256]{1,0:T(8,128)(2,1)S(1)}, u32[]{:S(2)}, u32[]{:S(2)}) %collective-permute-start.4) | collective-permute-done | bytes 131104 | tf_op jit(solution)/shard_map/ppermute | solution.py:260
  7.3 2.6 %collective-permute-start.1 = (f32[8,128]{1,0:T(8,128)S(1)}, f32[8,128]{1,0:T(8,128)S(1)}, u32[]{:S(2)}, u32[]{:S(2)}) collective-permute-start(f32[8,128]{1,0:T(8,128)S(1)} %get-tuple-element.22), channel_id=1, source_target_pairs={{0,2},{2,4},{4,6},{6,8},{8,10},{10,12},{12,14},{14,16},{16,18},{18... | collective-permute-start | bytes 12296 | tf_op jit(solution)/shard_map/ppermute | solution.py:261
  9.9 0.0 collective-permute-done.5.refs_3_
  9.9 0.0 collective-permute-done.3.left_other
  9.9 4.3 %centre.1 = (f32[4,1,4,128,256]{4,3,2,1,0:T(8,128)}, bf16[2,4,512,256]{3,2,1,0:T(8,128)(2,1)S(1)}) custom-call(bf16[4,1,4,256,256]{4,3,2,1,0:T(8,128)(2,1)} %psi.1, f32[16,256]{1,0:T(8,128)S(1)} %get-tuple-element.21.info_own.info, bf16[2,128,256]{2,1,0:T(8,128)(2,1)S(1)} %get-tuple-element.23.left_own, ...), custom_call_target="tpu_custom_call" | custom-call | tf_op jit(solution)/shard_map/centre/pallas_call | solution.py:290
  14.2 0.3 %collective-permute-done.2 = bf16[2,1,256,256]{3,2,1,0:T(8,128)(2,1)S(1)} collective-permute-done((bf16[2,1,256,256]{3,2,1,0:T(8,128)(2,1)}, bf16[2,1,256,256]{3,2,1,0:T(8,128)(2,1)S(1)}, u32[]{:S(2)}, u32[]{:S(2)}) %collective-permute-start.2) | collective-permute-done | bytes 262176 | tf_op jit(solution)/shard_map/ppermute | solution.py:254
  14.5 0.0 collective-permute-start.8
  14.5 0.0 collective-permute-done.1.note
  14.5 0.0 collective-permute-done
  14.5 0.5 %collective-permute-start.7 = (bf16[512,256]{1,0:T(8,128)(2,1)S(1)}, bf16[512,256]{1,0:T(8,128)(2,1)S(1)}, u32[]{:S(2)}, u32[]{:S(2)}) collective-permute-start(bf16[512,256]{1,0:T(8,128)(2,1)S(1)} %bitcast.2), channel_id=1, source_target_pairs={{0,1},{1,0},{2,3},{3,2},{4,5},{5,4},{6,7},{7,6},{8,9},{9,8},{10,11... | collective-permute-start | bytes 786440 | tf_op jit(solution)/shard_map/ppermute | solution.py:312
  15.0 0.1 collective-permute-start.6
  15.1 0.5 %own.1 = (f32[512,256]{1,0:T(8,128)S(1)}, f32[512,256]{1,0:T(8,128)S(1)}) custom-call(bf16[2,4,512,256]{3,2,1,0:T(8,128)(2,1)S(1)} %get-tuple-element.31.rim, bf16[512,256]{1,0:T(8,128)(2,1)S(1)} %bitcast.3, bf16[512,256]{1,0:T(8,128)(2,1)S(1)} %bitcast.5), custom_call_target="tpu_custom_call" | custom-call | tf_op jit(solution)/shard_map/own/pallas_call | solution.py:314
  15.5 0.5 %collective-permute-done.8.other_b = bf16[512,256]{1,0:T(8,128)(2,1)S(1)} collective-permute-done((bf16[512,256]{1,0:T(8,128)(2,1)S(1)}, bf16[512,256]{1,0:T(8,128)(2,1)S(1)}, u32[]{:S(2)}, u32[]{:S(2)}) %collective-permute-start.8) | collective-permute-done | bytes 262176 | tf_op jit(solution)/shard_map/ppermute | solution.py:311
  16.0 0.4 %other.1.part_b = f32[512,256]{1,0:T(8,128)S(1)} custom-call(bf16[2,4,512,256]{3,2,1,0:T(8,128)(2,1)S(1)} %get-tuple-element.31.rim, bf16[512,256]{1,0:T(8,128)(2,1)S(1)} %collective-permute-done.8.other_b, f32[512,256]{1,0:T(8,128)S(1)} %get-tuple-element.35.part_in), custom_call_target="tpu_custom_call", output_to_operand_aliasing={{}: (2, {})} | custom-call | tf_op jit(solution)/shard_map/other/pallas_call | solution.py:322
  16.4 0.0 collective-permute-done.6.note_other
  16.4 0.0 collective-permute-done.7.other_a
  16.4 1.2 %last.1 = f32[4,1,4,128,256]{4,3,2,1,0:T(8,128)} custom-call(f32[16,256]{1,0:T(8,128)S(1)} %get-tuple-element.21.info_own.info, f32[8,128]{1,0:T(8,128)S(1)} %collective-permute-done.1.note, f32[8,128]{1,0:T(8,128)S(1)} %collective-permute-done.6.note_other, bf16[2,4,512,256]{3,2,1,0:T(8,128)(2,1)S(1)} %get-tuple-element.31.rim, ...), custom_call_target="tpu_custom_call", output_to_operand_aliasing={{}: (7, {})} | custom-call | tf_op jit(solution)/shard_map/last/pallas_call | solution.py:331
Async XLA Ops:
  0.0 14.5 %collective-permute-start.2 = (bf16[2,1,256,256]{3,2,1,0:T(8,128)(2,1)}, bf16[2,1,256,256]{3,2,1,0:T(8,128)(2,1)S(1)}, u32[]{:S(2)}, u32[]{:S(2)}) collective-permute-start(bf16[2,1,256,256]{3,2,1,0:T(8,128)(2,1)} %right.1), channel_id=1, source_target_pairs={{0,2},{1,3},{2,0},{3,1},{4,6},{5,7},{6,4},{7,5},{8,10},{9,11},{10,... | collective-permute-start | bytes 786440 | tf_op jit(solution)/shard_map/ppermute | solution.py:254
  2.9 11.6 %collective-permute-start = (bf16[2,1,256,256]{3,2,1,0:T(8,128)(2,1)}, bf16[2,1,256,256]{3,2,1,0:T(8,128)(2,1)S(1)}, u32[]{:S(2)}, u32[]{:S(2)}) collective-permute-start(bf16[2,1,256,256]{3,2,1,0:T(8,128)(2,1)} %right.1), channel_id=1, source_target_pairs={{0,1},{1,0},{2,5},{3,4},{4,3},{5,2},{6,9},{7,8},{8,7},{9,6},{10,13... | collective-permute-start | bytes 786440 | tf_op jit(solution)/shard_map/ppermute | solution.py:255
  3.6 0.7 %copy-start = (s32[2]{0:T(128)S(1)}, s32[2]{0:T(128)}, u32[]{:S(2)}) copy-start(s32[2]{0:T(128)} %ops.1) | copy-start | bytes 28
  5.4 4.5 %collective-permute-start.3 = (bf16[272,256]{1,0:T(8,128)(2,1)S(1)}, bf16[272,256]{1,0:T(8,128)(2,1)S(1)}, u32[]{:S(2)}, u32[]{:S(2)}) collective-permute-start(bf16[272,256]{1,0:T(8,128)(2,1)S(1)} %get-tuple-element.24), channel_id=1, source_target_pairs={{0,1},{1,0},{2,3},{3,2},{4,5},{5,4},{6,7},{7,6},{8,9},{9,8},{10,11... | collective-permute-start | bytes 417800 | tf_op jit(solution)/shard_map/ppermute | solution.py:259
  6.0 1.3 %collective-permute-start.4 = (bf16[256,256]{1,0:T(8,128)(2,1)S(1)}, bf16[256,256]{1,0:T(8,128)(2,1)S(1)}, u32[]{:S(2)}, u32[]{:S(2)}) collective-permute-start(bf16[256,256]{1,0:T(8,128)(2,1)S(1)} %get-tuple-element.25.refs_0_), channel_id=1, source_target_pairs={{0,1},{1,0},{2,3},{3,2},{4,5},{5,4},{6,7},{7,6},{8,9},{9,8},{10,11... | collective-permute-start | bytes 393224 | tf_op jit(solution)/shard_map/ppermute | solution.py:260
  6.1 3.9 %collective-permute-start.5 = (bf16[256,256]{1,0:T(8,128)(2,1)S(1)}, bf16[256,256]{1,0:T(8,128)(2,1)S(1)}, u32[]{:S(2)}, u32[]{:S(2)}) collective-permute-start(bf16[256,256]{1,0:T(8,128)(2,1)S(1)} %get-tuple-element.26.refs_1_), channel_id=1, source_target_pairs={{0,1},{1,0},{2,3},{3,2},{4,5},{5,4},{6,7},{7,6},{8,9},{9,8},{10,11... | collective-permute-start | bytes 393224 | tf_op jit(solution)/shard_map/ppermute | solution.py:260
  7.3 7.2 %collective-permute-start.1 = (f32[8,128]{1,0:T(8,128)S(1)}, f32[8,128]{1,0:T(8,128)S(1)}, u32[]{:S(2)}, u32[]{:S(2)}) collective-permute-start(f32[8,128]{1,0:T(8,128)S(1)} %get-tuple-element.22), channel_id=1, source_target_pairs={{0,2},{2,4},{4,6},{6,8},{8,10},{10,12},{12,14},{14,16},{16,18},{18... | collective-permute-start | bytes 12296 | tf_op jit(solution)/shard_map/ppermute | solution.py:261
  14.5 1.5 %collective-permute-start.8 = (bf16[512,256]{1,0:T(8,128)(2,1)S(1)}, bf16[512,256]{1,0:T(8,128)(2,1)S(1)}, u32[]{:S(2)}, u32[]{:S(2)}) collective-permute-start(bf16[512,256]{1,0:T(8,128)(2,1)S(1)} %bitcast.4), channel_id=1, source_target_pairs={{0,1},{1,0},{2,3},{3,2},{4,5},{5,4},{6,7},{7,6},{8,9},{9,8},{10,11... | collective-permute-start | bytes 786440 | tf_op jit(solution)/shard_map/ppermute | solution.py:311
  14.5 1.9 %collective-permute-start.7 = (bf16[512,256]{1,0:T(8,128)(2,1)S(1)}, bf16[512,256]{1,0:T(8,128)(2,1)S(1)}, u32[]{:S(2)}, u32[]{:S(2)}) collective-permute-start(bf16[512,256]{1,0:T(8,128)(2,1)S(1)} %bitcast.2), channel_id=1, source_target_pairs={{0,1},{1,0},{2,3},{3,2},{4,5},{5,4},{6,7},{7,6},{8,9},{9,8},{10,11... | collective-permute-start | bytes 786440 | tf_op jit(solution)/shard_map/ppermute | solution.py:312
  15.0 1.4 %collective-permute-start.6 = (f32[8,128]{1,0:T(8,128)S(1)}, f32[8,128]{1,0:T(8,128)S(1)}, u32[]{:S(2)}, u32[]{:S(2)}) collective-permute-start(f32[8,128]{1,0:T(8,128)S(1)} %collective-permute-done.1.note), channel_id=1, source_target_pairs={{0,1},{1,0},{2,3},{3,2},{4,5},{5,4},{6,7},{7,6},{8,9},{9,8},{10,11... | collective-permute-start | bytes 12296 | tf_op jit(solution)/shard_map/ppermute | solution.py:313

commit v9 on v8

--- a/solution.py
+++ b/solution.py
@@ -306,7 +306,8 @@
 
     own_a, own_b = own_a.reshape(-1, size), own_b.reshape(-1, size)
     own_b, sigma, rim = lax.optimization_barrier((own_b, sigma, rim))
-    own_a, note, sigma = lax.optimization_barrier((own_a, note, sigma))
+    note, sigma = lax.optimization_barrier((note, sigma))
+    own_a, sigma = lax.optimization_barrier((own_a, sigma))
     if cores == 2:
         other_b = lax.ppermute(own_b, "term", swap)
         other_a = lax.ppermute(own_a, "term", swap)

time: 17.8 us -> 17.8 us (level)
  no operation moved by 1% of the time
where the time goes in v9:
time: 17.8 us; the launch traced here: 17.6 us
  Pallas kernels  7.47 us (42%)
  starting transfers between devices  7.19 us (40%)
  waiting for transfers between devices  1.62 us (9%)
  between operations  0.71 us (4%)
  local copies, waits for them, and re-layouts  0.65 us (4%)
    pallas_call x1, Pallas kernels, shards(): pl.pallas_call(centre_kernel, out_shape=(sigma_shape, rim_shape), in_spec...  4.26 us
    ppermute x1, starting transfers between devices, shards(): lax.ppermute(right_env, ('sector', 'term'), pair_exchange(sectors, 0, 0))  2.94 us
    ppermute x1, starting transfers between devices, shards(): note = lax.ppermute(note, ('sector', 'term'), cycle)  2.59 us
    pallas_call x1, Pallas kernels, shards(): pl.pallas_call(last_kernel, out_shape=sigma_shape, in_specs=[VMEM] * 7 +...  1.19 us
    pallas_call x1, Pallas kernels, pack(): pl.pallas_call(pack_kernel, out_shape=(jax.ShapeDtypeStruct((info_rows(te...  1.16 us
    ppermute x2, waiting for transfers between devices, shards(): rights += [lax.ppermute(x, 'term', swap) for x in rights]  0.84 us
    unnamed x2, local copies, waits for them, and re-layouts  0.65 us
    ppermute x1, starting transfers between devices, shards(): left_other = lax.ppermute(left_sent, 'term', swap)  0.57 us
  transfers between devices with their start and end apart: 9, of which 3 were waited for; matrix products, arithmetic and copies ran while one was open for 0% of the time, Pallas kernels for 36%

profile of v9, /device:TPU:0, one launch (start us, length us, event | category | flops | bytes accessed | tf_op | source)
XLA Modules:
  0.0 17.6 jit_solution(6640696141931498836)
XLA Ops:
  0.0 2.9 %collective-permute-start.1 = (bf16[2,1,256,256]{3,2,1,0:T(8,128)(2,1)}, bf16[2,1,256,256]{3,2,1,0:T(8,128)(2,1)S(1)}, u32[]{:S(2)}, u32[]{:S(2)}) collective-permute-start(bf16[2,1,256,256]{3,2,1,0:T(8,128)(2,1)} %right.1), channel_id=1, source_target_pairs={{0,2},{1,3},{2,0},{3,1},{4,6},{5,7},{6,4},{7,5},{8,10},{9,11},{10,... | collective-permute-start | bytes 786440 | tf_op jit(solution)/shard_map/ppermute | solution.py:254
  2.9 0.0 collective-permute-start.6
  3.6 0.0 copy-start
  3.6 0.6 %copy-done = s32[2]{0:T(128)S(1)} copy-done((s32[2]{0:T(128)S(1)}, s32[2]{0:T(128)}, u32[]{:S(2)}) %copy-start) | copy-done | bytes 32
  4.3 1.2 %pack.1 = (f32[16,256]{1,0:T(8,128)S(1)}, f32[8,128]{1,0:T(8,128)S(1)}, bf16[2,128,256]{2,1,0:T(8,128)(2,1)S(1)}, bf16[272,256]{1,0:T(8,128)(2,1)S(1)}, bf16[256...) custom-call(s32[1]{0:T(128)S(6)} %copy.10.kept, s32[2]{0:T(128)S(1)} %copy-done, bf16[2,1,256,256]{3,2,1,0:T(8,128)(2,1)} %left.1, ...), custom_call_target="tpu_custom_call" | custom-call | tf_op jit(solution)/shard_map/pack/pallas_call | solution.py:86
  5.4 0.6 %collective-permute-start.2 = (bf16[272,256]{1,0:T(8,128)(2,1)S(1)}, bf16[272,256]{1,0:T(8,128)(2,1)S(1)}, u32[]{:S(2)}, u32[]{:S(2)}) collective-permute-start(bf16[272,256]{1,0:T(8,128)(2,1)S(1)} %get-tuple-element.25), channel_id=1, source_target_pairs={{0,1},{1,0},{2,3},{3,2},{4,5},{5,4},{6,7},{7,6},{8,9},{9,8},{10,11... | collective-permute-start | bytes 417800 | tf_op jit(solution)/shard_map/ppermute | solution.py:259
  6.0 0.1 collective-permute-start.3
  6.1 0.4 %collective-permute-start.4 = (bf16[256,256]{1,0:T(8,128)(2,1)S(1)}, bf16[256,256]{1,0:T(8,128)(2,1)S(1)}, u32[]{:S(2)}, u32[]{:S(2)}) collective-permute-start(bf16[256,256]{1,0:T(8,128)(2,1)S(1)} %get-tuple-element.27.refs_1_), channel_id=1, source_target_pairs={{0,1},{1,0},{2,3},{3,2},{4,5},{5,4},{6,7},{7,6},{8,9},{9,8},{10,11... | collective-permute-start | bytes 393224 | tf_op jit(solution)/shard_map/ppermute | solution.py:260
  6.5 0.8 %collective-permute-done.3.refs_2_ = bf16[256,256]{1,0:T(8,128)(2,1)S(1)} collective-permute-done((bf16[256,256]{1,0:T(8,128)(2,1)S(1)}, bf16[256,256]{1,0:T(8,128)(2,1)S(1)}, u32[]{:S(2)}, u32[]{:S(2)}) %collective-permute-start.3) | collective-permute-done | bytes 131104 | tf_op jit(solution)/shard_map/ppermute | solution.py:260
  7.3 2.6 %collective-permute-start = (f32[8,128]{1,0:T(8,128)S(1)}, f32[8,128]{1,0:T(8,128)S(1)}, u32[]{:S(2)}, u32[]{:S(2)}) collective-permute-start(f32[8,128]{1,0:T(8,128)S(1)} %get-tuple-element.23), channel_id=1, source_target_pairs={{0,2},{2,4},{4,6},{6,8},{8,10},{10,12},{12,14},{14,16},{16,18},{18... | collective-permute-start | bytes 12296 | tf_op jit(solution)/shard_map/ppermute | solution.py:261
  9.9 0.0 collective-permute-done.4.refs_3_
  9.9 0.0 collective-permute-done.2.left_other
  9.9 4.3 %centre.1 = (f32[4,1,4,128,256]{4,3,2,1,0:T(8,128)}, bf16[2,4,512,256]{3,2,1,0:T(8,128)(2,1)S(1)}) custom-call(bf16[4,1,4,256,256]{4,3,2,1,0:T(8,128)(2,1)} %psi.1, f32[16,256]{1,0:T(8,128)S(1)} %get-tuple-element.22.info_own.info, bf16[2,128,256]{2,1,0:T(8,128)(2,1)S(1)} %get-tuple-element.24.left_own, ...), custom_call_target="tpu_custom_call" | custom-call | tf_op jit(solution)/shard_map/centre/pallas_call | solution.py:290
  14.2 0.3 %collective-permute-done.1 = bf16[2,1,256,256]{3,2,1,0:T(8,128)(2,1)S(1)} collective-permute-done((bf16[2,1,256,256]{3,2,1,0:T(8,128)(2,1)}, bf16[2,1,256,256]{3,2,1,0:T(8,128)(2,1)S(1)}, u32[]{:S(2)}, u32[]{:S(2)}) %collective-permute-start.1) | collective-permute-done | bytes 262176 | tf_op jit(solution)/shard_map/ppermute | solution.py:254
  14.5 0.0 collective-permute-done.note
  14.5 0.0 collective-permute-start.8
  14.5 0.0 collective-permute-done.6
  14.5 0.5 %collective-permute-start.7 = (bf16[512,256]{1,0:T(8,128)(2,1)S(1)}, bf16[512,256]{1,0:T(8,128)(2,1)S(1)}, u32[]{:S(2)}, u32[]{:S(2)}) collective-permute-start(bf16[512,256]{1,0:T(8,128)(2,1)S(1)} %bitcast.2), channel_id=1, source_target_pairs={{0,1},{1,0},{2,3},{3,2},{4,5},{5,4},{6,7},{7,6},{8,9},{9,8},{10,11... | collective-permute-start | bytes 786440 | tf_op jit(solution)/shard_map/ppermute | solution.py:313
  15.0 0.1 collective-permute-start.5
  15.1 0.5 %own.1 = (f32[512,256]{1,0:T(8,128)S(1)}, f32[512,256]{1,0:T(8,128)S(1)}) custom-call(bf16[2,4,512,256]{3,2,1,0:T(8,128)(2,1)S(1)} %get-tuple-element.32.rim, bf16[512,256]{1,0:T(8,128)(2,1)S(1)} %bitcast.3, bf16[512,256]{1,0:T(8,128)(2,1)S(1)} %bitcast.5), custom_call_target="tpu_custom_call" | custom-call | tf_op jit(solution)/shard_map/own/pallas_call | solution.py:315
  15.5 0.5 %collective-permute-done.8.other_b = bf16[512,256]{1,0:T(8,128)(2,1)S(1)} collective-permute-done((bf16[512,256]{1,0:T(8,128)(2,1)S(1)}, bf16[512,256]{1,0:T(8,128)(2,1)S(1)}, u32[]{:S(2)}, u32[]{:S(2)}) %collective-permute-start.8) | collective-permute-done | bytes 262176 | tf_op jit(solution)/shard_map/ppermute | solution.py:312
  16.0 0.4 %other.1.part_b = f32[512,256]{1,0:T(8,128)S(1)} custom-call(bf16[2,4,512,256]{3,2,1,0:T(8,128)(2,1)S(1)} %get-tuple-element.32.rim, bf16[512,256]{1,0:T(8,128)(2,1)S(1)} %collective-permute-done.8.other_b, f32[512,256]{1,0:T(8,128)S(1)} %get-tuple-element.37.part_in), custom_call_target="tpu_custom_call", output_to_operand_aliasing={{}: (2, {})} | custom-call | tf_op jit(solution)/shard_map/other/pallas_call | solution.py:323
  16.4 0.0 collective-permute-done.5.note_other
  16.4 0.0 collective-permute-done.7.other_a
  16.4 1.2 %last.1 = f32[4,1,4,128,256]{4,3,2,1,0:T(8,128)} custom-call(f32[16,256]{1,0:T(8,128)S(1)} %get-tuple-element.22.info_own.info, f32[8,128]{1,0:T(8,128)S(1)} %collective-permute-done.note, f32[8,128]{1,0:T(8,128)S(1)} %collective-permute-done.5.note_other, bf16[2,4,512,256]{3,2,1,0:T(8,128)(2,1)S(1)} %get-tuple-element.32.rim, ...), custom_call_target="tpu_custom_call", output_to_operand_aliasing={{}: (7, {})} | custom-call | tf_op jit(solution)/shard_map/last/pallas_call | solution.py:332
Async XLA Ops:
  0.0 14.5 %collective-permute-start.1 = (bf16[2,1,256,256]{3,2,1,0:T(8,128)(2,1)}, bf16[2,1,256,256]{3,2,1,0:T(8,128)(2,1)S(1)}, u32[]{:S(2)}, u32[]{:S(2)}) collective-permute-start(bf16[2,1,256,256]{3,2,1,0:T(8,128)(2,1)} %right.1), channel_id=1, source_target_pairs={{0,2},{1,3},{2,0},{3,1},{4,6},{5,7},{6,4},{7,5},{8,10},{9,11},{10,... | collective-permute-start | bytes 786440 | tf_op jit(solution)/shard_map/ppermute | solution.py:254
  2.9 11.6 %collective-permute-start.6 = (bf16[2,1,256,256]{3,2,1,0:T(8,128)(2,1)}, bf16[2,1,256,256]{3,2,1,0:T(8,128)(2,1)S(1)}, u32[]{:S(2)}, u32[]{:S(2)}) collective-permute-start(bf16[2,1,256,256]{3,2,1,0:T(8,128)(2,1)} %right.1), channel_id=1, source_target_pairs={{0,1},{1,0},{2,5},{3,4},{4,3},{5,2},{6,9},{7,8},{8,7},{9,6},{10,13... | collective-permute-start | bytes 786440 | tf_op jit(solution)/shard_map/ppermute | solution.py:255
  3.6 0.7 %copy-start = (s32[2]{0:T(128)S(1)}, s32[2]{0:T(128)}, u32[]{:S(2)}) copy-start(s32[2]{0:T(128)} %ops.1) | copy-start | bytes 28
  5.4 4.5 %collective-permute-start.2 = (bf16[272,256]{1,0:T(8,128)(2,1)S(1)}, bf16[272,256]{1,0:T(8,128)(2,1)S(1)}, u32[]{:S(2)}, u32[]{:S(2)}) collective-permute-start(bf16[272,256]{1,0:T(8,128)(2,1)S(1)} %get-tuple-element.25), channel_id=1, source_target_pairs={{0,1},{1,0},{2,3},{3,2},{4,5},{5,4},{6,7},{7,6},{8,9},{9,8},{10,11... | collective-permute-start | bytes 417800 | tf_op jit(solution)/shard_map/ppermute | solution.py:259
  6.0 1.3 %collective-permute-start.3 = (bf16[256,256]{1,0:T(8,128)(2,1)S(1)}, bf16[256,256]{1,0:T(8,128)(2,1)S(1)}, u32[]{:S(2)}, u32[]{:S(2)}) collective-permute-start(bf16[256,256]{1,0:T(8,128)(2,1)S(1)} %get-tuple-element.26.refs_0_), channel_id=1, source_target_pairs={{0,1},{1,0},{2,3},{3,2},{4,5},{5,4},{6,7},{7,6},{8,9},{9,8},{10,11... | collective-permute-start | bytes 393224 | tf_op jit(solution)/shard_map/ppermute | solution.py:260
  6.1 3.9 %collective-permute-start.4 = (bf16[256,256]{1,0:T(8,128)(2,1)S(1)}, bf16[256,256]{1,0:T(8,128)(2,1)S(1)}, u32[]{:S(2)}, u32[]{:S(2)}) collective-permute-start(bf16[256,256]{1,0:T(8,128)(2,1)S(1)} %get-tuple-element.27.refs_1_), channel_id=1, source_target_pairs={{0,1},{1,0},{2,3},{3,2},{4,5},{5,4},{6,7},{7,6},{8,9},{9,8},{10,11... | collective-permute-start | bytes 393224 | tf_op jit(solution)/shard_map/ppermute | solution.py:260
  7.3 7.1 %collective-permute-start = (f32[8,128]{1,0:T(8,128)S(1)}, f32[8,128]{1,0:T(8,128)S(1)}, u32[]{:S(2)}, u32[]{:S(2)}) collective-permute-start(f32[8,128]{1,0:T(8,128)S(1)} %get-tuple-element.23), channel_id=1, source_target_pairs={{0,2},{2,4},{4,6},{6,8},{8,10},{10,12},{12,14},{14,16},{16,18},{18... | collective-permute-start | bytes 12296 | tf_op jit(solution)/shard_map/ppermute | solution.py:261
  14.5 1.5 %collective-permute-start.8 = (bf16[512,256]{1,0:T(8,128)(2,1)S(1)}, bf16[512,256]{1,0:T(8,128)(2,1)S(1)}, u32[]{:S(2)}, u32[]{:S(2)}) collective-permute-start(bf16[512,256]{1,0:T(8,128)(2,1)S(1)} %bitcast.4), channel_id=1, source_target_pairs={{0,1},{1,0},{2,3},{3,2},{4,5},{5,4},{6,7},{7,6},{8,9},{9,8},{10,11... | collective-permute-start | bytes 786440 | tf_op jit(solution)/shard_map/ppermute | solution.py:312
  14.5 1.9 %collective-permute-start.7 = (bf16[512,256]{1,0:T(8,128)(2,1)S(1)}, bf16[512,256]{1,0:T(8,128)(2,1)S(1)}, u32[]{:S(2)}, u32[]{:S(2)}) collective-permute-start(bf16[512,256]{1,0:T(8,128)(2,1)S(1)} %bitcast.2), channel_id=1, source_target_pairs={{0,1},{1,0},{2,3},{3,2},{4,5},{5,4},{6,7},{7,6},{8,9},{9,8},{10,11... | collective-permute-start | bytes 786440 | tf_op jit(solution)/shard_map/ppermute | solution.py:313
  15.0 1.4 %collective-permute-start.5 = (f32[8,128]{1,0:T(8,128)S(1)}, f32[8,128]{1,0:T(8,128)S(1)}, u32[]{:S(2)}, u32[]{:S(2)}) collective-permute-start(f32[8,128]{1,0:T(8,128)S(1)} %collective-permute-done.note), channel_id=1, source_target_pairs={{0,1},{1,0},{2,3},{3,2},{4,5},{5,4},{6,7},{7,6},{8,9},{9,8},{10,11... | collective-permute-start | bytes 12296 | tf_op jit(solution)/shard_map/ppermute | solution.py:314

commit v10 on v8

--- a/solution.py
+++ b/solution.py
@@ -191,12 +191,13 @@
     part_b[...] = sum_terms(rim, 1, 0, own_b, count, rows)
 
 
-def other_kernel(rim, other_b, part_in, part_b):
+def other_kernel(rim, other_b, part_c):
     count, rows = other_b.shape[0] // rim.shape[-1], pl.ds(0, rim.shape[2])
-    part_b[...] = sum_terms(rim, 1, rim.shape[1] - count, other_b, count, rows, part_in[...])
-
-
-def last_kernel(info, note, note_other, rim, other_a, part_a, part_b, sigma_in, sigma, out_buf, out_sem):
+    part_c[...] = sum_terms(rim, 1, rim.shape[1] - count, other_b, count, rows)
+
+
+def last_kernel(info, note, note_other, rim, other_a, part_a, part_b, part_c, sigma_in, sigma, out_buf,
+                out_sem):
     _, nvec, half, size = out_buf.shape
     count, groups = other_a.shape[0] // size, out_sem.shape[1]
     first, per_group = 0 if crossed() else rim.shape[1] - count, nvec // groups
@@ -211,6 +212,8 @@
             total = part[rows, :]
             if which == 0:
                 total = sum_terms(rim, 0, first, other_a, count, rows, total)
+            else:
+                total = total + part_c[rows, :]
             for j in range(per_group):
                 out_buf[which, group * per_group + j] = jnp.where(
                     keep, total[j * half:(j + 1) * half], 0.0
@@ -319,28 +322,27 @@
         compiler_params=params,
         name="own",
     )(rim, own_a, own_b)
-    part_b = pl.pallas_call(
+    part_c = pl.pallas_call(
         other_kernel,
         out_shape=part_shape,
-        in_specs=[VMEM] * 3,
+        in_specs=[VMEM] * 2,
         out_specs=VMEM,
-        input_output_aliases={2: 0},
         compiler_params=params,
         name="other",
-    )(rim, other_b.reshape(-1, size), part_b)
+    )(rim, other_b.reshape(-1, size))
     return pl.pallas_call(
         last_kernel,
         out_shape=sigma_shape,
-        in_specs=[VMEM] * 7 + [HBM],
+        in_specs=[VMEM] * 8 + [HBM],
         out_specs=HBM,
         scratch_shapes=[
             pltpu.VMEM((2, nvec, half, size), jnp.float32),
             pltpu.SemaphoreType.DMA((2, 1)),
         ],
-        input_output_aliases={7: 0},
+        input_output_aliases={8: 0},
         compiler_params=params,
         name="last",
-    )(info_own, note, note_other, rim, other_a.reshape(-1, size), part_a, part_b, sigma)
+    )(info_own, note, note_other, rim, other_a.reshape(-1, size), part_a, part_b, part_c, sigma)
 
 
 def solution(mesh):

time: 17.8 us -> 17.8 us (level)
  transfers between devices with their start and end apart: 9 -> 9, of which waited for: 3 -> 3; matrix products, arithmetic and copies ran while one was open for 0% -> 0% of each run, Pallas kernels for 36% -> 35%
where the time goes in v10:
time: 17.8 us; the launch traced here: 17.6 us
  Pallas kernels  7.44 us (42%)
  starting transfers between devices  7.19 us (40%)
  waiting for transfers between devices  1.65 us (9%)
  between operations  0.7 us (4%)
  local copies, waits for them, and re-layouts  0.65 us (4%)
    pallas_call x1, Pallas kernels, shards(): pl.pallas_call(centre_kernel, out_shape=(sigma_shape, rim_shape), in_spec...  4.26 us
    ppermute x1, starting transfers between devices, shards(): lax.ppermute(right_env, ('sector', 'term'), pair_exchange(sectors, 0, 0))  2.94 us
    ppermute x1, starting transfers between devices, shards(): note = lax.ppermute(note, ('sector', 'term'), cycle)  2.59 us
    pallas_call x1, Pallas kernels, shards(): pl.pallas_call(last_kernel, out_shape=sigma_shape, in_specs=[VMEM] * 8 +...  1.23 us
    pallas_call x1, Pallas kernels, pack(): pl.pallas_call(pack_kernel, out_shape=(jax.ShapeDtypeStruct((info_rows(te...  1.16 us
    ppermute x2, waiting for transfers between devices, shards(): rights += [lax.ppermute(x, 'term', swap) for x in rights]  0.84 us
    unnamed x2, local copies, waits for them, and re-layouts  0.65 us
    ppermute x1, starting transfers between devices, shards(): left_other = lax.ppermute(left_sent, 'term', swap)  0.57 us
  transfers between devices with their start and end apart: 9, of which 3 were waited for; matrix products, arithmetic and copies ran while one was open for 0% of the time, Pallas kernels for 35%

profile of v10, /device:TPU:0, one launch (start us, length us, event | category | flops | bytes accessed | tf_op | source)
XLA Modules:
  0.0 17.6 jit_solution(6651426024278988114)
XLA Ops:
  0.0 2.9 %collective-permute-start.2 = (bf16[2,1,256,256]{3,2,1,0:T(8,128)(2,1)}, bf16[2,1,256,256]{3,2,1,0:T(8,128)(2,1)S(1)}, u32[]{:S(2)}, u32[]{:S(2)}) collective-permute-start(bf16[2,1,256,256]{3,2,1,0:T(8,128)(2,1)} %right.1), channel_id=1, source_target_pairs={{0,2},{1,3},{2,0},{3,1},{4,6},{5,7},{6,4},{7,5},{8,10},{9,11},{10,... | collective-permute-start | bytes 786440 | tf_op jit(solution)/shard_map/ppermute | solution.py:257
  2.9 0.0 collective-permute-start
  3.6 0.0 copy-start
  3.6 0.6 %copy-done = s32[2]{0:T(128)S(1)} copy-done((s32[2]{0:T(128)S(1)}, s32[2]{0:T(128)}, u32[]{:S(2)}) %copy-start) | copy-done | bytes 32
  4.3 1.2 %pack.1 = (f32[16,256]{1,0:T(8,128)S(1)}, f32[8,128]{1,0:T(8,128)S(1)}, bf16[2,128,256]{2,1,0:T(8,128)(2,1)S(1)}, bf16[272,256]{1,0:T(8,128)(2,1)S(1)}, bf16[256...) custom-call(s32[1]{0:T(128)S(6)} %copy.8.kept, s32[2]{0:T(128)S(1)} %copy-done, bf16[2,1,256,256]{3,2,1,0:T(8,128)(2,1)} %left.1, ...), custom_call_target="tpu_custom_call" | custom-call | tf_op jit(solution)/shard_map/pack/pallas_call | solution.py:86
  5.4 0.6 %collective-permute-start.3 = (bf16[272,256]{1,0:T(8,128)(2,1)S(1)}, bf16[272,256]{1,0:T(8,128)(2,1)S(1)}, u32[]{:S(2)}, u32[]{:S(2)}) collective-permute-start(bf16[272,256]{1,0:T(8,128)(2,1)S(1)} %get-tuple-element.24), channel_id=1, source_target_pairs={{0,1},{1,0},{2,3},{3,2},{4,5},{5,4},{6,7},{7,6},{8,9},{9,8},{10,11... | collective-permute-start | bytes 417800 | tf_op jit(solution)/shard_map/ppermute | solution.py:262
  6.0 0.1 collective-permute-start.4
  6.1 0.4 %collective-permute-start.5 = (bf16[256,256]{1,0:T(8,128)(2,1)S(1)}, bf16[256,256]{1,0:T(8,128)(2,1)S(1)}, u32[]{:S(2)}, u32[]{:S(2)}) collective-permute-start(bf16[256,256]{1,0:T(8,128)(2,1)S(1)} %get-tuple-element.26.refs_1_), channel_id=1, source_target_pairs={{0,1},{1,0},{2,3},{3,2},{4,5},{5,4},{6,7},{7,6},{8,9},{9,8},{10,11... | collective-permute-start | bytes 393224 | tf_op jit(solution)/shard_map/ppermute | solution.py:263
  6.5 0.8 %collective-permute-done.4.refs_2_ = bf16[256,256]{1,0:T(8,128)(2,1)S(1)} collective-permute-done((bf16[256,256]{1,0:T(8,128)(2,1)S(1)}, bf16[256,256]{1,0:T(8,128)(2,1)S(1)}, u32[]{:S(2)}, u32[]{:S(2)}) %collective-permute-start.4) | collective-permute-done | bytes 131104 | tf_op jit(solution)/shard_map/ppermute | solution.py:263
  7.3 2.6 %collective-permute-start.1 = (f32[8,128]{1,0:T(8,128)S(1)}, f32[8,128]{1,0:T(8,128)S(1)}, u32[]{:S(2)}, u32[]{:S(2)}) collective-permute-start(f32[8,128]{1,0:T(8,128)S(1)} %get-tuple-element.22), channel_id=1, source_target_pairs={{0,2},{2,4},{4,6},{6,8},{8,10},{10,12},{12,14},{14,16},{16,18},{18... | collective-permute-start | bytes 12296 | tf_op jit(solution)/shard_map/ppermute | solution.py:264
  9.9 0.0 collective-permute-done.5.refs_3_
  9.9 0.0 collective-permute-done.3.left_other
  9.9 4.3 %centre.1 = (f32[4,1,4,128,256]{4,3,2,1,0:T(8,128)}, bf16[2,4,512,256]{3,2,1,0:T(8,128)(2,1)S(1)}) custom-call(bf16[4,1,4,256,256]{4,3,2,1,0:T(8,128)(2,1)} %psi.1, f32[16,256]{1,0:T(8,128)S(1)} %get-tuple-element.21.info_own.info, bf16[2,128,256]{2,1,0:T(8,128)(2,1)S(1)} %get-tuple-element.23.left_own, ...), custom_call_target="tpu_custom_call" | custom-call | tf_op jit(solution)/shard_map/centre/pallas_call | solution.py:293
  14.2 0.3 %collective-permute-done.2 = bf16[2,1,256,256]{3,2,1,0:T(8,128)(2,1)S(1)} collective-permute-done((bf16[2,1,256,256]{3,2,1,0:T(8,128)(2,1)}, bf16[2,1,256,256]{3,2,1,0:T(8,128)(2,1)S(1)}, u32[]{:S(2)}, u32[]{:S(2)}) %collective-permute-start.2) | collective-permute-done | bytes 262176 | tf_op jit(solution)/shard_map/ppermute | solution.py:257
  14.5 0.0 collective-permute-start.8
  14.5 0.0 collective-permute-done.1.note
  14.5 0.0 collective-permute-done
  14.5 0.5 %collective-permute-start.7 = (bf16[512,256]{1,0:T(8,128)(2,1)S(1)}, bf16[512,256]{1,0:T(8,128)(2,1)S(1)}, u32[]{:S(2)}, u32[]{:S(2)}) collective-permute-start(bf16[512,256]{1,0:T(8,128)(2,1)S(1)} %bitcast.2), channel_id=1, source_target_pairs={{0,1},{1,0},{2,3},{3,2},{4,5},{5,4},{6,7},{7,6},{8,9},{9,8},{10,11... | collective-permute-start | bytes 786440 | tf_op jit(solution)/shard_map/ppermute | solution.py:315
  15.0 0.1 collective-permute-start.6
  15.1 0.5 %own.1 = (f32[512,256]{1,0:T(8,128)S(1)}, f32[512,256]{1,0:T(8,128)S(1)}) custom-call(bf16[2,4,512,256]{3,2,1,0:T(8,128)(2,1)S(1)} %get-tuple-element.31.rim, bf16[512,256]{1,0:T(8,128)(2,1)S(1)} %bitcast.3, bf16[512,256]{1,0:T(8,128)(2,1)S(1)} %bitcast.5), custom_call_target="tpu_custom_call" | custom-call | tf_op jit(solution)/shard_map/own/pallas_call | solution.py:317
  15.5 0.5 %collective-permute-done.8.other_b = bf16[512,256]{1,0:T(8,128)(2,1)S(1)} collective-permute-done((bf16[512,256]{1,0:T(8,128)(2,1)S(1)}, bf16[512,256]{1,0:T(8,128)(2,1)S(1)}, u32[]{:S(2)}, u32[]{:S(2)}) %collective-permute-start.8) | collective-permute-done | bytes 262176 | tf_op jit(solution)/shard_map/ppermute | solution.py:314
  16.0 0.3 %other.1.part_c = f32[512,256]{1,0:T(8,128)S(1)} custom-call(bf16[2,4,512,256]{3,2,1,0:T(8,128)(2,1)S(1)} %get-tuple-element.31.rim, bf16[512,256]{1,0:T(8,128)(2,1)S(1)} %collective-permute-done.8.other_b), custom_call_target="tpu_custom_call" | custom-call | tf_op jit(solution)/shard_map/other/pallas_call | solution.py:325
  16.4 0.0 collective-permute-done.6.note_other
  16.4 0.0 collective-permute-done.7.other_a
  16.4 1.2 %last.1 = f32[4,1,4,128,256]{4,3,2,1,0:T(8,128)} custom-call(f32[16,256]{1,0:T(8,128)S(1)} %get-tuple-element.21.info_own.info, f32[8,128]{1,0:T(8,128)S(1)} %collective-permute-done.1.note, f32[8,128]{1,0:T(8,128)S(1)} %collective-permute-done.6.note_other, bf16[2,4,512,256]{3,2,1,0:T(8,128)(2,1)S(1)} %get-tuple-element.31.rim, ...), custom_call_target="tpu_custom_call", output_to_operand_aliasing={{}: (8, {})} | custom-call | tf_op jit(solution)/shard_map/last/pallas_call | solution.py:333
Async XLA Ops:
  0.0 14.5 %collective-permute-start.2 = (bf16[2,1,256,256]{3,2,1,0:T(8,128)(2,1)}, bf16[2,1,256,256]{3,2,1,0:T(8,128)(2,1)S(1)}, u32[]{:S(2)}, u32[]{:S(2)}) collective-permute-start(bf16[2,1,256,256]{3,2,1,0:T(8,128)(2,1)} %right.1), channel_id=1, source_target_pairs={{0,2},{1,3},{2,0},{3,1},{4,6},{5,7},{6,4},{7,5},{8,10},{9,11},{10,... | collective-permute-start | bytes 786440 | tf_op jit(solution)/shard_map/ppermute | solution.py:257
  2.9 11.6 %collective-permute-start = (bf16[2,1,256,256]{3,2,1,0:T(8,128)(2,1)}, bf16[2,1,256,256]{3,2,1,0:T(8,128)(2,1)S(1)}, u32[]{:S(2)}, u32[]{:S(2)}) collective-permute-start(bf16[2,1,256,256]{3,2,1,0:T(8,128)(2,1)} %right.1), channel_id=1, source_target_pairs={{0,1},{1,0},{2,5},{3,4},{4,3},{5,2},{6,9},{7,8},{8,7},{9,6},{10,13... | collective-permute-start | bytes 786440 | tf_op jit(solution)/shard_map/ppermute | solution.py:258
  3.6 0.7 %copy-start = (s32[2]{0:T(128)S(1)}, s32[2]{0:T(128)}, u32[]{:S(2)}) copy-start(s32[2]{0:T(128)} %ops.1) | copy-start | bytes 28
  5.4 4.5 %collective-permute-start.3 = (bf16[272,256]{1,0:T(8,128)(2,1)S(1)}, bf16[272,256]{1,0:T(8,128)(2,1)S(1)}, u32[]{:S(2)}, u32[]{:S(2)}) collective-permute-start(bf16[272,256]{1,0:T(8,128)(2,1)S(1)} %get-tuple-element.24), channel_id=1, source_target_pairs={{0,1},{1,0},{2,3},{3,2},{4,5},{5,4},{6,7},{7,6},{8,9},{9,8},{10,11... | collective-permute-start | bytes 417800 | tf_op jit(solution)/shard_map/ppermute | solution.py:262
  6.0 1.3 %collective-permute-start.4 = (bf16[256,256]{1,0:T(8,128)(2,1)S(1)}, bf16[256,256]{1,0:T(8,128)(2,1)S(1)}, u32[]{:S(2)}, u32[]{:S(2)}) collective-permute-start(bf16[256,256]{1,0:T(8,128)(2,1)S(1)} %get-tuple-element.25.refs_0_), channel_id=1, source_target_pairs={{0,1},{1,0},{2,3},{3,2},{4,5},{5,4},{6,7},{7,6},{8,9},{9,8},{10,11... | collective-permute-start | bytes 393224 | tf_op jit(solution)/shard_map/ppermute | solution.py:263
  6.1 3.9 %collective-permute-start.5 = (bf16[256,256]{1,0:T(8,128)(2,1)S(1)}, bf16[256,256]{1,0:T(8,128)(2,1)S(1)}, u32[]{:S(2)}, u32[]{:S(2)}) collective-permute-start(bf16[256,256]{1,0:T(8,128)(2,1)S(1)} %get-tuple-element.26.refs_1_), channel_id=1, source_target_pairs={{0,1},{1,0},{2,3},{3,2},{4,5},{5,4},{6,7},{7,6},{8,9},{9,8},{10,11... | collective-permute-start | bytes 393224 | tf_op jit(solution)/shard_map/ppermute | solution.py:263
  7.3 7.2 %collective-permute-start.1 = (f32[8,128]{1,0:T(8,128)S(1)}, f32[8,128]{1,0:T(8,128)S(1)}, u32[]{:S(2)}, u32[]{:S(2)}) collective-permute-start(f32[8,128]{1,0:T(8,128)S(1)} %get-tuple-element.22), channel_id=1, source_target_pairs={{0,2},{2,4},{4,6},{6,8},{8,10},{10,12},{12,14},{14,16},{16,18},{18... | collective-permute-start | bytes 12296 | tf_op jit(solution)/shard_map/ppermute | solution.py:264
  14.5 1.5 %collective-permute-start.8 = (bf16[512,256]{1,0:T(8,128)(2,1)S(1)}, bf16[512,256]{1,0:T(8,128)(2,1)S(1)}, u32[]{:S(2)}, u32[]{:S(2)}) collective-permute-start(bf16[512,256]{1,0:T(8,128)(2,1)S(1)} %bitcast.4), channel_id=1, source_target_pairs={{0,1},{1,0},{2,3},{3,2},{4,5},{5,4},{6,7},{7,6},{8,9},{9,8},{10,11... | collective-permute-start | bytes 786440 | tf_op jit(solution)/shard_map/ppermute | solution.py:314
  14.5 1.9 %collective-permute-start.7 = (bf16[512,256]{1,0:T(8,128)(2,1)S(1)}, bf16[512,256]{1,0:T(8,128)(2,1)S(1)}, u32[]{:S(2)}, u32[]{:S(2)}) collective-permute-start(bf16[512,256]{1,0:T(8,128)(2,1)S(1)} %bitcast.2), channel_id=1, source_target_pairs={{0,1},{1,0},{2,3},{3,2},{4,5},{5,4},{6,7},{7,6},{8,9},{9,8},{10,11... | collective-permute-start | bytes 786440 | tf_op jit(solution)/shard_map/ppermute | solution.py:315
  15.0 1.4 %collective-permute-start.6 = (f32[8,128]{1,0:T(8,128)S(1)}, f32[8,128]{1,0:T(8,128)S(1)}, u32[]{:S(2)}, u32[]{:S(2)}) collective-permute-start(f32[8,128]{1,0:T(8,128)S(1)} %collective-permute-done.1.note), channel_id=1, source_target_pairs={{0,1},{1,0},{2,3},{3,2},{4,5},{5,4},{6,7},{7,6},{8,9},{9,8},{10,11... | collective-permute-start | bytes 12296 | tf_op jit(solution)/shard_map/ppermute | solution.py:316

commit v11 on v8

--- a/solution.py
+++ b/solution.py
@@ -198,14 +198,16 @@
 
 def last_kernel(info, note, note_other, rim, other_a, part_a, part_b, sigma_in, sigma, out_buf, out_sem):
     _, nvec, half, size = out_buf.shape
-    count, groups = other_a.shape[0] // size, out_sem.shape[1]
-    first, per_group = 0 if crossed() else rim.shape[1] - count, nvec // groups
+    count = other_a.shape[0] // size
+    first = 0 if crossed() else rim.shape[1] - count
     direct = (lax.axis_index("term") == 0) == below_is_a() if lax.axis_size("term") == 2 else True
     notes = [jnp.concatenate([x[0:1, :]] * (size // NOTE), 1) for x in (note, note_other)]
     note_a, note_b = jnp.where(direct, *notes), jnp.where(direct, *notes[::-1])
     stores = []
     for which, note, part in ((1, note_b, part_b), (0, note_a, part_a)):
         keep, state = state_mask(which, info, note, half)
+        groups = out_sem.shape[1] if which == 0 else 1
+        per_group = nvec // groups
         for group in range(groups):
             rows = pl.ds(group * per_group * half, per_group * half)
             total = part[rows, :]
@@ -335,7 +337,7 @@
         out_specs=HBM,
         scratch_shapes=[
             pltpu.VMEM((2, nvec, half, size), jnp.float32),
-            pltpu.SemaphoreType.DMA((2, 1)),
+            pltpu.SemaphoreType.DMA((2, groups)),
         ],
         input_output_aliases={7: 0},
         compiler_params=params,

time: 17.8 us -> 17.9 us (level)
  no operation moved by 1% of the time
where the time goes in v11:
time: 17.9 us; the launch traced here: 17.7 us
  Pallas kernels  7.54 us (42%)
  starting transfers between devices  7.19 us (40%)
  waiting for transfers between devices  1.61 us (9%)
  between operations  0.71 us (4%)
  local copies, waits for them, and re-layouts  0.65 us (4%)
    pallas_call x1, Pallas kernels, shards(): pl.pallas_call(centre_kernel, out_shape=(sigma_shape, rim_shape), in_spec...  4.26 us
    ppermute x1, starting transfers between devices, shards(): lax.ppermute(right_env, ('sector', 'term'), pair_exchange(sectors, 0, 0))  2.94 us
    ppermute x1, starting transfers between devices, shards(): note = lax.ppermute(note, ('sector', 'term'), cycle)  2.59 us
    pallas_call x1, Pallas kernels, shards(): pl.pallas_call(last_kernel, out_shape=sigma_shape, in_specs=[VMEM] * 7 +...  1.25 us
    pallas_call x1, Pallas kernels, pack(): pl.pallas_call(pack_kernel, out_shape=(jax.ShapeDtypeStruct((info_rows(te...  1.16 us
    ppermute x2, waiting for transfers between devices, shards(): rights += [lax.ppermute(x, 'term', swap) for x in rights]  0.84 us
    unnamed x2, local copies, waits for them, and re-layouts  0.65 us
    ppermute x1, starting transfers between devices, shards(): left_other = lax.ppermute(left_sent, 'term', swap)  0.57 us
  transfers between devices with their start and end apart: 9, of which 3 were waited for; matrix products, arithmetic and copies ran while one was open for 0% of the time, Pallas kernels for 36%

profile of v11, /device:TPU:0, one launch (start us, length us, event | category | flops | bytes accessed | tf_op | source)
XLA Modules:
  0.0 17.7 jit_solution(9058263387073306183)
XLA Ops:
  0.0 2.9 %collective-permute-start.2 = (bf16[2,1,256,256]{3,2,1,0:T(8,128)(2,1)}, bf16[2,1,256,256]{3,2,1,0:T(8,128)(2,1)S(1)}, u32[]{:S(2)}, u32[]{:S(2)}) collective-permute-start(bf16[2,1,256,256]{3,2,1,0:T(8,128)(2,1)} %right.1), channel_id=1, source_target_pairs={{0,2},{1,3},{2,0},{3,1},{4,6},{5,7},{6,4},{7,5},{8,10},{9,11},{10,... | collective-permute-start | bytes 786440 | tf_op jit(solution)/shard_map/ppermute | solution.py:256
  2.9 0.0 collective-permute-start
  3.6 0.0 copy-start
  3.6 0.6 %copy-done = s32[2]{0:T(128)S(1)} copy-done((s32[2]{0:T(128)S(1)}, s32[2]{0:T(128)}, u32[]{:S(2)}) %copy-start) | copy-done | bytes 32
  4.3 1.2 %pack.1 = (f32[16,256]{1,0:T(8,128)S(1)}, f32[8,128]{1,0:T(8,128)S(1)}, bf16[2,128,256]{2,1,0:T(8,128)(2,1)S(1)}, bf16[272,256]{1,0:T(8,128)(2,1)S(1)}, bf16[256...) custom-call(s32[1]{0:T(128)S(6)} %copy.10.kept, s32[2]{0:T(128)S(1)} %copy-done, bf16[2,1,256,256]{3,2,1,0:T(8,128)(2,1)} %left.1, ...), custom_call_target="tpu_custom_call" | custom-call | tf_op jit(solution)/shard_map/pack/pallas_call | solution.py:86
  5.4 0.6 %collective-permute-start.3 = (bf16[272,256]{1,0:T(8,128)(2,1)S(1)}, bf16[272,256]{1,0:T(8,128)(2,1)S(1)}, u32[]{:S(2)}, u32[]{:S(2)}) collective-permute-start(bf16[272,256]{1,0:T(8,128)(2,1)S(1)} %get-tuple-element.24), channel_id=1, source_target_pairs={{0,1},{1,0},{2,3},{3,2},{4,5},{5,4},{6,7},{7,6},{8,9},{9,8},{10,11... | collective-permute-start | bytes 417800 | tf_op jit(solution)/shard_map/ppermute | solution.py:261
  6.0 0.1 collective-permute-start.4
  6.1 0.4 %collective-permute-start.5 = (bf16[256,256]{1,0:T(8,128)(2,1)S(1)}, bf16[256,256]{1,0:T(8,128)(2,1)S(1)}, u32[]{:S(2)}, u32[]{:S(2)}) collective-permute-start(bf16[256,256]{1,0:T(8,128)(2,1)S(1)} %get-tuple-element.26.refs_1_), channel_id=1, source_target_pairs={{0,1},{1,0},{2,3},{3,2},{4,5},{5,4},{6,7},{7,6},{8,9},{9,8},{10,11... | collective-permute-start | bytes 393224 | tf_op jit(solution)/shard_map/ppermute | solution.py:262
  6.5 0.8 %collective-permute-done.4.refs_2_ = bf16[256,256]{1,0:T(8,128)(2,1)S(1)} collective-permute-done((bf16[256,256]{1,0:T(8,128)(2,1)S(1)}, bf16[256,256]{1,0:T(8,128)(2,1)S(1)}, u32[]{:S(2)}, u32[]{:S(2)}) %collective-permute-start.4) | collective-permute-done | bytes 131104 | tf_op jit(solution)/shard_map/ppermute | solution.py:262
  7.3 2.6 %collective-permute-start.1 = (f32[8,128]{1,0:T(8,128)S(1)}, f32[8,128]{1,0:T(8,128)S(1)}, u32[]{:S(2)}, u32[]{:S(2)}) collective-permute-start(f32[8,128]{1,0:T(8,128)S(1)} %get-tuple-element.22), channel_id=1, source_target_pairs={{0,2},{2,4},{4,6},{6,8},{8,10},{10,12},{12,14},{14,16},{16,18},{18... | collective-permute-start | bytes 12296 | tf_op jit(solution)/shard_map/ppermute | solution.py:263
  9.9 0.0 collective-permute-done.5.refs_3_
  9.9 0.0 collective-permute-done.3.left_other
  9.9 4.3 %centre.1 = (f32[4,1,4,128,256]{4,3,2,1,0:T(8,128)}, bf16[2,4,512,256]{3,2,1,0:T(8,128)(2,1)S(1)}) custom-call(bf16[4,1,4,256,256]{4,3,2,1,0:T(8,128)(2,1)} %psi.1, f32[16,256]{1,0:T(8,128)S(1)} %get-tuple-element.21.info_own.info, bf16[2,128,256]{2,1,0:T(8,128)(2,1)S(1)} %get-tuple-element.23.left_own, ...), custom_call_target="tpu_custom_call" | custom-call | tf_op jit(solution)/shard_map/centre/pallas_call | solution.py:292
  14.2 0.3 %collective-permute-done.2 = bf16[2,1,256,256]{3,2,1,0:T(8,128)(2,1)S(1)} collective-permute-done((bf16[2,1,256,256]{3,2,1,0:T(8,128)(2,1)}, bf16[2,1,256,256]{3,2,1,0:T(8,128)(2,1)S(1)}, u32[]{:S(2)}, u32[]{:S(2)}) %collective-permute-start.2) | collective-permute-done | bytes 262176 | tf_op jit(solution)/shard_map/ppermute | solution.py:256
  14.5 0.0 collective-permute-start.8
  14.5 0.0 collective-permute-done.1.note
  14.5 0.0 collective-permute-done
  14.5 0.5 %collective-permute-start.7 = (bf16[512,256]{1,0:T(8,128)(2,1)S(1)}, bf16[512,256]{1,0:T(8,128)(2,1)S(1)}, u32[]{:S(2)}, u32[]{:S(2)}) collective-permute-start(bf16[512,256]{1,0:T(8,128)(2,1)S(1)} %bitcast.2), channel_id=1, source_target_pairs={{0,1},{1,0},{2,3},{3,2},{4,5},{5,4},{6,7},{7,6},{8,9},{9,8},{10,11... | collective-permute-start | bytes 786440 | tf_op jit(solution)/shard_map/ppermute | solution.py:314
  15.0 0.1 collective-permute-start.6
  15.1 0.5 %own.1 = (f32[512,256]{1,0:T(8,128)S(1)}, f32[512,256]{1,0:T(8,128)S(1)}) custom-call(bf16[2,4,512,256]{3,2,1,0:T(8,128)(2,1)S(1)} %get-tuple-element.31.rim, bf16[512,256]{1,0:T(8,128)(2,1)S(1)} %bitcast.3, bf16[512,256]{1,0:T(8,128)(2,1)S(1)} %bitcast.5), custom_call_target="tpu_custom_call" | custom-call | tf_op jit(solution)/shard_map/own/pallas_call | solution.py:316
  15.5 0.5 %collective-permute-done.8.other_b = bf16[512,256]{1,0:T(8,128)(2,1)S(1)} collective-permute-done((bf16[512,256]{1,0:T(8,128)(2,1)S(1)}, bf16[512,256]{1,0:T(8,128)(2,1)S(1)}, u32[]{:S(2)}, u32[]{:S(2)}) %collective-permute-start.8) | collective-permute-done | bytes 262176 | tf_op jit(solution)/shard_map/ppermute | solution.py:313
  16.0 0.4 %other.1.part_b = f32[512,256]{1,0:T(8,128)S(1)} custom-call(bf16[2,4,512,256]{3,2,1,0:T(8,128)(2,1)S(1)} %get-tuple-element.31.rim, bf16[512,256]{1,0:T(8,128)(2,1)S(1)} %collective-permute-done.8.other_b, f32[512,256]{1,0:T(8,128)S(1)} %get-tuple-element.35.part_in), custom_call_target="tpu_custom_call", output_to_operand_aliasing={{}: (2, {})} | custom-call | tf_op jit(solution)/shard_map/other/pallas_call | solution.py:324
  16.4 0.0 collective-permute-done.6.note_other
  16.4 0.0 collective-permute-done.7.other_a
  16.4 1.3 %last.1 = f32[4,1,4,128,256]{4,3,2,1,0:T(8,128)} custom-call(f32[16,256]{1,0:T(8,128)S(1)} %get-tuple-element.21.info_own.info, f32[8,128]{1,0:T(8,128)S(1)} %collective-permute-done.1.note, f32[8,128]{1,0:T(8,128)S(1)} %collective-permute-done.6.note_other, bf16[2,4,512,256]{3,2,1,0:T(8,128)(2,1)S(1)} %get-tuple-element.31.rim, ...), custom_call_target="tpu_custom_call", output_to_operand_aliasing={{}: (7, {})} | custom-call | tf_op jit(solution)/shard_map/last/pallas_call | solution.py:333
Async XLA Ops:
  0.0 14.5 %collective-permute-start.2 = (bf16[2,1,256,256]{3,2,1,0:T(8,128)(2,1)}, bf16[2,1,256,256]{3,2,1,0:T(8,128)(2,1)S(1)}, u32[]{:S(2)}, u32[]{:S(2)}) collective-permute-start(bf16[2,1,256,256]{3,2,1,0:T(8,128)(2,1)} %right.1), channel_id=1, source_target_pairs={{0,2},{1,3},{2,0},{3,1},{4,6},{5,7},{6,4},{7,5},{8,10},{9,11},{10,... | collective-permute-start | bytes 786440 | tf_op jit(solution)/shard_map/ppermute | solution.py:256
  2.9 11.6 %collective-permute-start = (bf16[2,1,256,256]{3,2,1,0:T(8,128)(2,1)}, bf16[2,1,256,256]{3,2,1,0:T(8,128)(2,1)S(1)}, u32[]{:S(2)}, u32[]{:S(2)}) collective-permute-start(bf16[2,1,256,256]{3,2,1,0:T(8,128)(2,1)} %right.1), channel_id=1, source_target_pairs={{0,1},{1,0},{2,5},{3,4},{4,3},{5,2},{6,9},{7,8},{8,7},{9,6},{10,13... | collective-permute-start | bytes 786440 | tf_op jit(solution)/shard_map/ppermute | solution.py:257
  3.6 0.7 %copy-start = (s32[2]{0:T(128)S(1)}, s32[2]{0:T(128)}, u32[]{:S(2)}) copy-start(s32[2]{0:T(128)} %ops.1) | copy-start | bytes 28
  5.4 4.5 %collective-permute-start.3 = (bf16[272,256]{1,0:T(8,128)(2,1)S(1)}, bf16[272,256]{1,0:T(8,128)(2,1)S(1)}, u32[]{:S(2)}, u32[]{:S(2)}) collective-permute-start(bf16[272,256]{1,0:T(8,128)(2,1)S(1)} %get-tuple-element.24), channel_id=1, source_target_pairs={{0,1},{1,0},{2,3},{3,2},{4,5},{5,4},{6,7},{7,6},{8,9},{9,8},{10,11... | collective-permute-start | bytes 417800 | tf_op jit(solution)/shard_map/ppermute | solution.py:261
  6.0 1.3 %collective-permute-start.4 = (bf16[256,256]{1,0:T(8,128)(2,1)S(1)}, bf16[256,256]{1,0:T(8,128)(2,1)S(1)}, u32[]{:S(2)}, u32[]{:S(2)}) collective-permute-start(bf16[256,256]{1,0:T(8,128)(2,1)S(1)} %get-tuple-element.25.refs_0_), channel_id=1, source_target_pairs={{0,1},{1,0},{2,3},{3,2},{4,5},{5,4},{6,7},{7,6},{8,9},{9,8},{10,11... | collective-permute-start | bytes 393224 | tf_op jit(solution)/shard_map/ppermute | solution.py:262
  6.1 3.9 %collective-permute-start.5 = (bf16[256,256]{1,0:T(8,128)(2,1)S(1)}, bf16[256,256]{1,0:T(8,128)(2,1)S(1)}, u32[]{:S(2)}, u32[]{:S(2)}) collective-permute-start(bf16[256,256]{1,0:T(8,128)(2,1)S(1)} %get-tuple-element.26.refs_1_), channel_id=1, source_target_pairs={{0,1},{1,0},{2,3},{3,2},{4,5},{5,4},{6,7},{7,6},{8,9},{9,8},{10,11... | collective-permute-start | bytes 393224 | tf_op jit(solution)/shard_map/ppermute | solution.py:262
  7.3 7.2 %collective-permute-start.1 = (f32[8,128]{1,0:T(8,128)S(1)}, f32[8,128]{1,0:T(8,128)S(1)}, u32[]{:S(2)}, u32[]{:S(2)}) collective-permute-start(f32[8,128]{1,0:T(8,128)S(1)} %get-tuple-element.22), channel_id=1, source_target_pairs={{0,2},{2,4},{4,6},{6,8},{8,10},{10,12},{12,14},{14,16},{16,18},{18... | collective-permute-start | bytes 12296 | tf_op jit(solution)/shard_map/ppermute | solution.py:263
  14.5 1.5 %collective-permute-start.8 = (bf16[512,256]{1,0:T(8,128)(2,1)S(1)}, bf16[512,256]{1,0:T(8,128)(2,1)S(1)}, u32[]{:S(2)}, u32[]{:S(2)}) collective-permute-start(bf16[512,256]{1,0:T(8,128)(2,1)S(1)} %bitcast.4), channel_id=1, source_target_pairs={{0,1},{1,0},{2,3},{3,2},{4,5},{5,4},{6,7},{7,6},{8,9},{9,8},{10,11... | collective-permute-start | bytes 786440 | tf_op jit(solution)/shard_map/ppermute | solution.py:313
  14.5 1.9 %collective-permute-start.7 = (bf16[512,256]{1,0:T(8,128)(2,1)S(1)}, bf16[512,256]{1,0:T(8,128)(2,1)S(1)}, u32[]{:S(2)}, u32[]{:S(2)}) collective-permute-start(bf16[512,256]{1,0:T(8,128)(2,1)S(1)} %bitcast.2), channel_id=1, source_target_pairs={{0,1},{1,0},{2,3},{3,2},{4,5},{5,4},{6,7},{7,6},{8,9},{9,8},{10,11... | collective-permute-start | bytes 786440 | tf_op jit(solution)/shard_map/ppermute | solution.py:314
  15.0 1.4 %collective-permute-start.6 = (f32[8,128]{1,0:T(8,128)S(1)}, f32[8,128]{1,0:T(8,128)S(1)}, u32[]{:S(2)}, u32[]{:S(2)}) collective-permute-start(f32[8,128]{1,0:T(8,128)S(1)} %collective-permute-done.1.note), channel_id=1, source_target_pairs={{0,1},{1,0},{2,3},{3,2},{4,5},{5,4},{6,7},{7,6},{8,9},{9,8},{10,11... | collective-permute-start | bytes 12296 | tf_op jit(solution)/shard_map/ppermute | solution.py:315
